TPU v7x, 256 devices: a whole 4x4x8 slice. The times are simulated.
256 devices in a mesh: dp: 16 (over y, x), fsdp: 16 (over z, core).
Axes of the slice: x: 4, y: 4, z: 8, core: 2. Of those that a mesh axis runs over, the one named last changes fastest.
Arguments:
- fbank: bfloat16 [16, 16, 300, 640], P('dp', 'fsdp')
- lengths: int32 [16, 16, 3], replicated, may hold values from 50 to 200, as said below
- sources: int32 [16, 16, 3], replicated, may hold values from 0 to 47, as said below
- w_sub: bfloat16 [320, 1536], replicated, may hold values from -0.3125 to 0.3125
- gain_in: float32 [1536], replicated, may hold values from 0.25 to 1.75
- w_first: bfloat16 [1536, 3072], P(None, 'fsdp'), may hold values from -0.15625 to 0.15625
- taps: float32 [31, 1536], replicated, may hold values from -1 to 1
- gain_mid: float32 [1536], replicated, may hold values from 0.25 to 1.75
- w_second: bfloat16 [1536, 1536], P('fsdp'), may hold values from -0.15625 to 0.15625
- cotangent: bfloat16 [16, 16, 384, 1536], P('dp', 'fsdp'), may hold values from -0.046875 to 0.046875
Outputs:
- block_out: bfloat16 [16, 16, 384, 1536], P('dp', 'fsdp')
- grad_second: float32 [1536, 1536], P('fsdp')
- grad_taps: float32 [31, 1536], replicated
- grad_gain: float32 [1536], replicated
Inputs may be any that keep to these rules, and one draw needn't show every extreme that they name: Every length is even; the lengths of one owner (one row along the last dimension) add up to exactly 384, and one of them is exactly 200. `sources`: within each group (first index) the values are a permutation of 0 to 47: value // 3 is the loader (index along dp) whose shard holds the utterance, value % 3 its place there. The 3 utterances of one owner come from 3 different loaders, so no loader holds two utterances of one owner. A loader's utterances lie one after another in order of place from row 0 of its shard, each taking its length // 2 rows; the shard's other rows belong to no utterance.
All inputs are finite; a program needn't handle non-finite values.
Results may differ from a plain program's by a relative error of at most 0.029.
Values may be sent and summed in bfloat16 or wider, within the bound.
No kernel may reach another device: no remote copies, remote signals or barrier semaphores. Data moves between devices by JAX's collectives and lax.ppermute only.
A program may use at most 128 MiB of HBM per device.

v0:
```python
import jax
import jax.numpy as jnp
from jax import lax
from jax.sharding import PartitionSpec as P


def plan_rows(lengths_group, sources_group, load, rows_half):
    utt = lengths_group.shape[-1]
    pairs = lengths_group // 2
    flat_pairs = pairs.reshape(-1)
    flat_source = sources_group.reshape(-1)
    loader = flat_source // utt
    place = flat_source % utt
    earlier = (loader[None, :] == loader[:, None]) & (place[None, :] < place[:, None])
    offset = jnp.sum(jnp.where(earlier, flat_pairs[None, :], 0), axis=1)
    begin = (loader * load + offset).reshape(pairs.shape)
    ends = jnp.cumsum(pairs, axis=1)
    starts = ends - pairs
    position = jnp.arange(rows_half, dtype=jnp.int32)
    inside = (position[None, None, :] >= starts[:, :, None]) & (
        position[None, None, :] < ends[:, :, None]
    )
    source_row = jnp.sum(
        jnp.where(inside, begin[:, :, None] + position[None, None, :] - starts[:, :, None], 0),
        axis=1,
    )
    member = jnp.sum(jnp.where(inside, jnp.arange(utt, dtype=jnp.int32)[None, :, None], 0), axis=1)
    return (source_row, member)


def layer_norm(values):
    mean = jnp.mean(values, axis=-1, keepdims=True)
    spread = jnp.mean(jnp.square(values - mean), axis=-1, keepdims=True)
    rstd = lax.rsqrt(spread + 1e-05)
    return ((values - mean) * rstd, rstd)


def shifted(values, offset, half):
    total = values.shape[0]
    padded = jnp.pad(values, ((half, half), (0, 0)))
    return padded[half + offset : half + offset + total]


def same_mask(member, offset, half):
    total = member.shape[0]
    padded = jnp.pad(member, (half, half), constant_values=-1)
    return (padded[half + offset : half + offset + total] == member)[:, None]


def front(pairs, w_sub, gain_in):
    frames = pairs.reshape(-1, w_sub.shape[0])
    first = jnp.dot(frames, w_sub, preferred_element_type=jnp.float32).astype(jnp.bfloat16)
    centered, rstd = layer_norm(first.astype(jnp.float32))
    return (first, (centered * gain_in).astype(jnp.bfloat16))


def middle(hidden, taps, gain_mid, member):
    width = hidden.shape[1] // 2
    glu = (hidden[:, :width] * jax.nn.sigmoid(hidden[:, width:])).astype(jnp.bfloat16)
    half = taps.shape[0] // 2
    conv = jnp.zeros((hidden.shape[0], width), jnp.float32)
    for tap in range(taps.shape[0]):
        offset = tap - half
        moved = jnp.where(same_mask(member, offset, half), shifted(glu, offset, half), 0)
        conv = conv + moved * taps[tap]
    centered, rstd = layer_norm(conv)
    normed = centered * gain_mid
    swished = (normed * jax.nn.sigmoid(normed)).astype(jnp.bfloat16)
    return (glu, centered, rstd, normed, swished)


def back(d_swished, normed, centered, rstd, gain_mid, glu, member, kernel):
    sig = jax.nn.sigmoid(normed)
    d_normed = d_swished * sig * (1.0 + normed * (1.0 - sig))
    gain_term = jnp.sum(d_normed * centered, axis=0)
    scaled = d_normed * gain_mid
    d_conv = rstd * (
        scaled
        - jnp.mean(scaled, axis=-1, keepdims=True)
        - centered * jnp.mean(scaled * centered, axis=-1, keepdims=True)
    )
    half = kernel // 2
    rows_out = []
    for tap in range(kernel):
        offset = tap - half
        moved = jnp.where(same_mask(member, offset, half), shifted(glu, offset, half), 0)
        rows_out.append(jnp.sum(moved * d_conv, axis=0))
    return (jnp.stack(rows_out, axis=0), gain_term)


def body(fbank, lengths, sources, w_sub, gain_in, w_first, taps, gain_mid, w_second, cotangent):
    owner = lax.axis_index("dp")
    group = lax.axis_index("fsdp")
    load = fbank.shape[2]
    width = fbank.shape[3]
    rows = cotangent.shape[2]
    model = cotangent.shape[3]
    rows_half = rows // 2
    lengths_group = lax.dynamic_index_in_dim(lengths, group, 0, False)
    sources_group = lax.dynamic_index_in_dim(sources, group, 0, False)
    source_row, member_half = plan_rows(lengths_group, sources_group, load, rows_half)
    local = fbank.reshape(load, width)
    mine = lax.dynamic_index_in_dim(source_row, owner, 0, False)
    piece = lax.all_gather(local, "dp", axis=0, tiled=True)
    count = piece.shape[0]
    inside = (mine >= 0) & (mine < count)
    picked = jnp.take(piece, jnp.clip(mine, 0, count - 1), axis=0)
    pairs = jnp.where(inside[:, None], picked, jnp.zeros((rows_half, width), jnp.bfloat16))
    member = jnp.repeat(lax.dynamic_index_in_dim(member_half, owner, 0, False), 2)
    first, norm_in = front(pairs, w_sub, gain_in)
    hidden = jnp.dot(
        norm_in,
        lax.all_gather(w_first, "fsdp", axis=1, tiled=True),
        preferred_element_type=jnp.float32,
    )
    glu, centered, rstd, normed, swished = middle(hidden, taps, gain_mid, member)
    second = lax.all_gather(w_second, "fsdp", axis=0, tiled=True)
    projected = lax.dot_general(
        swished, second, (((1,), (1,)), ((), ())), preferred_element_type=jnp.float32
    )
    block = (first.astype(jnp.float32) + projected).astype(jnp.bfloat16)
    grad_out = cotangent.reshape(rows, model)
    d_swished = jnp.dot(grad_out, second, preferred_element_type=jnp.float32)
    kernel_term, gain_term = back(
        d_swished, normed, centered, rstd, gain_mid, glu, member, taps.shape[0]
    )
    grad_taps, grad_gain = lax.psum((kernel_term, gain_term), ("dp", "fsdp"))
    share = lax.psum_scatter(
        lax.dot_general(
            grad_out, swished, (((0,), (0,)), ((), ())), preferred_element_type=jnp.float32
        ).astype(jnp.bfloat16),
        "fsdp",
        scatter_dimension=0,
        tiled=True,
    )
    grad_second = lax.psum(share, "dp").astype(jnp.float32)
    return (block.reshape(1, 1, rows, model), grad_second, grad_taps, grad_gain)


def solution(mesh):
    in_specs = (
        P("dp", "fsdp", None, None),
        P(),
        P(),
        P(),
        P(),
        P(None, "fsdp"),
        P(),
        P(),
        P("fsdp", None),
        P("dp", "fsdp", None, None),
    )
    out_specs = (P("dp", "fsdp", None, None), P("fsdp", None), P(), P())
    return jax.shard_map(body, mesh=mesh, in_specs=in_specs, out_specs=out_specs, check_vma=False)
```

profile of v0, /device:TPU:2, one launch (start us, length us, event | category | flops | bytes accessed | tf_op | source)
XLA Modules:
  0.0 634.4 jit_solution(1996996177157765427)
XLA Ops:
  7.2 2.6 copy.65
  19.3 88.3 %all-gather.9.cloned.1.call-done = bf16[1,1,4800,640]{3,1,0,2:T(2,128)(2,1)} async-done(((bf16[1,1,300,640]{3,1,0,2:T(2,128)(2,1)}), bf16[1,1,4800,640]{3,1,0,2:T(2,128)(2,1)}) %all-gather.9.cloned.1.call-update) | async-done | bytes 6144016 | tf_op jit(solution)/shard_map/all_gather | solution.py:104
  107.7 8.2 %copy.101 = bf16[1,1,4800,640]{3,2,0,1:T(8,128)(2,1)} copy(bf16[1,1,4800,640]{3,1,0,2:T(2,128)(2,1)} %all-gather.9.cloned.1.call-done) | data formatting | bytes 12288000
  115.9 4.6 gather_fusion
  120.7 2.1 convert_reduce_fusion
  123.3 46.8 %all-gather.5.cloned.1.call-done = bf16[1536,3072]{0,1:T(8,128)(2,1)} async-done(((bf16[1536,192]{0,1:T(8,128)(2,1)}), bf16[1536,3072]{0,1:T(8,128)(2,1)}) %all-gather.5.cloned.1.call-update) | async-done | bytes 9437200 | tf_op jit(solution)/shard_map/all_gather | solution.py:113
  170.2 6.4 %fusion.75 = f32[384,3072]{1,0:T(8,128)S(1)} fusion(bf16[1536,3072]{0,1:T(8,128)(2,1)} %all-gather.5.cloned.1.call-done, bf16[384,1536]{1,0:T(8,128)(2,1)S(1)} %get-tuple-element.134, f32[1536]{0:T(1024)S(1)} %copy-done.92, f32[384]{0:T(512)S(1)} %add_rsqrt_fusion.1, f32[384]{0:T(512)S(1)} %broadcast_multiply_fusion.3), kind=kOutput, calls=%fused_computation.154 | convolution fusion | flops 3626827776 | bytes 15344640 | tf_op jit(solution)/shard_map/dot_general | solution.py:111
  178.0 16.8 %fusion.97 = (f32[384]{0:T(512)S(1)}, f32[384,1536]{1,0:T(8,128)S(1)}) fusion(f32[1536]{0:T(1024)S(1)} %copy-done.56, pred[384]{0:T(512)(128)(4,1)S(1)} %copy-done.68, f32[1536]{0:T(1024)S(1)} %copy-done.57, pred[384]{0:T(512)(128)(4,1)} %get-tuple-element.100, f32[1536]{0:T(1024)S(1)} %get-tuple-element.62, pred[384]{0:T(512)(128)(4,1)} %get-tuple-element.101, ...), kind=kLoop, calls=%fused_computation.303 | loop fusion | flops 72547968 | bytes 3742464 | tf_op jit(solution)/shard_map/reduce_sum | solution.py:32
  195.3 4.7 fusion
  199.9 6.6 %copy.67 = bf16[1536,1536]{1,0:T(8,128)(2,1)} copy(bf16[1536,1536]{0,1:T(8,128)(2,1)} %fusion) | data formatting | bytes 9437184
  206.7 6.8 %all-gather.7.cloned.1.call-done = bf16[1536,1536]{1,0:T(8,128)(2,1)} async-done(((bf16[96,1536]{1,0:T(8,128)(2,1)}), bf16[1536,1536]{1,0:T(8,128)(2,1)}) %all-gather.7.cloned.1.call-update) | async-done | bytes 4718608 | tf_op jit(solution)/shard_map/all_gather | solution.py:117
  213.4 5.7 multiply_reduce_fusion
  219.2 11.0 %fusion.69 = (f32[1536]{0:T(1024)S(1)}, f32[1536]{0:T(1024)S(1)}, f32[1536]{0:T(1024)}, f32[1536]{0:T(1024)}, f32[1536]{0:T(1024)}, /*index=5*/f32[1536]{0:T(1024)}, f32[384,1536]{1,0:T(8,128)S(1)}) fusion(pred[384]{0:T(512)(128)(4,1)} %get-tuple-element.128, bf16[384,1536]{1,0:T(8,128)(2,1)} %copy-done.1, pred[384]{0:T(512)(128)(4,1)} %get-tuple-element.100, ...), kind=kLoop, calls=%fused_computation.139 | loop fusion | flops 18275328 | bytes 8308992 | tf_op jit(solution)/shard_map/reduce_sum | solution.py:87
  230.2 4.2 fusion.58
  234.5 4.0 fusion.46
  238.6 4.2 fusion.40
  242.8 35.4 %reduce-scatter.4.cloned.1.call-done = bf16[96,1536]{1,0:T(8,128)(2,1)} async-done(((bf16[1536,1536]{1,0:T(8,128)(2,1)}), bf16[96,1536]{1,0:T(8,128)(2,1)}) %reduce-scatter.4.cloned.1.call-update) | async-done | bytes 294928
  278.2 1.9 copy.68
  280.3 7.4 %fusion.52 = (f32[1536]{0:T(1024)S(1)}, f32[1536]{0:T(1024)S(1)}, f32[1536]{0:T(1024)S(1)}, f32[1536]{0:T(1024)S(1)}, f32[1536]{0:T(1024)S(1)}, /*index=5*/f32[1536]{0:T(1024)S(1)}) fusion(f32[384,1536]{1,0:T(8,128)S(1)} %get-tuple-element.94, pred[384]{0:T(512)(128)(4,1)} %get-tuple-element.112, bf16[384,1536]{1,0:T(8,128)(2,1)} %copy-done.1, ...), kind=kLoop, calls=%fused_computation.122 | loop fusion | flops 13556736 | bytes 3577728 | tf_op jit(solution)/shard_map/reduce_sum | solution.py:87
  302.8 5.8 stack.127
  308.7 6.5 %fusion.5 = bf16[1,1,384,1536]{3,2,1,0:T(8,128)(2,1)} fusion(bf16[1536,1536]{1,0:T(8,128)(2,1)} %all-gather.7.cloned.1.call-done, bf16[384,1536]{1,0:T(8,128)(2,1)} %copy-done.5, f32[384,1536]{1,0:T(8,128)} %copy-done.4, f32[1536]{0:T(1024)} %param.17, f32[384]{0:T(512)} %copy-done.62, f32[384]{0:T(512)} %copy-done.58), kind=kOutput, calls=%fused_computation.75 | convolution fusion | flops 1818427392 | bytes 9446400 | tf_op jit(solution)/shard_map/dot_general | solution.py:118
  315.2 75.0 %psum.23 = f32[1536]{0:T(1024)} all-reduce(f32[1536]{0:T(1024)S(1)} %copy-done.63), channel_id=1, replica_groups=mesh['dp'=16,'fsdp'=16] {'dp','fsdp'}, use_global_device_ids=true, to_apply=%region_45.46 | all-reduce | flops 1536 | bytes 12288 | tf_op jit(solution)/shard_map/psum | solution.py:127
  390.2 2.0 copy.66
  392.2 233.8 %all-reduce.7.cloned.1.call-done = f32[31,1536]{1,0:T(8,128)} async-done(((f32[31,1536]{1,0:T(8,128)}), f32[31,1536]{1,0:T(8,128)}) %all-reduce.7.cloned.1.call-update) | async-done | bytes 190480 | tf_op jit(solution)/shard_map/psum | solution.py:127
  (280 shorter events, 28.1 us)
Async XLA Ops:
  7.2 188.1 %copy-start = (bf16[1,1,384,1536]{3,2,1,0:T(8,128)(2,1)S(1)}, bf16[1,1,384,1536]{3,2,1,0:T(8,128)(2,1)}, u32[]{:S(2)}) copy-start(bf16[1,1,384,1536]{3,2,1,0:T(8,128)(2,1)} %param.19) | copy-start | bytes 3538948
  7.2 100.5 %all-gather.9.cloned.1.call-start = ((), (), s32[]{:S(2)}) async-start(), calls=%async_computation.5 | async-start | bytes 13056000 | tf_op jit(solution)/shard_map/all_gather | solution.py:104
  9.9 160.3 %all-gather.5.cloned.1.call-start = ((), (), s32[]{:S(2)}) async-start(), calls=%async_computation.1 | async-start | bytes 10027008 | tf_op jit(solution)/shard_map/all_gather | solution.py:113
  10.6 202.8 %all-gather.7.cloned.1.call-start = ((), (), s32[]{:S(2)}) async-start(), calls=%async_computation.2 | async-start | bytes 5013504 | tf_op jit(solution)/shard_map/all_gather | solution.py:117
  11.3 266.8 %reduce-scatter.4.cloned.1.call-start = ((), (), s32[]{:S(2)}) async-start(), calls=%async_computation.6 | async-start | bytes 5013504
  120.5 49.6 %copy-start.92 = (f32[1536]{0:T(1024)S(1)}, f32[1536]{0:T(1024)}, u32[]{:S(2)}) copy-start(f32[1536]{0:T(1024)} %param.14) | copy-start | bytes 18436
  122.8 53.8 %copy-start.5 = (bf16[384,1536]{1,0:T(8,128)(2,1)}, bf16[384,1536]{1,0:T(8,128)(2,1)S(1)}, u32[]{:S(2)}) copy-start(bf16[384,1536]{1,0:T(8,128)(2,1)S(1)} %get-tuple-element.134) | copy-start | bytes 3538948
  177.6 17.6 %copy-start.1 = (bf16[384,1536]{1,0:T(8,128)(2,1)}, bf16[384,1536]{1,0:T(8,128)(2,1)S(1)}, u32[]{:S(2)}) copy-start(bf16[384,1536]{1,0:T(8,128)(2,1)S(1)} %fusion.74) | copy-start | bytes 3538948
  178.0 17.2 %copy-start.59 = (f32[1536]{0:T(1024)S(1)}, f32[1536]{0:T(1024)}, u32[]{:S(2)}) copy-start(f32[1536]{0:T(1024)} %param.17) | copy-start | bytes 18436
  194.8 18.6 %copy-start.4 = (f32[384,1536]{1,0:T(8,128)}, f32[384,1536]{1,0:T(8,128)S(1)}, u32[]{:S(2)}) copy-start(f32[384,1536]{1,0:T(8,128)S(1)} %get-tuple-element.96) | copy-start | bytes 7077892
  194.8 18.6 %copy-start.58 = (f32[384]{0:T(512)}, f32[384]{0:T(512)S(1)}, u32[]{:S(2)}) copy-start(f32[384]{0:T(512)S(1)} %broadcast_multiply_fusion.2) | copy-start | bytes 4612
  195.2 18.2 %copy-start.62 = (f32[384]{0:T(512)}, f32[384]{0:T(512)S(1)}, u32[]{:S(2)}) copy-start(f32[384]{0:T(512)S(1)} %add_rsqrt_fusion) | copy-start | bytes 4612
  206.6 183.6 %all-reduce.5.cloned.1.call-start = ((), (), s32[]{:S(2)}) async-start(), calls=%async_computation.3 | async-start | bytes 786432 | tf_op jit(solution)/shard_map/psum | solution.py:136
  280.1 345.9 %all-reduce.7.cloned.1.call-start = ((), (), s32[]{:S(2)}) async-start(), calls=%async_computation.4 | async-start | bytes 393216 | tf_op jit(solution)/shard_map/psum | solution.py:127
  280.2 17.1 %copy-start.30 = (f32[1536]{0:T(1024)S(1)}, f32[1536]{0:T(1024)}, u32[]{:S(2)}) copy-start(f32[1536]{0:T(1024)} %get-tuple-element.49) | copy-start | bytes 18436
  280.2 17.7 %copy-start.28 = (f32[1536]{0:T(1024)S(1)}, f32[1536]{0:T(1024)}, u32[]{:S(2)}) copy-start(f32[1536]{0:T(1024)} %get-tuple-element.48) | copy-start | bytes 18436
  280.2 18.3 %copy-start.39 = (f32[1536]{0:T(1024)S(1)}, f32[1536]{0:T(1024)}, u32[]{:S(2)}) copy-start(f32[1536]{0:T(1024)} %get-tuple-element.56) | copy-start | bytes 18436
  280.3 18.9 %copy-start.37 = (f32[1536]{0:T(1024)S(1)}, f32[1536]{0:T(1024)}, u32[]{:S(2)}) copy-start(f32[1536]{0:T(1024)} %get-tuple-element.55) | copy-start | bytes 18436
  280.3 19.5 %copy-start.35 = (f32[1536]{0:T(1024)S(1)}, f32[1536]{0:T(1024)}, u32[]{:S(2)}) copy-start(f32[1536]{0:T(1024)} %get-tuple-element.54) | copy-start | bytes 18436
  280.3 20.1 %copy-start.33 = (f32[1536]{0:T(1024)S(1)}, f32[1536]{0:T(1024)}, u32[]{:S(2)}) copy-start(f32[1536]{0:T(1024)} %get-tuple-element.59) | copy-start | bytes 18436
  280.3 20.7 %copy-start.31 = (f32[1536]{0:T(1024)S(1)}, f32[1536]{0:T(1024)}, u32[]{:S(2)}) copy-start(f32[1536]{0:T(1024)} %get-tuple-element.58) | copy-start | bytes 18436
  280.3 21.3 %copy-start.29 = (f32[1536]{0:T(1024)S(1)}, f32[1536]{0:T(1024)}, u32[]{:S(2)}) copy-start(f32[1536]{0:T(1024)} %get-tuple-element.57) | copy-start | bytes 18436
  280.3 21.9 %copy-start.3 = (bf16[384,1536]{1,0:T(8,128)(2,1)S(1)}, bf16[384,1536]{1,0:T(8,128)(2,1)}, u32[]{:S(2)}) copy-start(bf16[384,1536]{1,0:T(8,128)(2,1)} %copy-done.1) | copy-start | bytes 3538948
  280.3 21.9 %copy-start.91 = (pred[384]{0:T(512)(128)(4,1)S(1)}, pred[384]{0:T(512)(128)(4,1)}, u32[]{:S(2)}) copy-start(pred[384]{0:T(512)(128)(4,1)} %get-tuple-element.99) | copy-start | bytes 1156
  (75 other events, 370.9 us)
Sparse Core Ops, SparseCore 0:
  11.0 96.5 all-gather.8
  109.5 60.6 all-gather.4
  172.0 41.3 all-gather.6
  215.8 62.2 reduce-scatter.3
  281.8 92.5 all-reduce.4
  380.3 245.6 all-reduce.6
where the time goes:
time: 636 us; the launch traced here: 634 us
  waiting for transfers between devices  412 us (65%)
  blocking collectives  75 us (12%)
  local copies, waits for them, and re-layouts  53.1 us (8%)
  other arithmetic  52.7 us (8%)
  matrix products  25.4 us (4%)
  between operations  15.5 us (2%)
    psum x1, waiting for transfers between devices, body(): grad_taps, grad_gain = lax.psum((kernel_term, gain_term), ('dp', 'fsdp'))  234 us
    all_gather x1, waiting for transfers between devices, body(): piece = lax.all_gather(local, 'dp', axis=0, tiled=True)  88.3 us
    psum x1, blocking collectives, body(): grad_taps, grad_gain = lax.psum((kernel_term, gain_term), ('dp', 'fsdp'))  75 us
    all_gather x1, waiting for transfers between devices, body(): lax.all_gather(w_first, 'fsdp', axis=1, tiled=True)  46.8 us
    unnamed x7, waiting for transfers between devices  36.8 us
    reduce_sum x6, other arithmetic, back(): rows_out.append(jnp.sum(moved * d_conv, axis=0))  31.3 us
    unnamed x192, local copies, waits for them, and re-layouts  23.3 us
    another operation x32, local copies, waits for them, and re-layouts, back(): return (jnp.stack(rows_out, axis=0), gain_term)  20.2 us
  transfers between devices with their start and end apart: 6, of which 5 were waited for; matrix products, arithmetic and copies ran while one was open for 20% of the time, Pallas kernels for 0%

commit v1 on v0

v1 whole, which is shorter than its diff:
```python
import jax
import jax.numpy as jnp
from jax import lax
from jax.experimental import pallas as pl
from jax.experimental.pallas import tpu as pltpu
from jax.sharding import PartitionSpec as P

EDGE = 16
LANES = 128
SUBLANES = 8
BLOCK = 256
CONTRACT_LAST = (((1,), (1,)), ((), ()))


def row_chunk(total):
    for size in (104, 96, 80, 64, 48, 32, 16, 8):
        if total % size == 0:
            return size
    return total


def windows(pad_ref, base, size, lanes, kernel):
    reach = EDGE - kernel // 2
    for phase in range(SUBLANES):
        taps = [tap for tap in range(kernel) if (tap + reach) % SUBLANES == phase]
        if not taps:
            continue
        last = (taps[-1] + reach) // SUBLANES * SUBLANES
        held = pad_ref[base + phase : base + phase + last + size, lanes]
        for tap in taps:
            start = (tap + reach) // SUBLANES * SUBLANES
            yield tap, held[start : start + size]


def fill_padded(pad_ref, values):
    rows, width = values.shape
    zeros = jnp.zeros((EDGE, width), jnp.float32)
    pad_ref[:EDGE] = zeros
    pad_ref[EDGE + rows :] = zeros
    pad_ref[EDGE : EDGE + rows] = values


def forward_kernel(
    norm_ref, value_ref, gate_ref, taps_ref, gain_ref, select_ref,
    glu_ref, centered_ref, rstd_ref, swished_ref, pad_ref, conv_ref, half_ref,
):
    step = pl.program_id(0)
    steps = conv_ref.shape[0]
    rows, width = glu_ref.shape
    kernel = taps_ref.shape[0]
    norm = norm_ref[...]
    value = lax.dot_general(norm, value_ref[...], CONTRACT_LAST, preferred_element_type=jnp.float32)
    gate = lax.dot_general(norm, gate_ref[...], CONTRACT_LAST, preferred_element_type=jnp.float32)
    glu = (value * jax.nn.sigmoid(gate)).astype(jnp.bfloat16)
    glu_ref[...] = glu
    fill_padded(pad_ref, glu.astype(jnp.float32))
    size = row_chunk(rows)
    for column in range(0, width, LANES):
        lanes = slice(column, column + LANES)
        for base in range(0, rows, size):
            total = jnp.zeros((size, LANES), jnp.float32)
            for tap, moved in windows(pad_ref, base, size, lanes, kernel):
                total = total + moved * taps_ref[tap : tap + 1, lanes]
            conv_ref[step, base : base + size, lanes] = total

    @pl.when(step == steps - 1)
    def _():
        model = steps * width
        depth = 2 * SUBLANES

        def normalise(index, carry):
            chunk = pl.ds(pl.multiple_of(index * depth, depth), depth)
            parts = [conv_ref[block, chunk, :] for block in range(steps)]
            mean = sum(jnp.sum(part, axis=1, keepdims=True) for part in parts) / model
            parts = [part - mean for part in parts]
            spread = sum(jnp.sum(part * part, axis=1, keepdims=True) for part in parts) / model
            rstd = lax.rsqrt(spread + 1e-05)
            rstd_ref[chunk, :] = jnp.broadcast_to(rstd, (depth, LANES))
            for block in range(steps):
                centered = parts[block] * rstd
                centered_ref[block, chunk, :] = centered
                normed = centered * gain_ref[:, block * width : (block + 1) * width]
                half_ref[block, chunk, :] = (normed * jax.nn.sigmoid(normed)).astype(jnp.bfloat16)
            return carry

        lax.fori_loop(0, rows // depth, normalise, 0)
        for block in range(steps):
            swished_ref[:, block * width : (block + 1) * width] = jnp.dot(
                select_ref[...], half_ref[block], preferred_element_type=jnp.float32
            ).astype(jnp.bfloat16)


def forward(norm_in, first_t, taps, gain_mid, select):
    rows, model = norm_in.shape
    kernel = taps.shape[0]
    steps = model // BLOCK
    dense = select.shape[0]
    whole = lambda step: (0, 0)
    return pl.pallas_call(
        forward_kernel,
        grid=(steps,),
        in_specs=[
            pl.BlockSpec((rows, model), whole),
            pl.BlockSpec((BLOCK, model), lambda step: (step, 0)),
            pl.BlockSpec((BLOCK, model), lambda step: (step + steps, 0)),
            pl.BlockSpec((kernel, BLOCK), lambda step: (0, step)),
            pl.BlockSpec((1, model), whole),
            pl.BlockSpec((dense, rows), whole),
        ],
        out_specs=[
            pl.BlockSpec((rows, BLOCK), lambda step: (0, step)),
            pl.BlockSpec((steps, rows, BLOCK), lambda step: (0, 0, 0)),
            pl.BlockSpec((rows, LANES), whole),
            pl.BlockSpec((dense, model), whole),
        ],
        out_shape=[
            jax.ShapeDtypeStruct((rows, model), jnp.bfloat16),
            jax.ShapeDtypeStruct((steps, rows, BLOCK), jnp.float32),
            jax.ShapeDtypeStruct((rows, LANES), jnp.float32),
            jax.ShapeDtypeStruct((dense, model), jnp.bfloat16),
        ],
        scratch_shapes=[
            pltpu.VMEM((rows + 2 * EDGE, BLOCK), jnp.float32),
            pltpu.VMEM((steps, rows, BLOCK), jnp.float32),
            pltpu.VMEM((steps, rows, BLOCK), jnp.bfloat16),
        ],
        compiler_params=pltpu.CompilerParams(vmem_limit_bytes=48 * 2**20),
        cost_estimate=pl.CostEstimate(
            flops=4 * rows * model * model + 2 * kernel * rows * model,
            bytes_accessed=4 * model * model + 10 * rows * model,
            transcendentals=2 * rows * model,
        ),
        name="forward",
    )(norm_in, first_t, first_t, taps, gain_mid.reshape(1, model), select)


def backward_kernel(
    cotangent_ref, second_ref, centered_ref, rstd_ref, gain_ref, glu_ref,
    taps_out_ref, gain_out_ref, scaled_ref, sums_ref, pad_ref, part_ref,
):
    step = pl.program_id(0)
    steps = scaled_ref.shape[0]
    rows, width = glu_ref.shape
    kernel = taps_out_ref.shape[0]
    model = steps * width

    @pl.when(step == 0)
    def _():
        sums_ref[...] = jnp.zeros_like(sums_ref)

    @pl.when(step < steps)
    def _():
        scaled_ref[step] = jnp.dot(
            cotangent_ref[...], second_ref[...], preferred_element_type=jnp.float32
        )
        gain = gain_ref[...]
        depth = 32 if rows % 32 == 0 else SUBLANES

        def chunk_step(index, total):
            chunk = pl.ds(pl.multiple_of(index * depth, depth), depth)
            centered = centered_ref[0, chunk, :]
            normed = centered * gain
            sig = jax.nn.sigmoid(normed)
            d_normed = scaled_ref[step, chunk, :] * (sig * (1.0 + normed * (1.0 - sig)))
            weighed = d_normed * centered
            scaled = d_normed * gain
            scaled_ref[step, chunk, :] = scaled
            both = scaled * centered
            first = sums_ref[0, chunk, :]
            second = sums_ref[1, chunk, :]
            for column in range(0, width, LANES):
                first = first + scaled[:, column : column + LANES]
                second = second + both[:, column : column + LANES]
            sums_ref[0, chunk, :] = first
            sums_ref[1, chunk, :] = second
            return total + jnp.sum(weighed.reshape(-1, SUBLANES, width), axis=0)

        total = lax.fori_loop(
            0, rows // depth, chunk_step, jnp.zeros((SUBLANES, width), jnp.float32)
        )
        gain_out_ref[...] = jnp.sum(total, axis=0, keepdims=True)

    @pl.when(step == steps)
    def _():
        for index in range(2):
            mean = jnp.sum(sums_ref[index], axis=1, keepdims=True) / model
            sums_ref[index] = jnp.broadcast_to(mean, (rows, LANES))

    @pl.when(step >= steps)
    def _():
        block = step - steps
        fill_padded(pad_ref, glu_ref[...].astype(jnp.float32))
        size = row_chunk(rows)
        for column in range(0, width, LANES):
            lanes = slice(column, column + LANES)
            for base in range(0, rows, size):
                chunk = slice(base, base + size)
                d_conv = rstd_ref[chunk, :] * (
                    scaled_ref[block, chunk, lanes]
                    - sums_ref[0, chunk, :]
                    - centered_ref[0, chunk, lanes] * sums_ref[1, chunk, :]
                )
                for tap, moved in windows(pad_ref, base, size, lanes, kernel):
                    term = jnp.sum((moved * d_conv).reshape(-1, SUBLANES, LANES), axis=0)
                    if base == 0:
                        part_ref[tap, :, lanes] = term
                    else:
                        part_ref[tap, :, lanes] += term
        taps_out_ref[...] = jnp.sum(part_ref[...], axis=1)


def backward(cotangent, second, centered, rstd, gain_mid, glu, kernel):
    rows, model = cotangent.shape
    steps = model // BLOCK
    whole = lambda step: (0, 0)
    early = lambda step: (0, jnp.minimum(step, steps - 1))
    late = lambda step: (0, jnp.maximum(step - steps, 0))
    return pl.pallas_call(
        backward_kernel,
        grid=(2 * steps,),
        in_specs=[
            pl.BlockSpec((rows, model), whole),
            pl.BlockSpec((model, BLOCK), early),
            pl.BlockSpec((1, rows, BLOCK), lambda step: (step % steps, 0, 0)),
            pl.BlockSpec((rows, LANES), whole),
            pl.BlockSpec((1, BLOCK), early),
            pl.BlockSpec((rows, BLOCK), late),
        ],
        out_specs=[
            pl.BlockSpec((kernel, BLOCK), late),
            pl.BlockSpec((1, BLOCK), early),
        ],
        out_shape=[
            jax.ShapeDtypeStruct((kernel, model), jnp.float32),
            jax.ShapeDtypeStruct((1, model), jnp.float32),
        ],
        scratch_shapes=[
            pltpu.VMEM((steps, rows, BLOCK), jnp.float32),
            pltpu.VMEM((2, rows, LANES), jnp.float32),
            pltpu.VMEM((rows + 2 * EDGE, BLOCK), jnp.float32),
            pltpu.VMEM((kernel, SUBLANES, BLOCK), jnp.float32),
        ],
        compiler_params=pltpu.CompilerParams(vmem_limit_bytes=48 * 2**20),
        cost_estimate=pl.CostEstimate(
            flops=2 * rows * model * model + 2 * kernel * rows * model,
            bytes_accessed=2 * model * model + 12 * rows * model,
            transcendentals=rows * model,
        ),
        name="backward",
    )(cotangent, second, centered, rstd, gain_mid.reshape(1, model), glu)


def at(array, index, axis=0):
    return lax.dynamic_index_in_dim(array, index, axis, False)


def send_rows(fbank, lengths, sources, owner, utt, owners, most):
    halves = lengths.reshape(-1) // 2
    flat = sources.reshape(-1)
    places = jnp.arange(utt, dtype=jnp.int32) + owner * utt
    held = flat[None, :] == places[:, None]
    index = jnp.sum(jnp.where(held, jnp.arange(flat.shape[0], dtype=jnp.int32)[None, :], 0), axis=1)
    length = jnp.sum(jnp.where(held, halves[None, :], 0), axis=1)
    begin = jnp.cumsum(length) - length
    padded = jnp.pad(fbank, ((0, most), (0, 0)))
    blocks = jnp.zeros((owners, most, fbank.shape[1]), fbank.dtype)
    for place in range(utt):
        block = lax.dynamic_slice_in_dim(padded, begin[place], most, 0)
        blocks = lax.dynamic_update_index_in_dim(blocks, block, lax.div(index[place], utt), 0)
    return blocks


def place_rows(received, lengths, sources, rows_half):
    utt = lengths.shape[0]
    most = received.shape[1]
    halves = lengths // 2
    gap = EDGE // 2
    position = jnp.arange(rows_half + gap * (utt - 1), dtype=jnp.int32)
    column = jnp.full_like(position, -1)
    start = jnp.int32(0)
    for k in range(utt):
        inside = (position >= start) & (position < start + halves[k])
        column = jnp.where(inside, k * most + position - start, column)
        start = start + halves[k] + gap
    blocks = jnp.concatenate([at(received, lax.div(sources[k], utt)) for k in range(utt)], axis=0)
    return pick(one_hot(column, utt * most), blocks)


def frame_positions(lengths, rows):
    ends = jnp.cumsum(lengths)
    frame = jnp.arange(rows, dtype=jnp.int32)
    for k in range(lengths.shape[0] - 1):
        frame = frame + jnp.where(jnp.arange(rows, dtype=jnp.int32) >= ends[k], EDGE, 0)
    return frame


def one_hot(columns, count):
    wanted = jnp.arange(count, dtype=jnp.int32)
    return (columns[:, None] == wanted[None, :]).astype(jnp.bfloat16)


def layer_norm(values):
    mean = jnp.mean(values, axis=-1, keepdims=True)
    spread = jnp.mean(jnp.square(values - mean), axis=-1, keepdims=True)
    return (values - mean) * lax.rsqrt(spread + 1e-05)


def pick(matrix, values):
    return jnp.dot(matrix, values, preferred_element_type=jnp.float32).astype(jnp.bfloat16)


def spread(values, axis):
    copies = jnp.broadcast_to(values[None], (lax.axis_size(axis),) + values.shape)
    return lax.all_to_all(copies, axis, 0, 0, tiled=True)


def body(fbank, lengths, sources, w_sub, gain_in, w_first, taps, gain_mid, w_second, cotangent):
    owners = lax.axis_size("dp")
    groups = lax.axis_size("fsdp")
    chips = groups // 2
    owner = lax.axis_index("dp")
    group = lax.axis_index("fsdp")
    core = group % 2
    swap = [(i, i ^ 1) for i in range(groups)]
    same_core = [[2 * chip + side for chip in range(chips)] for side in range(2)]
    load, width = fbank.shape[2:]
    rows, model = cotangent.shape[2:]
    kernel = taps.shape[0]
    utt = lengths.shape[2]
    own_rows = w_second.shape[0]
    most = -(-(200 // 2) // SUBLANES) * SUBLANES

    first_t = lax.all_gather(w_first.T, "fsdp", axis=0, tiled=True)
    second = lax.all_gather(w_second, "fsdp", axis=0, tiled=True)

    lengths_group = at(lengths, group)
    sources_group = at(sources, group)
    own_lengths = at(lengths_group, owner)
    own_sources = at(sources_group, owner)
    blocks = send_rows(fbank.reshape(load, width), lengths_group, sources_group, owner, utt, owners, most)
    received = lax.all_to_all(blocks, "dp", 0, 0, tiled=True)
    pairs = place_rows(received, own_lengths, own_sources, rows // 2)
    frames = pairs.reshape(-1, w_sub.shape[0])
    spaced = frames.shape[0]
    select = one_hot(frame_positions(own_lengths, rows), spaced)

    x0 = jnp.dot(frames, w_sub, preferred_element_type=jnp.float32).astype(jnp.bfloat16)
    norm_in = (layer_norm(x0.astype(jnp.float32)) * gain_in).astype(jnp.bfloat16)
    x0 = pick(select, x0)
    grad_out = cotangent.reshape(rows, model)
    grad_spaced = pick(select.T, grad_out)
    grad_t = grad_out.T.reshape(chips, 2, own_rows, rows)
    grad_mine = at(grad_t, core, 1).reshape(chips * own_rows, rows)
    grad_theirs = lax.ppermute(
        at(grad_t, 1 - core, 1).reshape(chips * own_rows, rows), "fsdp", swap
    )

    norm_in, grad_spaced, grad_theirs = lax.optimization_barrier((norm_in, grad_spaced, grad_theirs))
    glu, centered, rstd, swished = forward(norm_in, first_t, taps, gain_mid, select)

    swished_theirs = lax.ppermute(swished, "fsdp", swap)
    partial = jnp.dot(
        jnp.concatenate([grad_mine, grad_theirs], axis=1),
        jnp.concatenate([swished, swished_theirs], axis=0),
        preferred_element_type=jnp.float32,
    ).astype(jnp.bfloat16)
    share = lax.psum_scatter(
        partial, "fsdp", scatter_dimension=0, tiled=True, axis_index_groups=same_core
    )

    taps_term, gain_term = backward(grad_spaced, second, centered, rstd, gain_mid, glu, kernel)
    projected = lax.dot_general(
        swished, second, CONTRACT_LAST, preferred_element_type=jnp.float32
    )
    block = (x0.astype(jnp.float32) + projected).astype(jnp.bfloat16)

    small = jnp.concatenate([taps_term, gain_term], axis=0).reshape(groups, -1, model)
    small = lax.all_to_all(small, "fsdp", 0, 0, tiled=True)
    small = spread(jnp.sum(small, axis=0).astype(jnp.bfloat16), "fsdp")

    own = own_rows // owners
    both = jnp.concatenate([share.reshape(owners, own, model), small.reshape(owners, -1, model)], axis=1)
    both = lax.all_to_all(both, "dp", 0, 0, tiled=True)
    both = spread(jnp.sum(both.astype(jnp.float32), axis=0).astype(jnp.bfloat16), "dp")
    both = both.astype(jnp.float32)
    grad_second = both[:, :own].reshape(own_rows, model)
    small = both[:, own:].reshape(kernel + 1, model)
    return (block.reshape(1, 1, rows, model), grad_second, small[:kernel], small[kernel])


def solution(mesh):
    in_specs = (
        P("dp", "fsdp", None, None),
        P(),
        P(),
        P(),
        P(),
        P(None, "fsdp"),
        P(),
        P(),
        P("fsdp", None),
        P("dp", "fsdp", None, None),
    )
    out_specs = (P("dp", "fsdp", None, None), P("fsdp", None), P(), P())
    return jax.shard_map(body, mesh=mesh, in_specs=in_specs, out_specs=out_specs, check_vma=False)
```

time: 636 us -> 212 us (0.33)
  waiting for transfers between devices: 412 us -> 54.7 us
  blocking collectives: 75 us -> 16.8 us
  other arithmetic: 52.7 us -> 5.67 us
  Pallas kernels: 0 us -> 44.3 us
  local copies, waits for them, and re-layouts: 53.1 us -> 23.3 us
  starting transfers between devices: 0.24 us -> 23.8 us
  between operations: 15.5 us -> 26 us
  matrix products: 25.4 us -> 16.5 us
    psum x2 -> x0, waiting for transfers between devices: 234 us -> none  [the longest x1 234 us: body(): grad_taps, grad_gain = lax.psum((kernel_term, gain_term), ('dp', 'fsdp'))]
    all_gather x2 -> x1, waiting for transfers between devices: 135 us -> 11.1 us  [body(): first_t = lax.all_gather(w_first.T, 'fsdp', axis=0, tiled=True)]
    psum x1 -> x0, blocking collectives: 75 us -> none  [body(): grad_taps, grad_gain = lax.psum((kernel_term, gain_term), ('dp', 'fsdp'))]
    reduce_sum x9 -> x3, other arithmetic: 48.4 us -> 1.31 us  [the longest x1 1.06 us: body(): jnp.sum(both.astype(jnp.float32), axis=0).astype(jnp.bfloat16)]
    pallas_call x0 -> x2, Pallas kernels: none -> 44.3 us  [the longest x1 24.6 us: forward(): pl.pallas_call(forward_kernel, grid=(steps,), in_specs=[pl.BlockSpec((row...]
    unnamed x7 -> x3, waiting for transfers between devices: 36.8 us -> 1.39 us
    all_to_all x0 -> x4, waiting for transfers between devices: none -> 27.2 us  [the longest x1 13.8 us: body(): received = lax.all_to_all(blocks, 'dp', 0, 0, tiled=True)]
    all_to_all x0 -> x4, starting transfers between devices: none -> 23.4 us  [the longest x2 8.31 us: spread(): return lax.all_to_all(copies, axis, 0, 0, tiled=True)]
  transfers between devices with their start and end apart: 6 -> 9, of which waited for: 5 -> 8; matrix products, arithmetic and copies ran while one was open for 20% -> 17% of each run, Pallas kernels for 0% -> 21%
where the time goes in v1:
time: 212 us; the launch traced here: 211 us
  waiting for transfers between devices  54.7 us (26%)
  Pallas kernels  44.3 us (21%)
  between operations  26 us (12%)
  starting transfers between devices  23.8 us (11%)
  local copies, waits for them, and re-layouts  23.3 us (11%)
  blocking collectives  16.8 us (8%)
  matrix products  16.5 us (8%)
  other arithmetic  5.67 us (3%)
    pallas_call x1, Pallas kernels, forward(): pl.pallas_call(forward_kernel, grid=(steps,), in_specs=[pl.BlockSpec((row...  24.6 us
    pallas_call x1, Pallas kernels, backward(): pl.pallas_call(backward_kernel, grid=(2 * steps,), in_specs=[pl.BlockSpec...  19.7 us
    all_to_all x1, blocking collectives, body(): small = lax.all_to_all(small, 'fsdp', 0, 0, tiled=True)  16.8 us
    all_to_all x1, waiting for transfers between devices, body(): received = lax.all_to_all(blocks, 'dp', 0, 0, tiled=True)  13.8 us
    all_gather x1, waiting for transfers between devices, body(): first_t = lax.all_gather(w_first.T, 'fsdp', axis=0, tiled=True)  11.1 us
    all_gather x1, waiting for transfers between devices, body(): second = lax.all_gather(w_second, 'fsdp', axis=0, tiled=True)  8.8 us
    all_to_all x2, starting transfers between devices, spread(): return lax.all_to_all(copies, axis, 0, 0, tiled=True)  8.31 us
    all_to_all x1, starting transfers between devices, body(): received = lax.all_to_all(blocks, 'dp', 0, 0, tiled=True)  7.59 us
  transfers between devices with their start and end apart: 9, of which 8 were waited for; matrix products, arithmetic and copies ran while one was open for 17% of the time, Pallas kernels for 21%

profile of v1, /device:TPU:2, one launch (start us, length us, event | category | flops | bytes accessed | tf_op | source)
XLA Modules:
  0.0 211.1 jit_solution(12943534700514825217)
XLA Ops:
  19.4 1.5 broadcast_in_dim.69
  23.1 7.6 %all-to-all-start = ((bf16[16,104,640]{2,1,0:T(8,128)(2,1)}), bf16[16,104,640]{2,1,0:T(8,128)(2,1)}, u32[]{:S(2)}, u32[]{:S(2)}) async-start(bf16[16,104,640]{2,1,0:T(8,128)(2,1)} %fusion.28), calls=%async_computation | async-start | bytes 4259840 | tf_op jit(solution)/shard_map/all_to_all | solution.py:341
  32.7 1.4 constant_dynamic-slice_fusion.2
  41.1 1.3 select_add_fusion
  42.6 2.0 convolution_convert_fusion.1.cotangent_ref
  44.6 13.8 %all-to-all-done = bf16[16,104,640]{2,1,0:T(8,128)(2,1)} async-done(((bf16[16,104,640]{2,1,0:T(8,128)(2,1)}), bf16[16,104,640]{2,1,0:T(8,128)(2,1)}, u32[]{:S(2)}, u32[]{:S(2)}) %all-to-all-start) | async-done | bytes 2129952 | tf_op jit(solution)/shard_map/all_to_all | solution.py:341
  62.6 11.1 %all-gather.3.cloned.1.call-done.value_ref.gate_ref = bf16[3072,1536]{1,0:T(8,128)(2,1)} async-done(((bf16[192,1536]{1,0:T(8,128)(2,1)}), bf16[3072,1536]{1,0:T(8,128)(2,1)}) %all-gather.3.cloned.1.call-update) | async-done | bytes 9437200 | tf_op jit(solution)/shard_map/all_gather | solution.py:333
  73.7 24.6 %forward.1 = (bf16[416,1536]{1,0:T(8,128)(2,1)S(1)}, f32[6,416,256]{2,1,0:T(8,128)}, f32[416,128]{1,0:T(8,128)S(1)}, bf16[384,1536]{1,0:T(8,128)(2,1)S(1)}) custom-call(bf16[416,1536]{1,0:T(8,128)(2,1)S(1)} %fusion.7.norm_ref, bf16[3072,1536]{1,0:T(8,128)(2,1)} %all-gather.3.cloned.1.call-done.value_ref.gate_ref, ...), custom_call_target="tpu_custom_call" | custom-call | flops 3965485056 | bytes 15826944 | tf_op jit(solution)/shard_map/forward/pallas_call | solution.py:99
  100.3 2.8 %collective-permute-done.1 = bf16[384,1536]{1,0:T(8,128)(2,1)S(1)} collective-permute-done((bf16[384,1536]{1,0:T(8,128)(2,1)S(1)}, bf16[384,1536]{1,0:T(8,128)(2,1)S(1)}, u32[]{:S(2)}, u32[]{:S(2)}) %collective-permute-start.1) | collective-permute-done | bytes 1179680 | tf_op jit(solution)/shard_map/ppermute | solution.py:361
  103.1 4.8 %convolution_convert_fusion = bf16[768,1536]{1,0:T(8,128)(2,1)} fusion(bf16[384,1536]{1,0:T(8,128)(2,1)S(1)} %collective-permute-done.1, bf16[384,1536]{1,0:T(8,128)(2,1)S(1)} %get-tuple-element.14, bf16[768,384]{1,0:T(8,128)(2,1)} %collective-permute-done, bf16[768,384]{1,0:T(8,128)(2,1)} %bitcast.61), kind=kOutput, calls=%fused_computation | convolution fusion | flops 1820196864 | bytes 5898240 | tf_op jit(solution)/shard_map/dot_general | solution.py:362
  108.0 8.8 %all-gather.5.cloned.1.call-done.second_ref = bf16[1536,1536]{1,0:T(8,128)(2,1)} async-done(((bf16[96,1536]{1,0:T(8,128)(2,1)}), bf16[1536,1536]{1,0:T(8,128)(2,1)}) %all-gather.5.cloned.1.call-update) | async-done | bytes 4718608 | tf_op jit(solution)/shard_map/all_gather | solution.py:334
  116.8 1.3 copy-done.2
  118.1 1.3 copy-done.4
  120.3 19.7 %backward.1 = (f32[31,1536]{1,0:T(8,128)S(1)}, f32[1,1536]{1,0:T(1,128)S(1)}) custom-call(bf16[416,1536]{1,0:T(8,128)(2,1)S(1)} %copy-done.2, bf16[1536,1536]{1,0:T(8,128)(2,1)} %all-gather.5.cloned.1.call-done.second_ref, f32[6,416,256]{2,1,0:T(8,128)S(1)} %copy-done.1, f32[416,128]{1,0:T(8,128)S(1)} %copy-done.6, f32[1,1536]{1,0:T(1,128)S(1)} %reshape.207.gain_ref, ...), custom_call_target="tpu_custom_call" | custom-call | flops 2002550784 | bytes 12386304 | tf_op jit(solution)/shard_map/backward/pallas_call | solution.py:218
  140.2 16.8 %all_to_all.25 = f32[16,2,1536]{2,1,0:T(2,128)S(1)} all-to-all(f32[16,2,1536]{2,1,0:T(2,128)S(1)} %reshape.211), channel_id=1, replica_groups=mesh['dp'=16,'fsdp'=16] {'fsdp'}, dimensions={0} | all-to-all | bytes 393216 | tf_op jit(solution)/shard_map/all_to_all | solution.py:378
  157.7 3.5 %all-to-all-start.2 = ((bf16[16,2,1536]{2,1,0:T(2,128)(2,1)}), bf16[16,2,1536]{2,1,0:T(2,128)(2,1)S(1)}, u32[]{:S(2)}, u32[]{:S(2)}) async-start(bf16[16,2,1536]{2,1,0:T(2,128)(2,1)} %broadcast_in_dim.76), calls=%async_computation.3 | async-start | bytes 196608 | tf_op jit(solution)/shard_map/all_to_all | solution.py:314
  161.3 3.3 %reduce-scatter.2.cloned.1.call-done = bf16[96,1536]{1,0:T(8,128)(2,1)} async-done(((bf16[768,1536]{1,0:T(8,128)(2,1)}), bf16[96,1536]{1,0:T(8,128)(2,1)}) %reduce-scatter.2.cloned.1.call-update) | async-done | bytes 294928 | tf_op jit(solution)/shard_map/reduce_scatter | solution.py:367
  165.7 3.8 %all-to-all-done.2 = bf16[16,2,1536]{2,1,0:T(2,128)(2,1)S(1)} async-done(((bf16[16,2,1536]{2,1,0:T(2,128)(2,1)}), bf16[16,2,1536]{2,1,0:T(2,128)(2,1)S(1)}, u32[]{:S(2)}, u32[]{:S(2)}) %all-to-all-start.2) | async-done | bytes 98336 | tf_op jit(solution)/shard_map/all_to_all | solution.py:314
  170.4 7.5 %all-to-all-start.3 = ((bf16[16,8,1536]{2,1,0:T(8,128)(2,1)}), bf16[16,8,1536]{2,1,0:T(8,128)(2,1)}, u32[]{:S(2)}, u32[]{:S(2)}) async-start(bf16[16,8,1536]{2,1,0:T(8,128)(2,1)} %pad_maximum_fusion), calls=%async_computation.4 | async-start | bytes 786432 | tf_op jit(solution)/shard_map/all_to_all | solution.py:383
  178.0 2.3 %fusion.3 = f32[384,1536]{1,0:T(8,128)} fusion(bf16[416,1536]{1,0:T(8,128)(2,1)S(1)} %copy-done.11, s32[384]{0:T(512)S(1)} %select_add_fusion), kind=kOutput, calls=%fused_computation.10 | convolution fusion | flops 492072960 | bytes 3638784 | tf_op jit(solution)/shard_map/dot_general | solution.py:309
  180.2 7.3 %all-to-all-done.3 = bf16[16,8,1536]{2,1,0:T(8,128)(2,1)} async-done(((bf16[16,8,1536]{2,1,0:T(8,128)(2,1)}), bf16[16,8,1536]{2,1,0:T(8,128)(2,1)}, u32[]{:S(2)}, u32[]{:S(2)}) %all-to-all-start.3) | async-done | bytes 393248 | tf_op jit(solution)/shard_map/all_to_all | solution.py:383
  189.4 4.8 %all-to-all-start.4 = ((bf16[16,8,1536]{2,1,0:T(8,128)(2,1)}), bf16[16,8,1536]{2,1,0:T(8,128)(2,1)S(1)}, u32[]{:S(2)}, u32[]{:S(2)}) async-start(bf16[16,8,1536]{2,1,0:T(8,128)(2,1)} %broadcast_in_dim.77), calls=%async_computation.5 | async-start | bytes 786432 | tf_op jit(solution)/shard_map/all_to_all | solution.py:314
  194.2 6.1 %fusion.4 = bf16[1,1,384,1536]{3,2,1,0:T(8,128)(2,1)} fusion(f32[384,1536]{1,0:T(8,128)} %fusion.3, bf16[384,1536]{1,0:T(8,128)(2,1)S(1)} %copy-done.9, bf16[1536,1536]{1,0:T(8,128)(2,1)} %all-gather.5.cloned.1.call-done.second_ref), kind=kOutput, calls=%fused_computation.11 | convolution fusion | flops 1813118976 | bytes 9437184 | tf_op jit(solution)/shard_map/dot_general | solution.py:372
  200.3 2.3 %all-to-all-done.4 = bf16[16,8,1536]{2,1,0:T(8,128)(2,1)S(1)} async-done(((bf16[16,8,1536]{2,1,0:T(8,128)(2,1)}), bf16[16,8,1536]{2,1,0:T(8,128)(2,1)S(1)}, u32[]{:S(2)}, u32[]{:S(2)}) %all-to-all-start.4) | async-done | bytes 393248 | tf_op jit(solution)/shard_map/all_to_all | solution.py:314
  (87 shorter events, 25.2 us)
Async XLA Ops:
  7.2 52.9 %copy-start = (bf16[320,1536]{1,0:T(8,128)(2,1)S(1)}, bf16[320,1536]{1,0:T(8,128)(2,1)}, u32[]{:S(2)}) copy-start(bf16[320,1536]{1,0:T(8,128)(2,1)} %param.13) | copy-start | bytes 2949124
  7.2 13.8 %copy-start.12 = (bf16[1,1,300,640]{3,2,1,0:T(8,128)(2,1)S(1)}, bf16[1,1,300,640]{3,2,1,0:T(8,128)(2,1)}, u32[]{:S(2)}) copy-start(bf16[1,1,300,640]{3,2,1,0:T(8,128)(2,1)} %param.10) | copy-start | bytes 1152004
  7.2 66.5 %all-gather.3.cloned.1.call-start = ((), (), s32[]{:S(2)}) async-start(), calls=%async_computation.6 | async-start | bytes 10027008 | tf_op jit(solution)/shard_map/all_gather | solution.py:333
  7.9 108.8 %all-gather.5.cloned.1.call-start = ((), (), s32[]{:S(2)}) async-start(), calls=%async_computation.7 | async-start | bytes 5013504 | tf_op jit(solution)/shard_map/all_gather | solution.py:334
  23.1 7.7 %copy-start.13 = (bf16[1,1,384,1536]{3,2,1,0:T(8,128)(2,1)S(1)}, bf16[1,1,384,1536]{3,2,1,0:T(8,128)(2,1)}, u32[]{:S(2)}) copy-start(bf16[1,1,384,1536]{3,2,1,0:T(8,128)(2,1)} %param.19) | copy-start | bytes 3538948
  23.1 35.2 %all-to-all-start = ((bf16[16,104,640]{2,1,0:T(8,128)(2,1)}), bf16[16,104,640]{2,1,0:T(8,128)(2,1)}, u32[]{:S(2)}, u32[]{:S(2)}) async-start(bf16[16,104,640]{2,1,0:T(8,128)(2,1)} %fusion.28), calls=%async_computation | async-start | bytes 4259840 | tf_op jit(solution)/shard_map/all_to_all | solution.py:341
  30.7 133.9 %reduce-scatter.2.cloned.1.call-start = ((), (), s32[]{:S(2)}) async-start(), calls=%async_computation.8 | async-start | bytes 2654208 | tf_op jit(solution)/shard_map/reduce_scatter | solution.py:367
  30.8 8.4 %copy-start.16 = (f32[1536]{0:T(1024)S(1)}, f32[1536]{0:T(1024)}, u32[]{:S(2)}) copy-start(f32[1536]{0:T(1024)} %param.17) | copy-start | bytes 18436
  32.7 29.8 %collective-permute-start = (bf16[768,384]{1,0:T(8,128)(2,1)}, bf16[768,384]{1,0:T(8,128)(2,1)}, u32[]{:S(2)}, u32[]{:S(2)}) collective-permute-start(bf16[768,384]{1,0:T(8,128)(2,1)} %bitcast.26), channel_id=1, source_target_pairs={{0,1},{1,0},{2,3},{3,2},{4,5},{5,4},{6,7},{7,6},{8,9},{9,8},{10,11... | collective-permute-start | bytes 1769480 | tf_op jit(solution)/shard_map/ppermute | solution.py:354
  60.1 2.0 copy-start.15
  61.0 1.1 copy-start.10
  61.0 12.7 %copy-start.7 = (f32[31,1536]{1,0:T(8,128)S(1)}, f32[31,1536]{1,0:T(8,128)}, u32[]{:S(2)}) copy-start(f32[31,1536]{1,0:T(8,128)} %taps_ref.1) | copy-start | bytes 571396
  98.3 1.1 copy-start.3
  100.0 3.1 %copy-start.8 = (bf16[384,1536]{1,0:T(8,128)(2,1)}, bf16[384,1536]{1,0:T(8,128)(2,1)S(1)}, u32[]{:S(2)}) copy-start(bf16[384,1536]{1,0:T(8,128)(2,1)S(1)} %get-tuple-element.14) | copy-start | bytes 3538948
  100.0 3.1 %collective-permute-start.1 = (bf16[384,1536]{1,0:T(8,128)(2,1)S(1)}, bf16[384,1536]{1,0:T(8,128)(2,1)S(1)}, u32[]{:S(2)}, u32[]{:S(2)}) collective-permute-start(bf16[384,1536]{1,0:T(8,128)(2,1)S(1)} %get-tuple-element.14), channel_id=1, source_target_pairs={{0,1},{1,0},{2,3},{3,2},{4,5},{5,4},{6,7},{7,6},{8,9},{9,8},{10,11... | collective-permute-start | bytes 3538952 | tf_op jit(solution)/shard_map/ppermute | solution.py:361
  103.1 13.6 %copy-start.1 = (f32[6,416,256]{2,1,0:T(8,128)S(1)}, f32[6,416,256]{2,1,0:T(8,128)}, u32[]{:S(2)}) copy-start(f32[6,416,256]{2,1,0:T(8,128)} %get-tuple-element.17.centered_ref) | copy-start | bytes 7667716
  116.8 1.3 copy-start.2
  118.1 1.3 copy-start.4
  119.4 0.9 copy-start.6
  140.1 37.9 %copy-start.11 = (bf16[416,1536]{1,0:T(8,128)(2,1)S(1)}, bf16[416,1536]{1,0:T(8,128)(2,1)}, u32[]{:S(2)}) copy-start(bf16[416,1536]{1,0:T(8,128)(2,1)} %copy-done.10) | copy-start | bytes 3833860
  157.7 11.8 %all-to-all-start.2 = ((bf16[16,2,1536]{2,1,0:T(2,128)(2,1)}), bf16[16,2,1536]{2,1,0:T(2,128)(2,1)S(1)}, u32[]{:S(2)}, u32[]{:S(2)}) async-start(bf16[16,2,1536]{2,1,0:T(2,128)(2,1)} %broadcast_in_dim.76), calls=%async_computation.3 | async-start | bytes 196608 | tf_op jit(solution)/shard_map/all_to_all | solution.py:314
  170.4 17.1 %all-to-all-start.3 = ((bf16[16,8,1536]{2,1,0:T(8,128)(2,1)}), bf16[16,8,1536]{2,1,0:T(8,128)(2,1)}, u32[]{:S(2)}, u32[]{:S(2)}) async-start(bf16[16,8,1536]{2,1,0:T(8,128)(2,1)} %pad_maximum_fusion), calls=%async_computation.4 | async-start | bytes 786432 | tf_op jit(solution)/shard_map/all_to_all | solution.py:383
  178.0 16.2 %copy-start.9 = (bf16[384,1536]{1,0:T(8,128)(2,1)S(1)}, bf16[384,1536]{1,0:T(8,128)(2,1)}, u32[]{:S(2)}) copy-start(bf16[384,1536]{1,0:T(8,128)(2,1)} %copy-done.8) | copy-start | bytes 3538948
  189.4 13.3 %all-to-all-start.4 = ((bf16[16,8,1536]{2,1,0:T(8,128)(2,1)}), bf16[16,8,1536]{2,1,0:T(8,128)(2,1)S(1)}, u32[]{:S(2)}, u32[]{:S(2)}) async-start(bf16[16,8,1536]{2,1,0:T(8,128)(2,1)} %broadcast_in_dim.77), calls=%async_computation.5 | async-start | bytes 786432 | tf_op jit(solution)/shard_map/all_to_all | solution.py:314
  (2 other events, 1.4 us)
Sparse Core Ops, SparseCore 0:
  9.9 63.7 all-gather.2
  75.5 41.1 all-gather.4
  119.3 45.2 reduce-scatter.1

commit v2 on v1

v2 whole, which is shorter than its diff:
```python
import jax
import jax.numpy as jnp
from jax import lax
from jax.experimental import pallas as pl
from jax.experimental.pallas import tpu as pltpu
from jax.sharding import PartitionSpec as P

EDGE = 16
LANES = 128
SUBLANES = 8
FORWARD_STEPS = 6
BACKWARD_STEPS = 2
MOST = 104
CONTRACT_LAST = (((1,), (1,)), ((), ()))


def row_chunk(total):
    for size in (104, 96, 80, 64, 48, 32, 16, 8):
        if total % size == 0:
            return size
    return total


def windows(pad_ref, base, size, kernel):
    reach = EDGE - kernel // 2
    for phase in range(SUBLANES):
        taps = [tap for tap in range(kernel) if (tap + reach) % SUBLANES == phase]
        if not taps:
            continue
        last = (taps[-1] + reach) // SUBLANES * SUBLANES
        held = pad_ref[base + phase : base + phase + last + size, :]
        for tap in taps:
            start = (tap + reach) // SUBLANES * SUBLANES
            yield tap, held[start : start + size]


def fill_padded(pad_ref, values):
    rows, width = values.shape
    zeros = jnp.zeros((EDGE, LANES), jnp.float32)
    for index in range(width // LANES):
        pad_ref[index, :EDGE] = zeros
        pad_ref[index, EDGE + rows :] = zeros
        pad_ref[index, EDGE : EDGE + rows] = values[:, index * LANES : (index + 1) * LANES]


def sigmoid(values):
    return 0.5 * jnp.tanh(0.5 * values) + 0.5


def dot(left, right):
    return jnp.dot(left, right, preferred_element_type=jnp.float32)


def dot_t(left, right):
    return lax.dot_general(left, right, CONTRACT_LAST, preferred_element_type=jnp.float32)


def iotas(shape):
    return lax.broadcasted_iota(jnp.int32, shape, 0), lax.broadcasted_iota(jnp.int32, shape, 1)


def vmem(count):
    return [pl.BlockSpec(memory_space=pltpu.VMEM)] * count


def send_kernel(utt, owners, meta_ref, fbank_ref, blocks_ref):
    count = utt * owners
    owner = meta_ref[2 * count]
    dest = [jnp.int32(0)] * utt
    length = [jnp.int32(0)] * utt
    for index in range(count):
        place = meta_ref[count + index] - owner * utt
        half = lax.shift_right_logical(meta_ref[index], 1)
        for j in range(utt):
            hit = place == j
            dest[j] = jnp.where(hit, index // utt, dest[j])
            length[j] = jnp.where(hit, half, length[j])
    row, column = iotas((MOST, fbank_ref.shape[0]))
    begin = jnp.int32(0)
    for j in range(utt):
        chosen = (column == row + begin).astype(jnp.bfloat16)
        blocks_ref[dest[j]] = dot(chosen, fbank_ref[...]).astype(jnp.bfloat16)
        begin = begin + length[j]


def send_rows(meta, fbank, utt, owners):
    return pl.pallas_call(
        lambda *refs: send_kernel(utt, owners, *refs),
        in_specs=[pl.BlockSpec(memory_space=pltpu.SMEM)] + vmem(1),
        out_specs=vmem(1)[0],
        out_shape=jax.ShapeDtypeStruct((owners, MOST, fbank.shape[1]), jnp.bfloat16),
        compiler_params=pltpu.CompilerParams(vmem_limit_bytes=12 * 2**20),
        cost_estimate=pl.CostEstimate(flops=2 * 3 * MOST * 300 * 640, bytes_accessed=2 * 2**20, transcendentals=0),
        name="send_rows",
    )(meta, fbank)


def front_kernel(
    utt, owners, meta_ref, received_ref, sub_ref, gain_ref, cotangent_ref,
    norm_ref, dense_ref, select_ref, spaced_ref, wide_ref,
):
    count = utt * owners
    owner = meta_ref[2 * count]
    spaced, model = norm_ref.shape
    rows = dense_ref.shape[0]
    gap = EDGE // 2
    halves = [lax.shift_right_logical(meta_ref[owner * utt + k], 1) for k in range(utt)]
    row, column = iotas((spaced // 2, MOST))
    start = jnp.int32(0)
    pairs = jnp.zeros((spaced // 2, received_ref.shape[2]), jnp.float32)
    for k in range(utt):
        chosen = ((row == column + start) & (column < halves[k])).astype(jnp.bfloat16)
        loader = lax.div(meta_ref[count + owner * utt + k], jnp.int32(utt))
        pairs = pairs + dot(chosen, received_ref[loader])
        start = start + halves[k] + gap
    values = sub_ref.shape[0]
    even = dot(pairs[:, :values].astype(jnp.bfloat16), sub_ref[...]).astype(jnp.bfloat16)
    odd = dot(pairs[:, values:].astype(jnp.bfloat16), sub_ref[...]).astype(jnp.bfloat16)

    row, column = iotas((spaced, spaced // 2))
    wide_ref[...] = dot((row == 2 * column).astype(jnp.bfloat16), even) + dot(
        (row == 2 * column + 1).astype(jnp.bfloat16), odd
    )
    depth = 4 * SUBLANES if spaced % (4 * SUBLANES) == 0 else 2 * SUBLANES

    def normalise(index, carry):
        chunk = pl.ds(pl.multiple_of(index * depth, depth), depth)
        values = wide_ref[chunk, :]
        mean = jnp.sum(values, axis=1, keepdims=True) / model
        values = values - mean
        spread = jnp.sum(values * values, axis=1, keepdims=True) / model
        norm_ref[chunk, :] = (values * lax.rsqrt(spread + 1e-05) * gain_ref[...]).astype(jnp.bfloat16)
        return carry

    lax.fori_loop(0, spaced // depth, normalise, 0)

    def spread_out(frame):
        end = jnp.int32(0)
        moved = frame
        for k in range(utt - 1):
            end = end + 2 * halves[k]
            moved = moved + jnp.where(frame >= end, EDGE, 0)
        return moved

    frame, column = iotas((rows, spaced // 2))
    moved = spread_out(frame)
    dense_ref[...] = (
        dot((moved == 2 * column).astype(jnp.bfloat16), even)
        + dot((moved == 2 * column + 1).astype(jnp.bfloat16), odd)
    ).astype(jnp.bfloat16)
    frame, column = iotas((rows, spaced))
    select_ref[...] = (spread_out(frame) == column).astype(jnp.bfloat16)
    row, frame = iotas((spaced, rows))
    back = (spread_out(frame) == row).astype(jnp.bfloat16)
    spaced_ref[...] = dot(back, cotangent_ref[...]).astype(jnp.bfloat16)


def front(meta, received, w_sub, gain_in, cotangent, utt, owners):
    rows, model = cotangent.shape
    spaced = rows + EDGE * (utt - 1)
    bf16 = lambda *shape: jax.ShapeDtypeStruct(shape, jnp.bfloat16)
    return pl.pallas_call(
        lambda *refs: front_kernel(utt, owners, *refs),
        in_specs=[pl.BlockSpec(memory_space=pltpu.SMEM)] + vmem(4),
        out_specs=vmem(4),
        out_shape=[
            bf16(spaced, model), bf16(rows, model), bf16(rows, spaced), bf16(spaced, model),
        ],
        scratch_shapes=[pltpu.VMEM((spaced, model), jnp.float32)],
        compiler_params=pltpu.CompilerParams(vmem_limit_bytes=32 * 2**20),
        cost_estimate=pl.CostEstimate(flops=4 * 10**9, bytes_accessed=16 * 2**20, transcendentals=0),
        name="front",
    )(meta, received, w_sub, gain_in.reshape(1, model), cotangent)


def forward_kernel(
    norm_ref, value_ref, gate_ref, taps_ref, gain_ref, select_ref,
    glu_ref, centered_ref, rstd_ref, swished_ref, pad_ref, conv_ref, half_ref,
):
    step = pl.program_id(0)
    steps = pl.num_programs(0)
    rows, width = glu_ref.shape
    count = conv_ref.shape[0]
    blocks = width // LANES
    kernel = taps_ref.shape[0]
    weights = jnp.concatenate([value_ref[...], gate_ref[...]], axis=0)
    hidden = dot_t(norm_ref[...], weights)
    glu = (hidden[:, :width] * sigmoid(hidden[:, width:])).astype(jnp.bfloat16)
    glu_ref[...] = glu
    fill_padded(pad_ref, glu.astype(jnp.float32))
    size = row_chunk(rows)
    for index in range(blocks):
        lanes = slice(index * LANES, (index + 1) * LANES)
        for base in range(0, rows, size):
            total = jnp.zeros((size, LANES), jnp.float32)
            for tap, moved in windows(pad_ref.at[index], base, size, kernel):
                total = total + moved * taps_ref[tap : tap + 1, lanes]
            conv_ref[step * blocks + index, base : base + size, :] = total

    @pl.when(step == steps - 1)
    def _():
        model = count * LANES
        depth = 4 * SUBLANES if rows % (4 * SUBLANES) == 0 else 2 * SUBLANES

        def normalise(index, carry):
            chunk = pl.ds(pl.multiple_of(index * depth, depth), depth)
            parts = [conv_ref[block, chunk, :] for block in range(count)]
            mean = jnp.sum(sum(parts), axis=1, keepdims=True) / model
            parts = [part - mean for part in parts]
            spread = jnp.sum(sum(part * part for part in parts), axis=1, keepdims=True) / model
            rstd = lax.rsqrt(spread + 1e-05)
            rstd_ref[chunk, :] = jnp.broadcast_to(rstd, (depth, LANES))
            for block in range(count):
                centered = parts[block] * rstd
                centered_ref[block, chunk, :] = centered
                normed = centered * gain_ref[:, block * LANES : (block + 1) * LANES]
                half_ref[block // blocks, chunk, block % blocks * LANES : (block % blocks + 1) * LANES] = (
                    normed * sigmoid(normed)
                ).astype(jnp.bfloat16)
            return carry

        lax.fori_loop(0, rows // depth, normalise, 0)
        for slot in range(count // blocks):
            swished_ref[:, slot * width : (slot + 1) * width] = dot(
                select_ref[...], half_ref[slot]
            ).astype(jnp.bfloat16)


def forward(norm_in, first_t, taps, gain_mid, select):
    rows, model = norm_in.shape
    kernel = taps.shape[0]
    steps = FORWARD_STEPS
    width = model // steps
    dense = select.shape[0]
    whole = lambda step: (0, 0)
    return pl.pallas_call(
        forward_kernel,
        grid=(steps,),
        in_specs=[
            pl.BlockSpec((rows, model), whole),
            pl.BlockSpec((width, model), lambda step: (step, 0)),
            pl.BlockSpec((width, model), lambda step: (step + steps, 0)),
            pl.BlockSpec((kernel, width), lambda step: (0, step)),
            pl.BlockSpec((1, model), whole),
            pl.BlockSpec((dense, rows), whole),
        ],
        out_specs=[
            pl.BlockSpec((rows, width), lambda step: (0, step)),
            pl.BlockSpec((model // LANES, rows, LANES), lambda step: (0, 0, 0)),
            pl.BlockSpec((rows, LANES), whole),
            pl.BlockSpec((dense, model), whole),
        ],
        out_shape=[
            jax.ShapeDtypeStruct((rows, model), jnp.bfloat16),
            jax.ShapeDtypeStruct((model // LANES, rows, LANES), jnp.float32),
            jax.ShapeDtypeStruct((rows, LANES), jnp.float32),
            jax.ShapeDtypeStruct((dense, model), jnp.bfloat16),
        ],
        scratch_shapes=[
            pltpu.VMEM((width // LANES, rows + 2 * EDGE, LANES), jnp.float32),
            pltpu.VMEM((model // LANES, rows, LANES), jnp.float32),
            pltpu.VMEM((steps, rows, width), jnp.bfloat16),
        ],
        compiler_params=pltpu.CompilerParams(vmem_limit_bytes=50 * 2**20),
        cost_estimate=pl.CostEstimate(
            flops=4 * rows * model * model + 20 * kernel * rows * model,
            bytes_accessed=4 * model * model + 10 * rows * model,
            transcendentals=2 * rows * model,
        ),
        name="forward",
    )(norm_in, first_t, first_t, taps, gain_mid.reshape(1, model), select)


def backward_kernel(
    cotangent_ref, second_ref, slope_ref, centered_ref, rstd_ref, gain_ref, glu_ref,
    taps_out_ref, gain_out_ref, scaled_ref, sums_ref, pad_ref, part_ref,
):
    step = pl.program_id(0)
    steps = pl.num_programs(0) // 2
    rows, width = glu_ref.shape
    kernel = taps_out_ref.shape[0]
    blocks = width // LANES
    model = steps * width

    @pl.when(step == 0)
    def _():
        sums_ref[...] = jnp.zeros_like(sums_ref)

    @pl.when(step < steps)
    def _():
        d_swished = dot(cotangent_ref[...], second_ref[...])
        for index in range(blocks):
            scaled_ref[step * blocks + index] = d_swished[:, index * LANES : (index + 1) * LANES]
        depth = 4 * SUBLANES if rows % (4 * SUBLANES) == 0 else 2 * SUBLANES

        def chunk_step(number, totals):
            chunk = pl.ds(pl.multiple_of(number * depth, depth), depth)
            first = sums_ref[0, chunk, :]
            second = sums_ref[1, chunk, :]
            result = []
            for index in range(blocks):
                place = step * blocks + index
                scaled = scaled_ref[place, chunk, :] * slope_ref[index, chunk, :]
                scaled_ref[place, chunk, :] = scaled
                both = scaled * centered_ref[index, chunk, :]
                first = first + scaled
                second = second + both
                result.append(totals[index] + jnp.sum(both.reshape(-1, SUBLANES, LANES), axis=0))
            sums_ref[0, chunk, :] = first
            sums_ref[1, chunk, :] = second
            return tuple(result)

        zero = jnp.zeros((SUBLANES, LANES), jnp.float32)
        totals = lax.fori_loop(0, rows // depth, chunk_step, (zero,) * blocks)
        for index in range(blocks):
            lanes = slice(index * LANES, (index + 1) * LANES)
            gain_out_ref[:, lanes] = jnp.sum(totals[index], axis=0, keepdims=True) / gain_ref[:, lanes]

    @pl.when(step == steps)
    def _():
        for index in range(2):
            mean = jnp.sum(sums_ref[index], axis=1, keepdims=True) / model
            sums_ref[index] = jnp.broadcast_to(mean, (rows, LANES))

    @pl.when(step >= steps)
    def _():
        fill_padded(pad_ref, glu_ref[...].astype(jnp.float32))
        size = row_chunk(rows)
        for index in range(blocks):
            lanes = slice(index * LANES, (index + 1) * LANES)
            for base in range(0, rows, size):
                chunk = slice(base, base + size)
                d_conv = rstd_ref[chunk, :] * (
                    scaled_ref[(step - steps) * blocks + index, chunk, :]
                    - sums_ref[0, chunk, :]
                    - centered_ref[index, chunk, :] * sums_ref[1, chunk, :]
                )
                for tap, moved in windows(pad_ref.at[index], base, size, kernel):
                    term = jnp.sum((moved * d_conv).reshape(-1, SUBLANES, LANES), axis=0)
                    if base == 0:
                        part_ref[index, tap] = term
                    else:
                        part_ref[index, tap] += term
            taps_out_ref[:, lanes] = jnp.sum(part_ref[index], axis=1)


def backward(cotangent, second, slope, centered, rstd, gain_mid, glu, kernel):
    rows, model = cotangent.shape
    steps = BACKWARD_STEPS
    width = model // steps
    blocks = width // LANES
    whole = lambda step: (0, 0)
    early = lambda step: (0, jnp.minimum(step, steps - 1))
    late = lambda step: (0, jnp.maximum(step - steps, 0))
    return pl.pallas_call(
        backward_kernel,
        grid=(2 * steps,),
        in_specs=[
            pl.BlockSpec((rows, model), whole),
            pl.BlockSpec((model, width), early),
            pl.BlockSpec((blocks, rows, LANES), lambda step: (jnp.minimum(step, steps - 1), 0, 0)),
            pl.BlockSpec((blocks, rows, LANES), lambda step: (lax.rem(step, steps), 0, 0)),
            pl.BlockSpec((rows, LANES), whole),
            pl.BlockSpec((1, width), early),
            pl.BlockSpec((rows, width), late),
        ],
        out_specs=[pl.BlockSpec((kernel, width), late), pl.BlockSpec((1, width), early)],
        out_shape=[
            jax.ShapeDtypeStruct((kernel, model), jnp.float32),
            jax.ShapeDtypeStruct((1, model), jnp.float32),
        ],
        scratch_shapes=[
            pltpu.VMEM((model // LANES, rows, LANES), jnp.float32),
            pltpu.VMEM((2, rows, LANES), jnp.float32),
            pltpu.VMEM((blocks, rows + 2 * EDGE, LANES), jnp.float32),
            pltpu.VMEM((blocks, kernel, SUBLANES, LANES), jnp.float32),
        ],
        compiler_params=pltpu.CompilerParams(vmem_limit_bytes=54 * 2**20),
        cost_estimate=pl.CostEstimate(
            flops=2 * rows * model * model + 20 * kernel * rows * model,
            bytes_accessed=2 * model * model + 12 * rows * model,
            transcendentals=rows * model,
        ),
        name="backward",
    )(cotangent, second, slope, centered, rstd, gain_mid.reshape(1, model), glu)


def weight_kernel(mine_ref, theirs_ref, swished_ref, other_ref, out_ref):
    out_ref[...] = (dot(mine_ref[...], swished_ref[...]) + dot(theirs_ref[...], other_ref[...])).astype(jnp.bfloat16)


def weight_gradient(mine, theirs, swished, other):
    out, rows = mine.shape
    model = swished.shape[1]
    width = model // 3
    whole = pl.BlockSpec((out, rows), lambda step: (0, 0))
    block = pl.BlockSpec((rows, width), lambda step: (0, step))
    return pl.pallas_call(
        weight_kernel,
        grid=(model // width,),
        in_specs=[whole, whole, block, block],
        out_specs=pl.BlockSpec((out, width), lambda step: (0, step)),
        out_shape=jax.ShapeDtypeStruct((out, model), jnp.bfloat16),
        compiler_params=pltpu.CompilerParams(vmem_limit_bytes=16 * 2**20),
        cost_estimate=pl.CostEstimate(
            flops=4 * rows * out * model, bytes_accessed=2 * out * model, transcendentals=0
        ),
        name="weight_gradient",
    )(mine, theirs, swished, other)


def spread(values, axis):
    copies = jnp.broadcast_to(values[None], (lax.axis_size(axis),) + values.shape)
    return lax.all_to_all(copies, axis, 0, 0, tiled=True)


def at(array, index, axis=0):
    return lax.dynamic_index_in_dim(array, index, axis, False)


def barrier(values):
    return lax.optimization_barrier(values)


def scatter_plane(values, owner):
    owners = values.shape[0]
    side = 4 if owners % 4 == 0 else 1
    across, along = lax.rem(owner, side), lax.div(owner, side)
    values = values.reshape((owners // side, side) + values.shape[1:])
    total = at(values, across, 1)
    for k in range(1, side):
        moves = [(i, i // side * side + (i % side + k) % side) for i in range(owners)]
        total = total + lax.ppermute(at(values, lax.rem(across + k, side), 1), "dp", moves)
    values, count = total, owners // side
    total = at(values, along)
    for k in range(1, count):
        moves = [(i, (i // side + k) % count * side + i % side) for i in range(owners)]
        total = total + lax.ppermute(at(values, lax.rem(along + k, count)), "dp", moves)
    return total


def body(fbank, lengths, sources, w_sub, gain_in, w_first, taps, gain_mid, w_second, cotangent):
    owners = lax.axis_size("dp")
    groups = lax.axis_size("fsdp")
    chips = groups // 2
    owner = lax.axis_index("dp")
    group = lax.axis_index("fsdp")
    core = lax.rem(group, 2)
    load, width = fbank.shape[2:]
    rows, model = cotangent.shape[2:]
    kernel = taps.shape[0]
    utt = lengths.shape[2]
    own_rows = w_second.shape[0]
    own = own_rows // owners

    swap = lambda block: lax.ppermute(block, "fsdp", [(i, i ^ 1) for i in range(groups)])

    first_t = lax.all_gather(w_first.T, "fsdp", axis=0, tiled=True)
    second = lax.all_gather(w_second, "fsdp", axis=0, tiled=True)

    meta = jnp.concatenate(
        [at(lengths, group).reshape(-1), at(sources, group).reshape(-1), jnp.stack([owner, group])]
    )
    blocks = send_rows(meta, fbank.reshape(load, width), utt, owners)
    received = lax.all_to_all(blocks, "dp", 0, 0, tiled=True)

    grad_out = cotangent.reshape(rows, model)
    grad_t = grad_out.T.reshape(chips, 2, owners, own, rows)
    of_core = lambda side: jnp.swapaxes(at(grad_t, side, 1), 0, 1).reshape(chips * own_rows, rows)
    grad_mine, grad_theirs = of_core(core), swap(of_core(1 - core))

    norm_in, x0, select, grad_spaced = front(meta, received, w_sub, gain_in, grad_out, utt, owners)
    norm_in, grad_mine, grad_theirs = barrier((norm_in, grad_mine, grad_theirs))
    glu, centered, rstd, swished = forward(norm_in, first_t, taps, gain_mid, select)

    partial = weight_gradient(grad_mine, grad_theirs, swished, swap(swished))
    centered, partial = barrier((centered, partial))
    partial = lax.all_to_all(partial.reshape(owners, chips * own, model), "dp", 0, 0, tiled=True)

    gains = gain_mid.reshape(-1, 1, LANES)
    normed = centered * gains
    sig = sigmoid(normed)
    slope = gains * (sig * (1.0 + normed * (1.0 - sig)))
    taps_term, gain_term = backward(grad_spaced, second, slope, centered, rstd, gain_mid, glu, kernel)
    block = (x0.astype(jnp.float32) + dot_t(swished, second)).astype(jnp.bfloat16)

    small = jnp.concatenate([taps_term, gain_term], axis=0)
    small = scatter_plane(small.reshape(owners, -1, model), owner)
    partial = jnp.sum(partial.astype(jnp.float32), axis=0).astype(jnp.bfloat16).reshape(chips, own, model)

    small = (small + swap(small)).astype(jnp.bfloat16)
    both = jnp.concatenate([partial, jnp.broadcast_to(small[None], (chips,) + small.shape)], axis=1)
    same_core = [[2 * chip + side for chip in range(chips)] for side in range(2)]
    both = lax.all_to_all(both, "fsdp", 0, 0, tiled=True, axis_index_groups=same_core)
    both = jnp.sum(both.astype(jnp.float32), axis=0).astype(jnp.bfloat16)
    both = spread(both, "dp").astype(jnp.float32)
    grad_second = both[:, :own].reshape(own_rows, model)
    small = both[:, own:].reshape(kernel + 1, model)
    return (block.reshape(1, 1, rows, model), grad_second, small[:kernel], small[kernel])


def solution(mesh):
    in_specs = (
        P("dp", "fsdp", None, None),
        P(),
        P(),
        P(),
        P(),
        P(None, "fsdp"),
        P(),
        P(),
        P("fsdp", None),
        P("dp", "fsdp", None, None),
    )
    out_specs = (P("dp", "fsdp", None, None), P("fsdp", None), P(), P())
    return jax.shard_map(body, mesh=mesh, in_specs=in_specs, out_specs=out_specs, check_vma=False)
```

time: 212 us -> 197 us (0.929)
  between operations: 26 us -> 14.3 us
  matrix products: 16.5 us -> 5.37 us
  starting transfers between devices: 23.8 us -> 34.2 us
  waiting for transfers between devices: 54.7 us -> 46.7 us
  local copies, waits for them, and re-layouts: 23.3 us -> 27.3 us
    pallas_call x0 -> x3, Pallas kernels: none -> 14.2 us  [the longest x1 6.71 us: front(): pl.pallas_call(lambda *refs: front_kernel(utt, owners, *refs), in_specs=[...]
    dot_general x6 -> x1, matrix products: 16.5 us -> 5.37 us  [dot_t(): lax.dot_general(left, right, CONTRACT_LAST, preferred_element_type=jnp.fl...]
    ppermute x2 -> x9, waiting for transfers between devices: 2.81 us -> 13.5 us  [the longest x3 8.38 us: scatter_plane(): lax.ppermute(at(values, lax.rem(across + k, side), 1), 'dp', moves)]
    ppermute x2 -> x9, starting transfers between devices: 0.25 us -> 10.4 us  [the longest x3 5.43 us: scatter_plane(): lax.ppermute(at(values, lax.rem(along + k, count)), 'dp', moves)]
    all_to_all x1, waiting for transfers between devices: 7.31 us -> 0.01 us  [body(): lax.all_to_all(partial.reshape(owners, chips * own, model), 'dp', 0, 0, t...]
    transpose x0 -> x4, local copies, waits for them, and re-layouts: none -> 7.11 us  [the longest x3 5.7 us: body(): jnp.swapaxes(at(grad_t, side, 1), 0, 1).reshape(chips * own_rows, rows)]
    pallas_call x1, Pallas kernels: 19.7 us -> 13.5 us  [backward(): pl.pallas_call(backward_kernel, grid=(2 * steps,), in_specs=[pl.BlockSpec...]
    reshape x4 -> x7, local copies, waits for them, and re-layouts: 1.46 us -> 7.68 us  [the longest x2 4.14 us: body(): jnp.swapaxes(at(grad_t, side, 1), 0, 1).reshape(chips * own_rows, rows)]
  transfers between devices with their start and end apart: 9 -> 14, of which waited for: 8 -> 10; matrix products, arithmetic and copies ran while one was open for 17% -> 13% of each run, Pallas kernels for 21% -> 24%
where the time goes in v2:
time: 197 us
  waiting for transfers between devices  46.7 us (24%)
  Pallas kernels  46.3 us (24%)
  starting transfers between devices  34.2 us (17%)
  local copies, waits for them, and re-layouts  27.3 us (14%)
  blocking collectives  14.9 us (8%)
  between operations  14.3 us (7%)
  other arithmetic  7.54 us (4%)
  matrix products  5.37 us (3%)
    pallas_call x1, Pallas kernels, forward(): pl.pallas_call(forward_kernel, grid=(steps,), in_specs=[pl.BlockSpec((row...  18.6 us
    all_to_all x1, blocking collectives, body(): lax.all_to_all(both, 'fsdp', 0, 0, tiled=True, axis_index_groups=same_core)  14.9 us
    all_gather x1, waiting for transfers between devices, body(): first_t = lax.all_gather(w_first.T, 'fsdp', axis=0, tiled=True)  13.5 us
    pallas_call x1, Pallas kernels, backward(): pl.pallas_call(backward_kernel, grid=(2 * steps,), in_specs=[pl.BlockSpec...  13.5 us
    all_to_all x1, waiting for transfers between devices, body(): received = lax.all_to_all(blocks, 'dp', 0, 0, tiled=True)  12.9 us
    unnamed x34, local copies, waits for them, and re-layouts  8.86 us
    all_to_all x1, starting transfers between devices, spread(): return lax.all_to_all(copies, axis, 0, 0, tiled=True)  8.86 us
    ppermute x3, waiting for transfers between devices, scatter_plane(): lax.ppermute(at(values, lax.rem(across + k, side), 1), 'dp', moves)  8.38 us
  transfers between devices with their start and end apart: 14, of which 10 were waited for; matrix products, arithmetic and copies ran while one was open for 13% of the time, Pallas kernels for 24%

profile of v2, /device:TPU:2, one launch (start us, length us, event | category | flops | bytes accessed | tf_op | source)
XLA Modules:
  0.0 196.7 jit_solution(18080847796694099812)
XLA Ops:
  10.8 2.4 %send_rows.1 = bf16[16,104,640]{2,1,0:T(8,128)(2,1)} custom-call(s32[98]{0:T(128)S(1)} %pad_add_fusion.refs_0_, bf16[300,640]{1,0:T(8,128)(2,1)S(1)} %bitcast.48), custom_call_target="tpu_custom_call" | custom-call | flops 119808000 | bytes 2097152 | tf_op jit(solution)/shard_map/send_rows/pallas_call | solution.py:87
  13.2 7.6 %all-to-all-start = ((bf16[16,104,640]{2,1,0:T(8,128)(2,1)}), bf16[16,104,640]{2,1,0:T(8,128)(2,1)S(1)}, u32[]{:S(2)}, u32[]{:S(2)}) async-start(bf16[16,104,640]{2,1,0:T(8,128)(2,1)} %send_rows.1), calls=%async_computation | async-start | bytes 4259840 | tf_op jit(solution)/shard_map/all_to_all | solution.py:465
  22.2 3.3 %reshape.62 = bf16[8,2,16,6,384]{4,3,2,1,0:T(8,128)(2,1)} reshape(bf16[1536,384]{1,0:T(8,128)(2,1)} %copy.23) | data formatting | bytes 2359296 | tf_op jit(solution)/shard_map/reshape | solution.py:468
  25.5 2.4 %dynamic-slice_bitcast_fusion = (bf16[16,8,6,384]{3,2,0,1:T(8,128)(2,1)S(1)}, bf16[16,8,6,384]{3,2,0,1:T(8,128)(2,1)}) fusion(bf16[8,2,16,6,384]{4,3,2,1,0:T(8,128)(2,1)} %reshape.62, s32[]{:T(128)S(6)} %select_n.40, s32[]{:T(128)S(6)} %select_n.39), kind=kLoop, calls=%fused_computation.4 | loop fusion | bytes 2359304 | tf_op jit(solution)/shard_map/transpose | solution.py:469
  29.0 2.1 %reshape.64 = bf16[768,384]{1,0:T(8,128)(2,1)} reshape(bf16[16,8,6,384]{3,2,1,0:T(8,128)(2,1)} %copy.27) | data formatting | bytes 1179648 | tf_op jit(solution)/shard_map/reshape | solution.py:469
  31.1 2.2 %copy.25 = bf16[16,8,6,384]{3,2,1,0:T(8,128)(2,1)} copy(bf16[16,8,6,384]{3,2,0,1:T(8,128)(2,1)} %get-tuple-element.35) | data formatting | bytes 1179648 | tf_op jit(solution)/shard_map/transpose | solution.py:469
  35.4 12.9 %all-to-all-done.refs_1_ = bf16[16,104,640]{2,1,0:T(8,128)(2,1)S(1)} async-done(((bf16[16,104,640]{2,1,0:T(8,128)(2,1)}), bf16[16,104,640]{2,1,0:T(8,128)(2,1)S(1)}, u32[]{:S(2)}, u32[]{:S(2)}) %all-to-all-start) | async-done | bytes 2129952 | tf_op jit(solution)/shard_map/all_to_all | solution.py:465
  49.5 6.7 %front.1 = (bf16[416,1536]{1,0:T(8,128)(2,1)S(1)}, bf16[384,1536]{1,0:T(8,128)(2,1)S(1)}, bf16[384,416]{1,0:T(8,128)(2,1)S(1)}, bf16[416,1536]{1,0:T(8,128)(2,1)S(1)}) custom-call(s32[98]{0:T(128)S(1)} %pad_add_fusion.refs_0_, bf16[16,104,640]{2,1,0:T(8,128)(2,1)S(1)} %all-to-all-done.refs_1_, bf16[320,1536]{1,0:T(8,128)(2,1)S(1)} %copy-done.11, ...), custom_call_target="tpu_custom_call" | custom-call | flops 4000000000 | bytes 16777216 | tf_op jit(solution)/shard_map/front/pallas_call | solution.py:162
  60.1 13.5 %all-gather.3.cloned.1.call-done.value_ref.gate_ref = bf16[3072,1536]{1,0:T(8,128)(2,1)} async-done(((bf16[192,1536]{1,0:T(8,128)(2,1)}), bf16[3072,1536]{1,0:T(8,128)(2,1)}) %all-gather.3.cloned.1.call-update) | async-done | bytes 9437200 | tf_op jit(solution)/shard_map/all_gather | solution.py:458
  74.7 18.6 %forward.1 = (bf16[416,1536]{1,0:T(8,128)(2,1)S(1)}, f32[12,416,128]{2,1,0:T(8,128)}, f32[416,128]{1,0:T(8,128)S(1)}, bf16[384,1536]{1,0:T(8,128)(2,1)S(1)}) custom-call(bf16[416,1536]{1,0:T(8,128)(2,1)} %copy-done, bf16[3072,1536]{1,0:T(8,128)(2,1)} %all-gather.3.cloned.1.call-done.value_ref.gate_ref, ...), custom_call_target="tpu_custom_call" | custom-call | flops 4322033664 | bytes 15826944 | tf_op jit(solution)/shard_map/forward/pallas_call | solution.py:236
  95.2 2.6 %collective-permute-done.1.other_ref = bf16[384,1536]{1,0:T(8,128)(2,1)S(1)} collective-permute-done((bf16[384,1536]{1,0:T(8,128)(2,1)S(1)}, bf16[384,1536]{1,0:T(8,128)(2,1)S(1)}, u32[]{:S(2)}, u32[]{:S(2)}) %collective-permute-start.1) | collective-permute-done | bytes 1179680 | tf_op jit(solution)/shard_map/ppermute | solution.py:456
  97.8 5.1 %weight_gradient.1 = bf16[768,1536]{1,0:T(8,128)(2,1)} custom-call(bf16[768,384]{1,0:T(8,128)(2,1)S(1)} %copy-done.4, bf16[768,384]{1,0:T(8,128)(2,1)} %collective-permute-done.theirs_ref, bf16[384,1536]{1,0:T(8,128)(2,1)S(1)} %get-tuple-element.23.swished_ref, bf16[384,1536]{1,0:T(8,128)(2,1)S(1)} %collective-permute-done.1.other_ref), custom_call_target="tpu_custom_call" | custom-call | flops 1811939328 | bytes 2359296 | tf_op jit(solution)/shard_map/weight_gradient/pallas_call | solution.py:398
  102.9 7.3 %all-to-all-start.1 = ((bf16[16,48,1536]{2,1,0:T(8,128)(2,1)}), bf16[16,48,1536]{2,1,0:T(8,128)(2,1)}, u32[]{:S(2)}, u32[]{:S(2)}) async-start(bf16[16,48,1536]{2,1,0:T(8,128)(2,1)} %bitcast.13), calls=%async_computation.1 | async-start | bytes 4718592 | tf_op jit(solution)/shard_map/all_to_all | solution.py:478
  110.2 4.2 %multiply_multiply_fusion.slope_ref = f32[12,416,128]{2,1,0:T(8,128)} fusion(f32[12,416,128]{2,1,0:T(8,128)} %get-tuple-element.29.centered_ref, f32[12,128]{1,0:T(8,128)S(1)} %bitcast.51), kind=kLoop, calls=%fused_computation.3 | loop fusion | flops 5750784 | bytes 5117952 | tf_op jit(solution)/shard_map/mul | solution.py:483
  114.4 2.7 %all-gather.5.cloned.1.call-done.second_ref = bf16[1536,1536]{1,0:T(8,128)(2,1)} async-done(((bf16[96,1536]{1,0:T(8,128)(2,1)}), bf16[1536,1536]{1,0:T(8,128)(2,1)}) %all-gather.5.cloned.1.call-update) | async-done | bytes 4718608 | tf_op jit(solution)/shard_map/all_gather | solution.py:459
  117.1 13.5 %backward.1 = (f32[31,1536]{1,0:T(8,128)}, f32[1,1536]{1,0:T(1,128)}) custom-call(bf16[416,1536]{1,0:T(8,128)(2,1)} %copy-done.1, bf16[1536,1536]{1,0:T(8,128)(2,1)} %all-gather.5.cloned.1.call-done.second_ref, f32[12,416,128]{2,1,0:T(8,128)} %multiply_multiply_fusion.slope_ref, f32[12,416,128]{2,1,0:T(8,128)} %get-tuple-element.29.centered_ref, ...), custom_call_target="tpu_custom_call" | custom-call | flops 2359099392 | bytes 12386304 | tf_op jit(solution)/shard_map/backward/pallas_call | solution.py:355
  136.4 7.6 %collective-permute-done.2 = f32[4,2,1536]{2,1,0:T(2,128)S(1)} collective-permute-done((f32[4,2,1536]{2,1,0:T(2,128)S(1)}, f32[4,2,1536]{2,1,0:T(2,128)S(1)}, u32[]{:S(2)}, u32[]{:S(2)}) %collective-permute-start.2) | collective-permute-done | bytes 49184 | tf_op jit(solution)/shard_map/ppermute | solution.py:433
  145.0 2.8 %collective-permute-start.6 = (f32[2,1536]{1,0:T(2,128)S(1)}, f32[2,1536]{1,0:T(2,128)S(1)}, u32[]{:S(2)}, u32[]{:S(2)}) collective-permute-start(f32[2,1536]{1,0:T(2,128)S(1)} %get-tuple-element.41), channel_id=1, source_target_pairs={{0,128},{16,144},{32,160},{48,176},{64,192},{80,208},{96,224},{112... | collective-permute-start | bytes 36872 | tf_op jit(solution)/shard_map/ppermute | solution.py:438
  147.8 2.5 %collective-permute-start.7 = (f32[2,1536]{1,0:T(2,128)S(1)}, f32[2,1536]{1,0:T(2,128)S(1)}, u32[]{:S(2)}, u32[]{:S(2)}) collective-permute-start(f32[2,1536]{1,0:T(2,128)S(1)} %get-tuple-element.40), channel_id=1, source_target_pairs={{0,192},{16,208},{32,224},{48,240},{64,0},{80,16},{96,32},{112,48}... | collective-permute-start | bytes 36872 | tf_op jit(solution)/shard_map/ppermute | solution.py:438
  153.0 2.1 %reduce_sum.24 = bf16[48,1536]{1,0:T(8,128)(2,1)S(1)} reduce(bf16[16,48,1536]{2,1,0:T(8,128)(2,1)} %all-to-all-done.1, bf16[]{:T(256)} %constant.72.clone.1), dimensions={0}, to_apply=%region_0.1 | reduce | flops 1105920 | bytes 2506754 | tf_op jit(solution)/shard_map/reduce_sum | solution.py:489
  155.3 14.9 %all_to_all.20 = bf16[8,8,1536]{2,1,0:T(8,128)(2,1)S(1)} all-to-all(bf16[8,8,1536]{2,1,0:T(8,128)(2,1)S(1)} %pad_maximum_fusion.1), channel_id=1, replica_groups={{0,2,4,6,8,10,12,14},{1,3,5,7,9,11,13,15},{16,18,20,22,24,26,28,30},{17..., dimensions={0} | all-to-all | bytes 393216 | tf_op jit(solution)/shard_map/all_to_all | solution.py:494
  171.0 8.9 %all-to-all-start.3 = ((bf16[16,8,1536]{2,1,0:T(8,128)(2,1)}), bf16[16,8,1536]{2,1,0:T(8,128)(2,1)S(1)}, u32[]{:S(2)}, u32[]{:S(2)}) async-start(bf16[16,8,1536]{2,1,0:T(8,128)(2,1)} %broadcast_in_dim.5), calls=%async_computation.3 | async-start | bytes 786432 | tf_op jit(solution)/shard_map/all_to_all | solution.py:414
  179.9 5.4 %fusion.1 = bf16[1,1,384,1536]{3,2,1,0:T(8,128)(2,1)} fusion(bf16[384,1536]{1,0:T(8,128)(2,1)S(1)} %get-tuple-element.23.swished_ref, bf16[1536,1536]{1,0:T(8,128)(2,1)} %all-gather.5.cloned.1.call-done.second_ref, bf16[384,1536]{1,0:T(8,128)(2,1)S(1)} %copy-done.13), kind=kOutput, calls=%fused_computation.2 | convolution fusion | flops 1813708800 | bytes 8257536 | tf_op jit(solution)/shard_map/dot_general | solution.py:55
  185.3 2.7 %all-to-all-done.3 = bf16[16,8,1536]{2,1,0:T(8,128)(2,1)S(1)} async-done(((bf16[16,8,1536]{2,1,0:T(8,128)(2,1)}), bf16[16,8,1536]{2,1,0:T(8,128)(2,1)S(1)}, u32[]{:S(2)}, u32[]{:S(2)}) %all-to-all-start.3) | async-done | bytes 393248 | tf_op jit(solution)/shard_map/all_to_all | solution.py:414
  (81 shorter events, 28.5 us)
Async XLA Ops:
  7.2 66.5 %all-gather.3.cloned.1.call-start = ((), (), s32[]{:S(2)}) async-start(), calls=%async_computation.4 | async-start | bytes 10027008 | tf_op jit(solution)/shard_map/all_gather | solution.py:458
  7.9 109.2 %all-gather.5.cloned.1.call-start = ((), (), s32[]{:S(2)}) async-start(), calls=%async_computation.5 | async-start | bytes 5013504 | tf_op jit(solution)/shard_map/all_gather | solution.py:459
  13.2 7.6 %copy-start.3 = (bf16[1,1,384,1536]{3,2,1,0:T(8,128)(2,1)S(1)}, bf16[1,1,384,1536]{3,2,1,0:T(8,128)(2,1)}, u32[]{:S(2)}) copy-start(bf16[1,1,384,1536]{3,2,1,0:T(8,128)(2,1)} %param.19) | copy-start | bytes 3538948
  13.2 35.1 %all-to-all-start = ((bf16[16,104,640]{2,1,0:T(8,128)(2,1)}), bf16[16,104,640]{2,1,0:T(8,128)(2,1)S(1)}, u32[]{:S(2)}, u32[]{:S(2)}) async-start(bf16[16,104,640]{2,1,0:T(8,128)(2,1)} %send_rows.1), calls=%async_computation | async-start | bytes 4259840 | tf_op jit(solution)/shard_map/all_to_all | solution.py:465
  29.0 6.4 %copy-start.16 = (f32[1536]{0:T(1024)S(1)}, f32[1536]{0:T(1024)}, u32[]{:S(2)}) copy-start(f32[1536]{0:T(1024)} %param.14) | copy-start | bytes 18436
  29.0 6.4 %copy-start.15 = (f32[1536]{0:T(1024)S(1)}, f32[1536]{0:T(1024)}, u32[]{:S(2)}) copy-start(f32[1536]{0:T(1024)} %param.17) | copy-start | bytes 18436
  31.1 29.0 %collective-permute-start = (bf16[768,384]{1,0:T(8,128)(2,1)}, bf16[768,384]{1,0:T(8,128)(2,1)}, u32[]{:S(2)}, u32[]{:S(2)}) collective-permute-start(bf16[768,384]{1,0:T(8,128)(2,1)} %reshape.64), channel_id=1, source_target_pairs={{0,1},{1,0},{2,3},{3,2},{4,5},{5,4},{6,7},{7,6},{8,9},{9,8},{10,11... | collective-permute-start | bytes 1769480 | tf_op jit(solution)/shard_map/ppermute | solution.py:456
  35.4 38.3 %copy-start.10 = (f32[1,1536]{1,0:T(1,128)}, f32[1,1536]{1,0:T(1,128)S(1)}, u32[]{:S(2)}) copy-start(f32[1,1536]{1,0:T(1,128)S(1)} %reshape.65.gain_ref) | copy-start | bytes 18436
  48.3 1.2 copy-start.11
  49.5 24.2 %copy-start.9 = (f32[31,1536]{1,0:T(8,128)S(1)}, f32[31,1536]{1,0:T(8,128)}, u32[]{:S(2)}) copy-start(f32[31,1536]{1,0:T(8,128)} %taps_ref.1) | copy-start | bytes 571396
  56.2 1.1 copy-start
  57.3 1.1 copy-start.1
  74.7 23.1 %copy-start.4 = (bf16[768,384]{1,0:T(8,128)(2,1)S(1)}, bf16[768,384]{1,0:T(8,128)(2,1)}, u32[]{:S(2)}) copy-start(bf16[768,384]{1,0:T(8,128)(2,1)} %reshape.63.mine_ref) | copy-start | bytes 1769476
  95.0 2.8 %collective-permute-start.1 = (bf16[384,1536]{1,0:T(8,128)(2,1)S(1)}, bf16[384,1536]{1,0:T(8,128)(2,1)S(1)}, u32[]{:S(2)}, u32[]{:S(2)}) collective-permute-start(bf16[384,1536]{1,0:T(8,128)(2,1)S(1)} %get-tuple-element.23.swished_ref), channel_id=1, source_target_pairs={{0,1},{1,0},{2,3},{3,2},{4,5},{5,4},{6,7},{7,6},{8,9},{9,8},{10,11... | collective-permute-start | bytes 3538952 | tf_op jit(solution)/shard_map/ppermute | solution.py:456
  102.9 50.1 %all-to-all-start.1 = ((bf16[16,48,1536]{2,1,0:T(8,128)(2,1)}), bf16[16,48,1536]{2,1,0:T(8,128)(2,1)}, u32[]{:S(2)}, u32[]{:S(2)}) async-start(bf16[16,48,1536]{2,1,0:T(8,128)(2,1)} %bitcast.13), calls=%async_computation.1 | async-start | bytes 4718592 | tf_op jit(solution)/shard_map/all_to_all | solution.py:478
  131.8 12.2 %collective-permute-start.2 = (f32[4,2,1536]{2,1,0:T(2,128)S(1)}, f32[4,2,1536]{2,1,0:T(2,128)S(1)}, u32[]{:S(2)}, u32[]{:S(2)}) collective-permute-start(f32[4,2,1536]{2,1,0:T(2,128)S(1)} %get-tuple-element.36), channel_id=1, source_target_pairs={{0,16},{16,32},{32,48},{48,0},{64,80},{80,96},{96,112},{112,64},{1... | collective-permute-start | bytes 147464 | tf_op jit(solution)/shard_map/ppermute | solution.py:433
  133.2 11.1 %collective-permute-start.3 = (f32[4,2,1536]{2,1,0:T(2,128)S(1)}, f32[4,2,1536]{2,1,0:T(2,128)S(1)}, u32[]{:S(2)}, u32[]{:S(2)}) collective-permute-start(f32[4,2,1536]{2,1,0:T(2,128)S(1)} %get-tuple-element.38), channel_id=1, source_target_pairs={{0,32},{16,48},{32,0},{48,16},{64,96},{80,112},{96,64},{112,80},{1... | collective-permute-start | bytes 147464 | tf_op jit(solution)/shard_map/ppermute | solution.py:433
  134.3 10.5 %collective-permute-start.4 = (f32[4,2,1536]{2,1,0:T(2,128)S(1)}, f32[4,2,1536]{2,1,0:T(2,128)S(1)}, u32[]{:S(2)}, u32[]{:S(2)}) collective-permute-start(f32[4,2,1536]{2,1,0:T(2,128)S(1)} %get-tuple-element.37), channel_id=1, source_target_pairs={{0,48},{16,0},{32,16},{48,32},{64,112},{80,64},{96,80},{112,96},{1... | collective-permute-start | bytes 147464 | tf_op jit(solution)/shard_map/ppermute | solution.py:433
  144.9 5.4 %collective-permute-start.5 = (f32[2,1536]{1,0:T(2,128)S(1)}, f32[2,1536]{1,0:T(2,128)S(1)}, u32[]{:S(2)}, u32[]{:S(2)}) collective-permute-start(f32[2,1536]{1,0:T(2,128)S(1)} %get-tuple-element.39), channel_id=1, source_target_pairs={{0,64},{16,80},{32,96},{48,112},{64,128},{80,144},{96,160},{112,17... | collective-permute-start | bytes 36872 | tf_op jit(solution)/shard_map/ppermute | solution.py:438
  145.0 5.4 %collective-permute-start.6 = (f32[2,1536]{1,0:T(2,128)S(1)}, f32[2,1536]{1,0:T(2,128)S(1)}, u32[]{:S(2)}, u32[]{:S(2)}) collective-permute-start(f32[2,1536]{1,0:T(2,128)S(1)} %get-tuple-element.41), channel_id=1, source_target_pairs={{0,128},{16,144},{32,160},{48,176},{64,192},{80,208},{96,224},{112... | collective-permute-start | bytes 36872 | tf_op jit(solution)/shard_map/ppermute | solution.py:438
  147.8 3.9 %collective-permute-start.7 = (f32[2,1536]{1,0:T(2,128)S(1)}, f32[2,1536]{1,0:T(2,128)S(1)}, u32[]{:S(2)}, u32[]{:S(2)}) collective-permute-start(f32[2,1536]{1,0:T(2,128)S(1)} %get-tuple-element.40), channel_id=1, source_target_pairs={{0,192},{16,208},{32,224},{48,240},{64,0},{80,16},{96,32},{112,48}... | collective-permute-start | bytes 36872 | tf_op jit(solution)/shard_map/ppermute | solution.py:438
  151.7 1.3 collective-permute-start.8
  153.0 26.9 %copy-start.13 = (bf16[384,1536]{1,0:T(8,128)(2,1)S(1)}, bf16[384,1536]{1,0:T(8,128)(2,1)}, u32[]{:S(2)}) copy-start(bf16[384,1536]{1,0:T(8,128)(2,1)} %copy-done.12) | copy-start | bytes 3538948
  171.0 16.9 %all-to-all-start.3 = ((bf16[16,8,1536]{2,1,0:T(8,128)(2,1)}), bf16[16,8,1536]{2,1,0:T(8,128)(2,1)S(1)}, u32[]{:S(2)}, u32[]{:S(2)}) async-start(bf16[16,8,1536]{2,1,0:T(8,128)(2,1)} %broadcast_in_dim.5), calls=%async_computation.3 | async-start | bytes 786432 | tf_op jit(solution)/shard_map/all_to_all | solution.py:414
  (7 other events, 6.2 us)
Sparse Core Ops, SparseCore 0:
  9.8 63.7 all-gather.2
  75.5 41.5 all-gather.4

commit v3 on v2

--- a/solution.py
+++ b/solution.py
@@ -61,6 +61,20 @@
 
 def vmem(count):
     return [pl.BlockSpec(memory_space=pltpu.VMEM)] * count
+
+
+def own_halves(meta_ref, utt, owners):
+    owner = meta_ref[2 * utt * owners]
+    return [lax.shift_right_logical(meta_ref[owner * utt + k], 1) for k in range(utt)]
+
+
+def spaced_row(frame, halves):
+    end = jnp.int32(0)
+    moved = frame
+    for half in halves[:-1]:
+        end = end + 2 * half
+        moved = moved + jnp.where(frame >= end, EDGE, 0)
+    return moved
 
 
 def send_kernel(utt, owners, meta_ref, fbank_ref, blocks_ref):
@@ -97,14 +111,14 @@
 
 def front_kernel(
     utt, owners, meta_ref, received_ref, sub_ref, gain_ref, cotangent_ref,
-    norm_ref, dense_ref, select_ref, spaced_ref, wide_ref,
+    norm_ref, dense_ref, spaced_ref, wide_ref,
 ):
     count = utt * owners
     owner = meta_ref[2 * count]
     spaced, model = norm_ref.shape
     rows = dense_ref.shape[0]
     gap = EDGE // 2
-    halves = [lax.shift_right_logical(meta_ref[owner * utt + k], 1) for k in range(utt)]
+    halves = own_halves(meta_ref, utt, owners)
     row, column = iotas((spaced // 2, MOST))
     start = jnp.int32(0)
     pairs = jnp.zeros((spaced // 2, received_ref.shape[2]), jnp.float32)
@@ -134,24 +148,14 @@
 
     lax.fori_loop(0, spaced // depth, normalise, 0)
 
-    def spread_out(frame):
-        end = jnp.int32(0)
-        moved = frame
-        for k in range(utt - 1):
-            end = end + 2 * halves[k]
-            moved = moved + jnp.where(frame >= end, EDGE, 0)
-        return moved
-
     frame, column = iotas((rows, spaced // 2))
-    moved = spread_out(frame)
+    moved = spaced_row(frame, halves)
     dense_ref[...] = (
         dot((moved == 2 * column).astype(jnp.bfloat16), even)
         + dot((moved == 2 * column + 1).astype(jnp.bfloat16), odd)
     ).astype(jnp.bfloat16)
-    frame, column = iotas((rows, spaced))
-    select_ref[...] = (spread_out(frame) == column).astype(jnp.bfloat16)
     row, frame = iotas((spaced, rows))
-    back = (spread_out(frame) == row).astype(jnp.bfloat16)
+    back = (spaced_row(frame, halves) == row).astype(jnp.bfloat16)
     spaced_ref[...] = dot(back, cotangent_ref[...]).astype(jnp.bfloat16)
 
 
@@ -162,9 +166,9 @@
     return pl.pallas_call(
         lambda *refs: front_kernel(utt, owners, *refs),
         in_specs=[pl.BlockSpec(memory_space=pltpu.SMEM)] + vmem(4),
-        out_specs=vmem(4),
+        out_specs=vmem(3),
         out_shape=[
-            bf16(spaced, model), bf16(rows, model), bf16(rows, spaced), bf16(spaced, model),
+            bf16(spaced, model), bf16(rows, model), bf16(spaced, model),
         ],
         scratch_shapes=[pltpu.VMEM((spaced, model), jnp.float32)],
         compiler_params=pltpu.CompilerParams(vmem_limit_bytes=32 * 2**20),
@@ -174,8 +178,8 @@
 
 
 def forward_kernel(
-    norm_ref, value_ref, gate_ref, taps_ref, gain_ref, select_ref,
-    glu_ref, centered_ref, rstd_ref, swished_ref, pad_ref, conv_ref, half_ref,
+    utt, owners, meta_ref, norm_ref, value_ref, gate_ref, taps_ref, gain_ref,
+    glu_ref, conv_out_ref, mean_ref, rstd_ref, swished_ref, pad_ref, conv_ref, half_ref,
 ):
     step = pl.program_id(0)
     steps = pl.num_programs(0)
@@ -183,9 +187,13 @@
     count = conv_ref.shape[0]
     blocks = width // LANES
     kernel = taps_ref.shape[0]
-    weights = jnp.concatenate([value_ref[...], gate_ref[...]], axis=0)
-    hidden = dot_t(norm_ref[...], weights)
-    glu = (hidden[:, :width] * sigmoid(hidden[:, width:])).astype(jnp.bfloat16)
+    @pl.when(step == 0)
+    def _():
+        mean_ref[...] = jnp.zeros_like(mean_ref)
+
+    value = dot_t(norm_ref[...], value_ref[...])
+    gate = dot_t(norm_ref[...], gate_ref[...])
+    glu = (value * sigmoid(gate)).astype(jnp.bfloat16)
     glu_ref[...] = glu
     fill_padded(pad_ref, glu.astype(jnp.float32))
     size = row_chunk(rows)
@@ -196,6 +204,8 @@
             for tap, moved in windows(pad_ref.at[index], base, size, kernel):
                 total = total + moved * taps_ref[tap : tap + 1, lanes]
             conv_ref[step * blocks + index, base : base + size, :] = total
+            conv_out_ref[index, base : base + size, :] = total
+            mean_ref[base : base + size, :] += total
 
     @pl.when(step == steps - 1)
     def _():
@@ -205,54 +215,54 @@
         def normalise(index, carry):
             chunk = pl.ds(pl.multiple_of(index * depth, depth), depth)
             parts = [conv_ref[block, chunk, :] for block in range(count)]
-            mean = jnp.sum(sum(parts), axis=1, keepdims=True) / model
+            mean = jnp.sum(mean_ref[chunk, :], axis=1, keepdims=True) / model
+            mean_ref[chunk, :] = jnp.broadcast_to(mean, (depth, LANES))
             parts = [part - mean for part in parts]
             spread = jnp.sum(sum(part * part for part in parts), axis=1, keepdims=True) / model
             rstd = lax.rsqrt(spread + 1e-05)
             rstd_ref[chunk, :] = jnp.broadcast_to(rstd, (depth, LANES))
             for block in range(count):
-                centered = parts[block] * rstd
-                centered_ref[block, chunk, :] = centered
-                normed = centered * gain_ref[:, block * LANES : (block + 1) * LANES]
+                normed = parts[block] * rstd * gain_ref[:, block * LANES : (block + 1) * LANES]
                 half_ref[block // blocks, chunk, block % blocks * LANES : (block % blocks + 1) * LANES] = (
                     normed * sigmoid(normed)
                 ).astype(jnp.bfloat16)
             return carry
 
-        lax.fori_loop(0, rows // depth, normalise, 0)
+        lax.fori_loop(0, rows // depth, normalise, 0, unroll=True)
+        frame, column = iotas((swished_ref.shape[0], rows))
+        chosen = (spaced_row(frame, own_halves(meta_ref, utt, owners)) == column).astype(jnp.bfloat16)
         for slot in range(count // blocks):
-            swished_ref[:, slot * width : (slot + 1) * width] = dot(
-                select_ref[...], half_ref[slot]
-            ).astype(jnp.bfloat16)
-
-
-def forward(norm_in, first_t, taps, gain_mid, select):
+            swished_ref[:, slot * width : (slot + 1) * width] = dot(chosen, half_ref[slot]).astype(jnp.bfloat16)
+
+
+def forward(meta, norm_in, first_t, taps, gain_mid, dense, utt, owners):
     rows, model = norm_in.shape
     kernel = taps.shape[0]
     steps = FORWARD_STEPS
     width = model // steps
-    dense = select.shape[0]
     whole = lambda step: (0, 0)
     return pl.pallas_call(
-        forward_kernel,
+        lambda *refs: forward_kernel(utt, owners, *refs),
         grid=(steps,),
         in_specs=[
+            pl.BlockSpec(memory_space=pltpu.SMEM),
             pl.BlockSpec((rows, model), whole),
             pl.BlockSpec((width, model), lambda step: (step, 0)),
             pl.BlockSpec((width, model), lambda step: (step + steps, 0)),
             pl.BlockSpec((kernel, width), lambda step: (0, step)),
             pl.BlockSpec((1, model), whole),
-            pl.BlockSpec((dense, rows), whole),
         ],
         out_specs=[
             pl.BlockSpec((rows, width), lambda step: (0, step)),
-            pl.BlockSpec((model // LANES, rows, LANES), lambda step: (0, 0, 0)),
+            pl.BlockSpec((width // LANES, rows, LANES), lambda step: (step, 0, 0)),
+            pl.BlockSpec((rows, LANES), whole),
             pl.BlockSpec((rows, LANES), whole),
             pl.BlockSpec((dense, model), whole),
         ],
         out_shape=[
             jax.ShapeDtypeStruct((rows, model), jnp.bfloat16),
             jax.ShapeDtypeStruct((model // LANES, rows, LANES), jnp.float32),
+            jax.ShapeDtypeStruct((rows, LANES), jnp.float32),
             jax.ShapeDtypeStruct((rows, LANES), jnp.float32),
             jax.ShapeDtypeStruct((dense, model), jnp.bfloat16),
         ],
@@ -268,17 +278,17 @@
             transcendentals=2 * rows * model,
         ),
         name="forward",
-    )(norm_in, first_t, first_t, taps, gain_mid.reshape(1, model), select)
+    )(meta, norm_in, first_t, first_t, taps, gain_mid.reshape(1, model))
 
 
 def backward_kernel(
     cotangent_ref, second_ref, slope_ref, centered_ref, rstd_ref, gain_ref, glu_ref,
-    taps_out_ref, gain_out_ref, scaled_ref, sums_ref, pad_ref, part_ref,
+    small_ref, scaled_ref, sums_ref, pad_ref, part_ref,
 ):
     step = pl.program_id(0)
     steps = pl.num_programs(0) // 2
     rows, width = glu_ref.shape
-    kernel = taps_out_ref.shape[0]
+    kernel = small_ref.shape[0] - 1
     blocks = width // LANES
     model = steps * width
 
@@ -314,7 +324,8 @@
         totals = lax.fori_loop(0, rows // depth, chunk_step, (zero,) * blocks)
         for index in range(blocks):
             lanes = slice(index * LANES, (index + 1) * LANES)
-            gain_out_ref[:, lanes] = jnp.sum(totals[index], axis=0, keepdims=True) / gain_ref[:, lanes]
+            place = pl.ds(pl.multiple_of((step * blocks + index) * LANES, LANES), LANES)
+            small_ref[kernel:, place] = jnp.sum(totals[index], axis=0, keepdims=True) / gain_ref[:, lanes]
 
     @pl.when(step == steps)
     def _():
@@ -327,7 +338,6 @@
         fill_padded(pad_ref, glu_ref[...].astype(jnp.float32))
         size = row_chunk(rows)
         for index in range(blocks):
-            lanes = slice(index * LANES, (index + 1) * LANES)
             for base in range(0, rows, size):
                 chunk = slice(base, base + size)
                 d_conv = rstd_ref[chunk, :] * (
@@ -341,7 +351,8 @@
                         part_ref[index, tap] = term
                     else:
                         part_ref[index, tap] += term
-            taps_out_ref[:, lanes] = jnp.sum(part_ref[index], axis=1)
+            place = pl.ds(pl.multiple_of(((step - steps) * blocks + index) * LANES, LANES), LANES)
+            small_ref[:kernel, place] = jnp.sum(part_ref[index], axis=1)
 
 
 def backward(cotangent, second, slope, centered, rstd, gain_mid, glu, kernel):
@@ -364,11 +375,8 @@
             pl.BlockSpec((1, width), early),
             pl.BlockSpec((rows, width), late),
         ],
-        out_specs=[pl.BlockSpec((kernel, width), late), pl.BlockSpec((1, width), early)],
-        out_shape=[
-            jax.ShapeDtypeStruct((kernel, model), jnp.float32),
-            jax.ShapeDtypeStruct((1, model), jnp.float32),
-        ],
+        out_specs=pl.BlockSpec((kernel + 1, model), whole),
+        out_shape=jax.ShapeDtypeStruct((kernel + 1, model), jnp.float32),
         scratch_shapes=[
             pltpu.VMEM((model // LANES, rows, LANES), jnp.float32),
             pltpu.VMEM((2, rows, LANES), jnp.float32),
@@ -385,30 +393,6 @@
     )(cotangent, second, slope, centered, rstd, gain_mid.reshape(1, model), glu)
 
 
-def weight_kernel(mine_ref, theirs_ref, swished_ref, other_ref, out_ref):
-    out_ref[...] = (dot(mine_ref[...], swished_ref[...]) + dot(theirs_ref[...], other_ref[...])).astype(jnp.bfloat16)
-
-
-def weight_gradient(mine, theirs, swished, other):
-    out, rows = mine.shape
-    model = swished.shape[1]
-    width = model // 3
-    whole = pl.BlockSpec((out, rows), lambda step: (0, 0))
-    block = pl.BlockSpec((rows, width), lambda step: (0, step))
-    return pl.pallas_call(
-        weight_kernel,
-        grid=(model // width,),
-        in_specs=[whole, whole, block, block],
-        out_specs=pl.BlockSpec((out, width), lambda step: (0, step)),
-        out_shape=jax.ShapeDtypeStruct((out, model), jnp.bfloat16),
-        compiler_params=pltpu.CompilerParams(vmem_limit_bytes=16 * 2**20),
-        cost_estimate=pl.CostEstimate(
-            flops=4 * rows * out * model, bytes_accessed=2 * out * model, transcendentals=0
-        ),
-        name="weight_gradient",
-    )(mine, theirs, swished, other)
-
-
 def spread(values, axis):
     copies = jnp.broadcast_to(values[None], (lax.axis_size(axis),) + values.shape)
     return lax.all_to_all(copies, axis, 0, 0, tiled=True)
@@ -422,7 +406,7 @@
     return lax.optimization_barrier(values)
 
 
-def scatter_plane(values, owner):
+def scatter_plane(values, owner, beside):
     owners = values.shape[0]
     side = 4 if owners % 4 == 0 else 1
     across, along = lax.rem(owner, side), lax.div(owner, side)
@@ -431,12 +415,13 @@
     for k in range(1, side):
         moves = [(i, i // side * side + (i % side + k) % side) for i in range(owners)]
         total = total + lax.ppermute(at(values, lax.rem(across + k, side), 1), "dp", moves)
-    values, count = total, owners // side
+    count = owners // side
+    values, beside = barrier((total, beside))
     total = at(values, along)
     for k in range(1, count):
         moves = [(i, (i // side + k) % count * side + i % side) for i in range(owners)]
         total = total + lax.ppermute(at(values, lax.rem(along + k, count)), "dp", moves)
-    return total
+    return total, beside
 
 
 def body(fbank, lengths, sources, w_sub, gain_in, w_first, taps, gain_mid, w_second, cotangent):
@@ -467,28 +452,29 @@
     grad_out = cotangent.reshape(rows, model)
     grad_t = grad_out.T.reshape(chips, 2, owners, own, rows)
     of_core = lambda side: jnp.swapaxes(at(grad_t, side, 1), 0, 1).reshape(chips * own_rows, rows)
-    grad_mine, grad_theirs = of_core(core), swap(of_core(1 - core))
-
-    norm_in, x0, select, grad_spaced = front(meta, received, w_sub, gain_in, grad_out, utt, owners)
-    norm_in, grad_mine, grad_theirs = barrier((norm_in, grad_mine, grad_theirs))
-    glu, centered, rstd, swished = forward(norm_in, first_t, taps, gain_mid, select)
-
-    partial = weight_gradient(grad_mine, grad_theirs, swished, swap(swished))
-    centered, partial = barrier((centered, partial))
+    left = jnp.concatenate([of_core(core), swap(of_core(1 - core))], axis=1)
+
+    norm_in, x0, grad_spaced = front(meta, received, w_sub, gain_in, grad_out, utt, owners)
+    norm_in, left = barrier((norm_in, left))
+    glu, conv, mean, rstd, swished = forward(meta, norm_in, first_t, taps, gain_mid, rows, utt, owners)
+
+    partial = dot(left, jnp.concatenate([swished, swap(swished)], axis=0)).astype(jnp.bfloat16)
+    conv, partial = barrier((conv, partial))
     partial = lax.all_to_all(partial.reshape(owners, chips * own, model), "dp", 0, 0, tiled=True)
 
     gains = gain_mid.reshape(-1, 1, LANES)
+    centered = (conv - mean) * rstd
     normed = centered * gains
     sig = sigmoid(normed)
     slope = gains * (sig * (1.0 + normed * (1.0 - sig)))
-    taps_term, gain_term = backward(grad_spaced, second, slope, centered, rstd, gain_mid, glu, kernel)
+    small = backward(grad_spaced, second, slope, centered, rstd, gain_mid, glu, kernel)
     block = (x0.astype(jnp.float32) + dot_t(swished, second)).astype(jnp.bfloat16)
 
-    small = jnp.concatenate([taps_term, gain_term], axis=0)
-    small = scatter_plane(small.reshape(owners, -1, model), owner)
+    small = small + swap(small)
+    small, partial = scatter_plane(small.reshape(owners, -1, model), owner, partial)
     partial = jnp.sum(partial.astype(jnp.float32), axis=0).astype(jnp.bfloat16).reshape(chips, own, model)
 
-    small = (small + swap(small)).astype(jnp.bfloat16)
+    small = small.astype(jnp.bfloat16)
     both = jnp.concatenate([partial, jnp.broadcast_to(small[None], (chips,) + small.shape)], axis=1)
     same_core = [[2 * chip + side for chip in range(chips)] for side in range(2)]
     both = lax.all_to_all(both, "fsdp", 0, 0, tiled=True, axis_index_groups=same_core)

time: 197 us -> 188 us (0.954)
  Pallas kernels: 46.3 us -> 38.6 us
  local copies, waits for them, and re-layouts: 27.3 us -> 23.8 us
  matrix products: 5.37 us -> 8.86 us
  other arithmetic: 7.54 us -> 10.9 us
  waiting for transfers between devices: 46.7 us -> 43.8 us
    pallas_call x2 -> x1, Pallas kernels: 23.7 us -> 16 us  [forward(): pl.pallas_call(lambda *refs: forward_kernel(utt, owners, *refs), grid=(st...]
    ppermute x3, waiting for transfers between devices: 8.38 us -> 2.58 us  [scatter_plane(): lax.ppermute(at(values, lax.rem(across + k, side), 1), 'dp', moves)]
    all_gather x1, waiting for transfers between devices: 2.73 us -> 8.21 us  [body(): second = lax.all_gather(w_second, 'fsdp', axis=0, tiled=True)]
    dot_general x0 -> x1, matrix products: none -> 3.48 us  [dot(): return jnp.dot(left, right, preferred_element_type=jnp.float32)]
    unnamed x34 -> x30, local copies, waits for them, and re-layouts: 8.86 us -> 5.38 us
    all_to_all x1, waiting for transfers between devices: 12.9 us -> 10.6 us  [body(): received = lax.all_to_all(blocks, 'dp', 0, 0, tiled=True)]
  transfers between devices with their start and end apart: 14 -> 14, of which waited for: 10 -> 9; matrix products, arithmetic and copies ran while one was open for 13% -> 19% of each run, Pallas kernels for 24% -> 21%
where the time goes in v3:
time: 188 us; the launch traced here: 187 us
  waiting for transfers between devices  43.8 us (23%)
  Pallas kernels  38.6 us (21%)
  starting transfers between devices  33.3 us (18%)
  local copies, waits for them, and re-layouts  23.8 us (13%)
  between operations  14.3 us (8%)
  blocking collectives  14 us (7%)
  other arithmetic  10.9 us (6%)
  matrix products  8.86 us (5%)
    pallas_call x1, Pallas kernels, forward(): pl.pallas_call(lambda *refs: forward_kernel(utt, owners, *refs), grid=(st...  16 us
    all_gather x1, waiting for transfers between devices, body(): first_t = lax.all_gather(w_first.T, 'fsdp', axis=0, tiled=True)  14.3 us
    all_to_all x1, blocking collectives, body(): lax.all_to_all(both, 'fsdp', 0, 0, tiled=True, axis_index_groups=same_core)  14 us
    pallas_call x1, Pallas kernels, backward(): pl.pallas_call(backward_kernel, grid=(2 * steps,), in_specs=[pl.BlockSpec...  13.5 us
    all_to_all x1, waiting for transfers between devices, body(): received = lax.all_to_all(blocks, 'dp', 0, 0, tiled=True)  10.6 us
    all_gather x1, waiting for transfers between devices, body(): second = lax.all_gather(w_second, 'fsdp', axis=0, tiled=True)  8.21 us
    all_to_all x1, starting transfers between devices, body(): received = lax.all_to_all(blocks, 'dp', 0, 0, tiled=True)  7.61 us
    all_to_all x1, starting transfers between devices, spread(): return lax.all_to_all(copies, axis, 0, 0, tiled=True)  7.36 us
  transfers between devices with their start and end apart: 14, of which 9 were waited for; matrix products, arithmetic and copies ran while one was open for 19% of the time, Pallas kernels for 21%

profile of v3, /device:TPU:2, one launch (start us, length us, event | category | flops | bytes accessed | tf_op | source)
XLA Modules:
  0.0 187.5 jit_solution(9473219411597738989)
XLA Ops:
  10.8 2.4 %send_rows.1 = bf16[16,104,640]{2,1,0:T(8,128)(2,1)} custom-call(s32[98]{0:T(128)S(1)} %pad_add_fusion.refs_0_, bf16[300,640]{1,0:T(8,128)(2,1)S(1)} %bitcast.51), custom_call_target="tpu_custom_call" | custom-call | flops 119808000 | bytes 2097152 | tf_op jit(solution)/shard_map/send_rows/pallas_call | solution.py:101
  13.2 7.6 %all-to-all-start = ((bf16[16,104,640]{2,1,0:T(8,128)(2,1)}), bf16[16,104,640]{2,1,0:T(8,128)(2,1)S(1)}, u32[]{:S(2)}, u32[]{:S(2)}) async-start(bf16[16,104,640]{2,1,0:T(8,128)(2,1)} %send_rows.1), calls=%async_computation | async-start | bytes 4259840 | tf_op jit(solution)/shard_map/all_to_all | solution.py:450
  22.2 3.3 %reshape.64 = bf16[8,2,16,6,384]{4,3,2,1,0:T(8,128)(2,1)} reshape(bf16[1536,384]{1,0:T(8,128)(2,1)} %copy.21) | data formatting | bytes 2359296 | tf_op jit(solution)/shard_map/reshape | solution.py:453
  25.5 2.4 %dynamic-slice_bitcast_fusion.1 = (bf16[16,8,6,384]{3,2,0,1:T(8,128)(2,1)}, bf16[16,8,6,384]{3,2,0,1:T(8,128)(2,1)S(1)}) fusion(bf16[8,2,16,6,384]{4,3,2,1,0:T(8,128)(2,1)} %reshape.64, s32[]{:T(128)S(6)} %select_n.39, s32[]{:T(128)S(6)} %select_n.40), kind=kLoop, calls=%fused_computation.11 | loop fusion | bytes 2359304 | tf_op jit(solution)/shard_map/transpose | solution.py:454
  29.0 2.1 %reshape.66 = bf16[768,384]{1,0:T(8,128)(2,1)} reshape(bf16[16,8,6,384]{3,2,1,0:T(8,128)(2,1)} %copy.25) | data formatting | bytes 1179648 | tf_op jit(solution)/shard_map/reshape | solution.py:454
  31.1 2.1 %copy.23 = bf16[16,8,6,384]{3,2,1,0:T(8,128)(2,1)} copy(bf16[16,8,6,384]{3,2,0,1:T(8,128)(2,1)} %get-tuple-element.34) | data formatting | bytes 1179648 | tf_op jit(solution)/shard_map/transpose | solution.py:454
  35.3 2.4 %pad_maximum_fusion = bf16[768,768]{1,0:T(8,128)(2,1)} fusion(bf16[768,384]{1,0:T(8,128)(2,1)} %collective-permute-done, bf16[768,384]{1,0:T(8,128)(2,1)} %reshape.65), kind=kLoop, calls=%fused_computation.9 | loop fusion | flops 2359296 | bytes 2359296 | tf_op jit(solution)/shard_map/concatenate | solution.py:455
  37.7 10.6 %all-to-all-done.refs_1_ = bf16[16,104,640]{2,1,0:T(8,128)(2,1)S(1)} async-done(((bf16[16,104,640]{2,1,0:T(8,128)(2,1)}), bf16[16,104,640]{2,1,0:T(8,128)(2,1)S(1)}, u32[]{:S(2)}, u32[]{:S(2)}) %all-to-all-start) | async-done | bytes 2129952 | tf_op jit(solution)/shard_map/all_to_all | solution.py:450
  49.5 6.7 %front.1 = (bf16[416,1536]{1,0:T(8,128)(2,1)S(1)}, bf16[384,1536]{1,0:T(8,128)(2,1)S(1)}, bf16[416,1536]{1,0:T(8,128)(2,1)S(1)}) custom-call(s32[98]{0:T(128)S(1)} %pad_add_fusion.refs_0_, bf16[16,104,640]{2,1,0:T(8,128)(2,1)S(1)} %all-to-all-done.refs_1_, bf16[320,1536]{1,0:T(8,128)(2,1)S(1)} %copy-done.8, f32[1,1536]{1,0:T(1,128)S(1)} %reshape.62.refs_3_, ...), custom_call_target="tpu_custom_call" | custom-call | flops 4000000000 | bytes 16777216 | tf_op jit(solution)/shard_map/front/pallas_call | solution.py:166
  59.3 14.3 %all-gather.3.cloned.1.call-done.refs_2_.refs_3_ = bf16[3072,1536]{1,0:T(8,128)(2,1)} async-done(((bf16[192,1536]{1,0:T(8,128)(2,1)}), bf16[3072,1536]{1,0:T(8,128)(2,1)}) %all-gather.3.cloned.1.call-update) | async-done | bytes 9437200 | tf_op jit(solution)/shard_map/all_gather | solution.py:443
  73.7 16.0 %forward.1 = (bf16[416,1536]{1,0:T(8,128)(2,1)S(1)}, f32[12,416,128]{2,1,0:T(8,128)}, f32[416,128]{1,0:T(8,128)S(1)}, f32[416,128]{1,0:T(8,128)S(1)}, bf16[384,1536]{1,0:T(8,128)(2,1)S(1)}) custom-call(s32[98]{0:T(128)S(1)} %pad_add_fusion.refs_0_, bf16[416,1536]{1,0:T(8,128)(2,1)} %copy-done, ...), custom_call_target="tpu_custom_call" | custom-call | flops 4322033664 | bytes 15826944 | tf_op jit(solution)/shard_map/forward/pallas_call | solution.py:244
  90.0 2.6 %collective-permute-done.1 = bf16[384,1536]{1,0:T(8,128)(2,1)S(1)} collective-permute-done((bf16[384,1536]{1,0:T(8,128)(2,1)S(1)}, bf16[384,1536]{1,0:T(8,128)(2,1)S(1)}, u32[]{:S(2)}, u32[]{:S(2)}) %collective-permute-start.1) | collective-permute-done | bytes 1179680 | tf_op jit(solution)/shard_map/ppermute | solution.py:441
  92.6 3.5 %convolution_convert_fusion = bf16[768,1536]{1,0:T(8,128)(2,1)} fusion(bf16[768,768]{1,0:T(8,128)(2,1)S(1)} %copy-done.11, bf16[384,1536]{1,0:T(8,128)(2,1)S(1)} %collective-permute-done.1, bf16[384,1536]{1,0:T(8,128)(2,1)S(1)} %get-tuple-element.21), kind=kOutput, calls=%fused_computation | convolution fusion | flops 1817837568 | bytes 5898240 | tf_op jit(solution)/shard_map/dot_general | solution.py:51
  96.1 7.3 %all-to-all-start.1 = ((bf16[16,48,1536]{2,1,0:T(8,128)(2,1)}), bf16[16,48,1536]{2,1,0:T(8,128)(2,1)}, u32[]{:S(2)}, u32[]{:S(2)}) async-start(bf16[16,48,1536]{2,1,0:T(8,128)(2,1)} %bitcast.52), calls=%async_computation.1 | async-start | bytes 4718592 | tf_op jit(solution)/shard_map/all_to_all | solution.py:463
  103.4 5.2 %multiply_multiply_fusion = (f32[12,416,128]{2,1,0:T(8,128)}, f32[12,416,128]{2,1,0:T(8,128)}) fusion(f32[12,128]{1,0:T(8,128)S(1)} %bitcast.55, f32[416,128]{1,0:T(8,128)S(1)} %get-tuple-element.27.rstd_ref, f32[12,416,128]{2,1,0:T(8,128)} %get-tuple-element.25, f32[416,128]{1,0:T(8,128)S(1)} %get-tuple-element.26), kind=kLoop, calls=%fused_computation.4 | loop fusion | flops 7028736 | bytes 8099840 | tf_op jit(solution)/shard_map/mul | solution.py:469
  108.6 8.2 %all-gather.5.cloned.1.call-done.second_ref = bf16[1536,1536]{1,0:T(8,128)(2,1)} async-done(((bf16[96,1536]{1,0:T(8,128)(2,1)}), bf16[1536,1536]{1,0:T(8,128)(2,1)}) %all-gather.5.cloned.1.call-update) | async-done | bytes 4718608 | tf_op jit(solution)/shard_map/all_gather | solution.py:444
  116.8 13.5 %backward.1 = f32[32,1536]{1,0:T(8,128)} custom-call(bf16[416,1536]{1,0:T(8,128)(2,1)} %copy-done.1, bf16[1536,1536]{1,0:T(8,128)(2,1)} %all-gather.5.cloned.1.call-done.second_ref, f32[12,416,128]{2,1,0:T(8,128)} %get-tuple-element.32.slope_ref, f32[12,416,128]{2,1,0:T(8,128)} %get-tuple-element.33.centered_ref, f32[416,128]{1,0:T(8,128)} %copy-done.4, ...), custom_call_target="tpu_custom_call" | custom-call | flops 2359099392 | bytes 12386304 | tf_op jit(solution)/shard_map/backward/pallas_call | solution.py:366
  137.8 2.5 %collective-permute-done.4 = f32[4,2,1536]{2,1,0:T(2,128)S(1)} collective-permute-done((f32[4,2,1536]{2,1,0:T(2,128)S(1)}, f32[4,2,1536]{2,1,0:T(2,128)S(1)}, u32[]{:S(2)}, u32[]{:S(2)}) %collective-permute-start.4) | collective-permute-done | bytes 49184 | tf_op jit(solution)/shard_map/ppermute | solution.py:417
  142.0 2.7 %collective-permute-start.7 = (f32[2,1536]{1,0:T(2,128)S(1)}, f32[2,1536]{1,0:T(2,128)S(1)}, u32[]{:S(2)}, u32[]{:S(2)}) collective-permute-start(f32[2,1536]{1,0:T(2,128)S(1)} %get-tuple-element.41), channel_id=1, source_target_pairs={{0,128},{16,144},{32,160},{48,176},{64,192},{80,208},{96,224},{112... | collective-permute-start | bytes 36872 | tf_op jit(solution)/shard_map/ppermute | solution.py:423
  146.2 2.1 %reduce_sum.24 = bf16[48,1536]{1,0:T(8,128)(2,1)S(1)} reduce(bf16[16,48,1536]{2,1,0:T(8,128)(2,1)} %all-to-all-done.1, bf16[]{:T(256)} %constant.75.clone.1), dimensions={0}, to_apply=%region_0.1 | reduce | flops 1105920 | bytes 2506754 | tf_op jit(solution)/shard_map/reduce_sum | solution.py:475
  148.6 14.0 %all_to_all.20 = bf16[8,8,1536]{2,1,0:T(8,128)(2,1)S(1)} all-to-all(bf16[8,8,1536]{2,1,0:T(8,128)(2,1)S(1)} %pad_maximum_fusion.1), channel_id=1, replica_groups={{0,2,4,6,8,10,12,14},{1,3,5,7,9,11,13,15},{16,18,20,22,24,26,28,30},{17..., dimensions={0} | all-to-all | bytes 393216 | tf_op jit(solution)/shard_map/all_to_all | solution.py:480
  163.3 7.4 %all-to-all-start.3 = ((bf16[16,8,1536]{2,1,0:T(8,128)(2,1)}), bf16[16,8,1536]{2,1,0:T(8,128)(2,1)S(1)}, u32[]{:S(2)}, u32[]{:S(2)}) async-start(bf16[16,8,1536]{2,1,0:T(8,128)(2,1)} %broadcast_in_dim.5), calls=%async_computation.3 | async-start | bytes 786432 | tf_op jit(solution)/shard_map/all_to_all | solution.py:398
  170.7 5.4 %fusion.1 = bf16[1,1,384,1536]{3,2,1,0:T(8,128)(2,1)} fusion(bf16[384,1536]{1,0:T(8,128)(2,1)S(1)} %get-tuple-element.21, bf16[1536,1536]{1,0:T(8,128)(2,1)} %all-gather.5.cloned.1.call-done.second_ref, bf16[384,1536]{1,0:T(8,128)(2,1)S(1)} %copy-done.10), kind=kOutput, calls=%fused_computation.3 | convolution fusion | flops 1813708800 | bytes 8257536 | tf_op jit(solution)/shard_map/dot_general | solution.py:55
  176.1 2.7 %all-to-all-done.3 = bf16[16,8,1536]{2,1,0:T(8,128)(2,1)S(1)} async-done(((bf16[16,8,1536]{2,1,0:T(8,128)(2,1)}), bf16[16,8,1536]{2,1,0:T(8,128)(2,1)S(1)}, u32[]{:S(2)}, u32[]{:S(2)}) %all-to-all-start.3) | async-done | bytes 393248 | tf_op jit(solution)/shard_map/all_to_all | solution.py:398
  (77 shorter events, 26.3 us)
Async XLA Ops:
  7.2 66.5 %all-gather.3.cloned.1.call-start = ((), (), s32[]{:S(2)}) async-start(), calls=%async_computation.4 | async-start | bytes 10027008 | tf_op jit(solution)/shard_map/all_gather | solution.py:443
  7.9 108.9 %all-gather.5.cloned.1.call-start = ((), (), s32[]{:S(2)}) async-start(), calls=%async_computation.5 | async-start | bytes 5013504 | tf_op jit(solution)/shard_map/all_gather | solution.py:444
  13.2 7.6 %copy-start.3 = (bf16[1,1,384,1536]{3,2,1,0:T(8,128)(2,1)S(1)}, bf16[1,1,384,1536]{3,2,1,0:T(8,128)(2,1)}, u32[]{:S(2)}) copy-start(bf16[1,1,384,1536]{3,2,1,0:T(8,128)(2,1)} %param.19) | copy-start | bytes 3538948
  13.2 35.1 %all-to-all-start = ((bf16[16,104,640]{2,1,0:T(8,128)(2,1)}), bf16[16,104,640]{2,1,0:T(8,128)(2,1)S(1)}, u32[]{:S(2)}, u32[]{:S(2)}) async-start(bf16[16,104,640]{2,1,0:T(8,128)(2,1)} %send_rows.1), calls=%async_computation | async-start | bytes 4259840 | tf_op jit(solution)/shard_map/all_to_all | solution.py:450
  29.0 6.3 %copy-start.14 = (f32[1536]{0:T(1024)S(1)}, f32[1536]{0:T(1024)}, u32[]{:S(2)}) copy-start(f32[1536]{0:T(1024)} %param.14) | copy-start | bytes 18436
  29.0 6.3 %copy-start.13 = (f32[1536]{0:T(1024)S(1)}, f32[1536]{0:T(1024)}, u32[]{:S(2)}) copy-start(f32[1536]{0:T(1024)} %param.17) | copy-start | bytes 18436
  31.1 4.3 %collective-permute-start = (bf16[768,384]{1,0:T(8,128)(2,1)}, bf16[768,384]{1,0:T(8,128)(2,1)}, u32[]{:S(2)}, u32[]{:S(2)}) collective-permute-start(bf16[768,384]{1,0:T(8,128)(2,1)} %reshape.66), channel_id=1, source_target_pairs={{0,1},{1,0},{2,3},{3,2},{4,5},{5,4},{6,7},{7,6},{8,9},{9,8},{10,11... | collective-permute-start | bytes 1769480 | tf_op jit(solution)/shard_map/ppermute | solution.py:441
  35.3 38.3 %copy-start.7 = (f32[1,1536]{1,0:T(1,128)}, f32[1,1536]{1,0:T(1,128)S(1)}, u32[]{:S(2)}) copy-start(f32[1,1536]{1,0:T(1,128)S(1)} %reshape.67.refs_5_.gain_ref) | copy-start | bytes 18436
  48.3 1.2 copy-start.8
  49.5 24.2 %copy-start.6 = (f32[31,1536]{1,0:T(8,128)S(1)}, f32[31,1536]{1,0:T(8,128)}, u32[]{:S(2)}) copy-start(f32[31,1536]{1,0:T(8,128)} %refs_4_.1) | copy-start | bytes 571396
  73.7 18.9 %copy-start.11 = (bf16[768,768]{1,0:T(8,128)(2,1)S(1)}, bf16[768,768]{1,0:T(8,128)(2,1)}, u32[]{:S(2)}) copy-start(bf16[768,768]{1,0:T(8,128)(2,1)} %pad_maximum_fusion) | copy-start | bytes 3538948
  89.7 6.4 %copy-start.2 = (bf16[416,1536]{1,0:T(8,128)(2,1)}, bf16[416,1536]{1,0:T(8,128)(2,1)S(1)}, u32[]{:S(2)}) copy-start(bf16[416,1536]{1,0:T(8,128)(2,1)S(1)} %get-tuple-element.28.glu_ref) | copy-start | bytes 3833860
  89.7 13.7 %copy-start.4 = (f32[416,128]{1,0:T(8,128)}, f32[416,128]{1,0:T(8,128)S(1)}, u32[]{:S(2)}) copy-start(f32[416,128]{1,0:T(8,128)S(1)} %get-tuple-element.27.rstd_ref) | copy-start | bytes 638980
  89.7 2.9 %collective-permute-start.1 = (bf16[384,1536]{1,0:T(8,128)(2,1)S(1)}, bf16[384,1536]{1,0:T(8,128)(2,1)S(1)}, u32[]{:S(2)}, u32[]{:S(2)}) collective-permute-start(bf16[384,1536]{1,0:T(8,128)(2,1)S(1)} %get-tuple-element.21), channel_id=1, source_target_pairs={{0,1},{1,0},{2,3},{3,2},{4,5},{5,4},{6,7},{7,6},{8,9},{9,8},{10,11... | collective-permute-start | bytes 3538952 | tf_op jit(solution)/shard_map/ppermute | solution.py:441
  96.1 44.4 %all-to-all-start.1 = ((bf16[16,48,1536]{2,1,0:T(8,128)(2,1)}), bf16[16,48,1536]{2,1,0:T(8,128)(2,1)}, u32[]{:S(2)}, u32[]{:S(2)}) async-start(bf16[16,48,1536]{2,1,0:T(8,128)(2,1)} %bitcast.52), calls=%async_computation.1 | async-start | bytes 4718592 | tf_op jit(solution)/shard_map/all_to_all | solution.py:463
  130.3 1.7 collective-permute-start.2
  133.1 4.8 %collective-permute-start.3 = (f32[4,2,1536]{2,1,0:T(2,128)S(1)}, f32[4,2,1536]{2,1,0:T(2,128)S(1)}, u32[]{:S(2)}, u32[]{:S(2)}) collective-permute-start(f32[4,2,1536]{2,1,0:T(2,128)S(1)} %get-tuple-element.36), channel_id=1, source_target_pairs={{0,16},{16,32},{32,48},{48,0},{64,80},{80,96},{96,112},{112,64},{1... | collective-permute-start | bytes 147464 | tf_op jit(solution)/shard_map/ppermute | solution.py:417
  134.6 5.8 %collective-permute-start.4 = (f32[4,2,1536]{2,1,0:T(2,128)S(1)}, f32[4,2,1536]{2,1,0:T(2,128)S(1)}, u32[]{:S(2)}, u32[]{:S(2)}) collective-permute-start(f32[4,2,1536]{2,1,0:T(2,128)S(1)} %get-tuple-element.38), channel_id=1, source_target_pairs={{0,32},{16,48},{32,0},{48,16},{64,96},{80,112},{96,64},{112,80},{1... | collective-permute-start | bytes 147464 | tf_op jit(solution)/shard_map/ppermute | solution.py:417
  135.8 4.6 %collective-permute-start.5 = (f32[4,2,1536]{2,1,0:T(2,128)S(1)}, f32[4,2,1536]{2,1,0:T(2,128)S(1)}, u32[]{:S(2)}, u32[]{:S(2)}) collective-permute-start(f32[4,2,1536]{2,1,0:T(2,128)S(1)} %get-tuple-element.37), channel_id=1, source_target_pairs={{0,48},{16,0},{32,16},{48,32},{64,112},{80,64},{96,80},{112,96},{1... | collective-permute-start | bytes 147464 | tf_op jit(solution)/shard_map/ppermute | solution.py:417
  140.5 7.9 %collective-permute-start.6 = (f32[2,1536]{1,0:T(2,128)S(1)}, f32[2,1536]{1,0:T(2,128)S(1)}, u32[]{:S(2)}, u32[]{:S(2)}) collective-permute-start(f32[2,1536]{1,0:T(2,128)S(1)} %get-tuple-element.39), channel_id=1, source_target_pairs={{0,64},{16,80},{32,96},{48,112},{64,128},{80,144},{96,160},{112,17... | collective-permute-start | bytes 36872 | tf_op jit(solution)/shard_map/ppermute | solution.py:423
  142.0 6.3 %collective-permute-start.7 = (f32[2,1536]{1,0:T(2,128)S(1)}, f32[2,1536]{1,0:T(2,128)S(1)}, u32[]{:S(2)}, u32[]{:S(2)}) collective-permute-start(f32[2,1536]{1,0:T(2,128)S(1)} %get-tuple-element.41), channel_id=1, source_target_pairs={{0,128},{16,144},{32,160},{48,176},{64,192},{80,208},{96,224},{112... | collective-permute-start | bytes 36872 | tf_op jit(solution)/shard_map/ppermute | solution.py:423
  144.7 3.7 %collective-permute-start.8 = (f32[2,1536]{1,0:T(2,128)S(1)}, f32[2,1536]{1,0:T(2,128)S(1)}, u32[]{:S(2)}, u32[]{:S(2)}) collective-permute-start(f32[2,1536]{1,0:T(2,128)S(1)} %get-tuple-element.40), channel_id=1, source_target_pairs={{0,192},{16,208},{32,224},{48,240},{64,0},{80,16},{96,32},{112,48}... | collective-permute-start | bytes 36872 | tf_op jit(solution)/shard_map/ppermute | solution.py:423
  146.2 24.5 %copy-start.10 = (bf16[384,1536]{1,0:T(8,128)(2,1)S(1)}, bf16[384,1536]{1,0:T(8,128)(2,1)}, u32[]{:S(2)}) copy-start(bf16[384,1536]{1,0:T(8,128)(2,1)} %copy-done.9) | copy-start | bytes 3538948
  163.3 15.4 %all-to-all-start.3 = ((bf16[16,8,1536]{2,1,0:T(8,128)(2,1)}), bf16[16,8,1536]{2,1,0:T(8,128)(2,1)S(1)}, u32[]{:S(2)}, u32[]{:S(2)}) async-start(bf16[16,8,1536]{2,1,0:T(8,128)(2,1)} %broadcast_in_dim.5), calls=%async_computation.3 | async-start | bytes 786432 | tf_op jit(solution)/shard_map/all_to_all | solution.py:398
  (5 other events, 4.8 us)
Sparse Core Ops, SparseCore 0:
  9.8 63.7 all-gather.2
  75.5 41.2 all-gather.4

commit v4 on v3

--- a/solution.py
+++ b/solution.py
@@ -393,6 +393,56 @@
     )(cotangent, second, slope, centered, rstd, gain_mid.reshape(1, model), glu)
 
 
+def total_kernel(pieces_ref, out_ref):
+    total = pieces_ref[0].astype(jnp.float32)
+    for index in range(1, pieces_ref.shape[0]):
+        total = total + pieces_ref[index].astype(jnp.float32)
+    out_ref[...] = total.astype(jnp.bfloat16)
+
+
+def total_of(pieces):
+    count, rows, model = pieces.shape
+    width = model // 3
+    return pl.pallas_call(
+        total_kernel,
+        grid=(3,),
+        in_specs=[pl.BlockSpec((count, rows, width), lambda step: (0, 0, step))],
+        out_specs=pl.BlockSpec((rows, width), lambda step: (0, step)),
+        out_shape=jax.ShapeDtypeStruct((rows, model), jnp.bfloat16),
+        compiler_params=pltpu.CompilerParams(vmem_limit_bytes=12 * 2**20),
+        cost_estimate=pl.CostEstimate(flops=count * rows * model, bytes_accessed=2 * count * rows * model, transcendentals=0),
+        name="total",
+    )(pieces)
+
+
+def outputs_kernel(own, both_ref, large_ref, taps_ref, gain_ref):
+    owners, both_rows, model = both_ref.shape
+    kernel = taps_ref.shape[0]
+    share = both_rows - own
+    for owner in range(owners):
+        block = both_ref[owner].astype(jnp.float32)
+        large_ref[owner * own : (owner + 1) * own, :] = block[:own]
+        for index in range(share):
+            row = owner * share + index
+            if row < kernel:
+                taps_ref[row : row + 1, :] = block[own + index : own + index + 1]
+            else:
+                gain_ref[...] = block[own + index : own + index + 1]
+
+
+def outputs(both, own, kernel):
+    owners, _, model = both.shape
+    f32 = lambda *shape: jax.ShapeDtypeStruct(shape, jnp.float32)
+    return pl.pallas_call(
+        lambda *refs: outputs_kernel(own, *refs),
+        in_specs=vmem(1),
+        out_specs=vmem(3),
+        out_shape=[f32(owners * own, model), f32(kernel, model), f32(1, model)],
+        compiler_params=pltpu.CompilerParams(vmem_limit_bytes=12 * 2**20),
+        name="outputs",
+    )(both)
+
+
 def spread(values, axis):
     copies = jnp.broadcast_to(values[None], (lax.axis_size(axis),) + values.shape)
     return lax.all_to_all(copies, axis, 0, 0, tiled=True)
@@ -472,17 +522,15 @@
 
     small = small + swap(small)
     small, partial = scatter_plane(small.reshape(owners, -1, model), owner, partial)
-    partial = jnp.sum(partial.astype(jnp.float32), axis=0).astype(jnp.bfloat16).reshape(chips, own, model)
+    partial = total_of(partial).reshape(chips, own, model)
 
     small = small.astype(jnp.bfloat16)
     both = jnp.concatenate([partial, jnp.broadcast_to(small[None], (chips,) + small.shape)], axis=1)
     same_core = [[2 * chip + side for chip in range(chips)] for side in range(2)]
     both = lax.all_to_all(both, "fsdp", 0, 0, tiled=True, axis_index_groups=same_core)
     both = jnp.sum(both.astype(jnp.float32), axis=0).astype(jnp.bfloat16)
-    both = spread(both, "dp").astype(jnp.float32)
-    grad_second = both[:, :own].reshape(own_rows, model)
-    small = both[:, own:].reshape(kernel + 1, model)
-    return (block.reshape(1, 1, rows, model), grad_second, small[:kernel], small[kernel])
+    grad_second, grad_taps, grad_gain = outputs(spread(both, "dp"), own, kernel)
+    return (block.reshape(1, 1, rows, model), grad_second, grad_taps, grad_gain.reshape(model))
 
 
 def solution(mesh):

time: 188 us -> 188 us (level)
  local copies, waits for them, and re-layouts: 23.8 us -> 21.9 us
    reduce_sum x1 -> x0, other arithmetic: 2.1 us -> none  [body(): jnp.sum(partial.astype(jnp.float32), axis=0).astype(jnp.bfloat16)]
  transfers between devices with their start and end apart: 14 -> 14, of which waited for: 9 -> 9; matrix products, arithmetic and copies ran while one was open for 19% -> 18% of each run, Pallas kernels for 21% -> 21%
where the time goes in v4:
time: 188 us; the launch traced here: 187 us
  waiting for transfers between devices  45.3 us (24%)
  Pallas kernels  40 us (21%)
  starting transfers between devices  33.6 us (18%)
  local copies, waits for them, and re-layouts  21.9 us (12%)
  between operations  14.2 us (8%)
  blocking collectives  13.9 us (7%)
  other arithmetic  9.31 us (5%)
  matrix products  9.12 us (5%)
    pallas_call x1, Pallas kernels, forward(): pl.pallas_call(lambda *refs: forward_kernel(utt, owners, *refs), grid=(st...  15.9 us
    all_gather x1, waiting for transfers between devices, body(): first_t = lax.all_gather(w_first.T, 'fsdp', axis=0, tiled=True)  14.3 us
    all_to_all x1, blocking collectives, body(): lax.all_to_all(both, 'fsdp', 0, 0, tiled=True, axis_index_groups=same_core)  13.9 us
    pallas_call x1, Pallas kernels, backward(): pl.pallas_call(backward_kernel, grid=(2 * steps,), in_specs=[pl.BlockSpec...  13.5 us
    all_to_all x1, waiting for transfers between devices, body(): received = lax.all_to_all(blocks, 'dp', 0, 0, tiled=True)  10.6 us
    all_gather x1, waiting for transfers between devices, body(): second = lax.all_gather(w_second, 'fsdp', axis=0, tiled=True)  8.5 us
    all_to_all x1, starting transfers between devices, body(): received = lax.all_to_all(blocks, 'dp', 0, 0, tiled=True)  7.61 us
    all_to_all x1, starting transfers between devices, spread(): return lax.all_to_all(copies, axis, 0, 0, tiled=True)  7.6 us
  transfers between devices with their start and end apart: 14, of which 9 were waited for; matrix products, arithmetic and copies ran while one was open for 18% of the time, Pallas kernels for 21%

profile of v4, /device:TPU:2, one launch (start us, length us, event | category | flops | bytes accessed | tf_op | source)
XLA Modules:
  0.0 187.4 jit_solution(4959748451878709716)
XLA Ops:
  10.8 2.4 %send_rows.1 = bf16[16,104,640]{2,1,0:T(8,128)(2,1)} custom-call(s32[98]{0:T(128)S(1)} %pad_add_fusion.refs_0_, bf16[300,640]{1,0:T(8,128)(2,1)S(1)} %bitcast.50), custom_call_target="tpu_custom_call" | custom-call | flops 119808000 | bytes 2097152 | tf_op jit(solution)/shard_map/send_rows/pallas_call | solution.py:101
  13.2 7.6 %all-to-all-start = ((bf16[16,104,640]{2,1,0:T(8,128)(2,1)}), bf16[16,104,640]{2,1,0:T(8,128)(2,1)S(1)}, u32[]{:S(2)}, u32[]{:S(2)}) async-start(bf16[16,104,640]{2,1,0:T(8,128)(2,1)} %send_rows.1), calls=%async_computation | async-start | bytes 4259840 | tf_op jit(solution)/shard_map/all_to_all | solution.py:500
  22.2 3.3 %reshape.61 = bf16[8,2,16,6,384]{4,3,2,1,0:T(8,128)(2,1)} reshape(bf16[1536,384]{1,0:T(8,128)(2,1)} %copy.21) | data formatting | bytes 2359296 | tf_op jit(solution)/shard_map/reshape | solution.py:503
  25.5 2.4 %dynamic-slice_bitcast_fusion.1 = (bf16[16,8,6,384]{3,2,0,1:T(8,128)(2,1)}, bf16[16,8,6,384]{3,2,0,1:T(8,128)(2,1)S(1)}) fusion(bf16[8,2,16,6,384]{4,3,2,1,0:T(8,128)(2,1)} %reshape.61, s32[]{:T(128)S(6)} %select_n.39, s32[]{:T(128)S(6)} %select_n.40), kind=kLoop, calls=%fused_computation.11 | loop fusion | bytes 2359304 | tf_op jit(solution)/shard_map/transpose | solution.py:504
  31.0 2.1 %copy.23 = bf16[16,8,6,384]{3,2,1,0:T(8,128)(2,1)} copy(bf16[16,8,6,384]{3,2,0,1:T(8,128)(2,1)} %get-tuple-element.40) | data formatting | bytes 1179648 | tf_op jit(solution)/shard_map/transpose | solution.py:504
  33.2 2.1 %reshape.62 = bf16[768,384]{1,0:T(8,128)(2,1)} reshape(bf16[16,8,6,384]{3,2,1,0:T(8,128)(2,1)} %copy.23) | data formatting | bytes 1179648 | tf_op jit(solution)/shard_map/reshape | solution.py:504
  35.3 2.4 %pad_maximum_fusion = bf16[768,768]{1,0:T(8,128)(2,1)} fusion(bf16[768,384]{1,0:T(8,128)(2,1)} %collective-permute-done, bf16[768,384]{1,0:T(8,128)(2,1)} %reshape.62), kind=kLoop, calls=%fused_computation.9 | loop fusion | flops 2359296 | bytes 2359296 | tf_op jit(solution)/shard_map/concatenate | solution.py:505
  37.7 10.6 %all-to-all-done.refs_1_ = bf16[16,104,640]{2,1,0:T(8,128)(2,1)S(1)} async-done(((bf16[16,104,640]{2,1,0:T(8,128)(2,1)}), bf16[16,104,640]{2,1,0:T(8,128)(2,1)S(1)}, u32[]{:S(2)}, u32[]{:S(2)}) %all-to-all-start) | async-done | bytes 2129952 | tf_op jit(solution)/shard_map/all_to_all | solution.py:500
  49.5 6.7 %front.1 = (bf16[416,1536]{1,0:T(8,128)(2,1)S(1)}, bf16[384,1536]{1,0:T(8,128)(2,1)S(1)}, bf16[416,1536]{1,0:T(8,128)(2,1)S(1)}) custom-call(s32[98]{0:T(128)S(1)} %pad_add_fusion.refs_0_, bf16[16,104,640]{2,1,0:T(8,128)(2,1)S(1)} %all-to-all-done.refs_1_, bf16[320,1536]{1,0:T(8,128)(2,1)S(1)} %copy-done.10, f32[1,1536]{1,0:T(1,128)S(1)} %reshape.59.refs_3_, ...), custom_call_target="tpu_custom_call" | custom-call | flops 4000000000 | bytes 16777216 | tf_op jit(solution)/shard_map/front/pallas_call | solution.py:166
  59.3 14.3 %all-gather.3.cloned.1.call-done.refs_2_.refs_3_ = bf16[3072,1536]{1,0:T(8,128)(2,1)} async-done(((bf16[192,1536]{1,0:T(8,128)(2,1)}), bf16[3072,1536]{1,0:T(8,128)(2,1)}) %all-gather.3.cloned.1.call-update) | async-done | bytes 9437200 | tf_op jit(solution)/shard_map/all_gather | solution.py:493
  73.7 15.9 %forward.1 = (bf16[416,1536]{1,0:T(8,128)(2,1)S(1)}, f32[12,416,128]{2,1,0:T(8,128)}, f32[416,128]{1,0:T(8,128)S(1)}, f32[416,128]{1,0:T(8,128)S(1)}, bf16[384,1536]{1,0:T(8,128)(2,1)S(1)}) custom-call(s32[98]{0:T(128)S(1)} %pad_add_fusion.refs_0_, bf16[416,1536]{1,0:T(8,128)(2,1)} %copy-done, ...), custom_call_target="tpu_custom_call" | custom-call | flops 4322033664 | bytes 15826944 | tf_op jit(solution)/shard_map/forward/pallas_call | solution.py:244
  89.9 2.6 %collective-permute-done.1 = bf16[384,1536]{1,0:T(8,128)(2,1)S(1)} collective-permute-done((bf16[384,1536]{1,0:T(8,128)(2,1)S(1)}, bf16[384,1536]{1,0:T(8,128)(2,1)S(1)}, u32[]{:S(2)}, u32[]{:S(2)}) %collective-permute-start.1) | collective-permute-done | bytes 1179680 | tf_op jit(solution)/shard_map/ppermute | solution.py:491
  92.5 3.4 %convolution_convert_fusion = bf16[768,1536]{1,0:T(8,128)(2,1)} fusion(bf16[768,768]{1,0:T(8,128)(2,1)S(1)} %copy-done.12, bf16[384,1536]{1,0:T(8,128)(2,1)S(1)} %collective-permute-done.1, bf16[384,1536]{1,0:T(8,128)(2,1)S(1)} %get-tuple-element.24), kind=kOutput, calls=%fused_computation | convolution fusion | flops 1817837568 | bytes 5898240 | tf_op jit(solution)/shard_map/dot_general | solution.py:51
  95.9 7.3 %all-to-all-start.1 = ((bf16[16,48,1536]{2,1,0:T(8,128)(2,1)}), bf16[16,48,1536]{2,1,0:T(8,128)(2,1)S(1)}, u32[]{:S(2)}, u32[]{:S(2)}) async-start(bf16[16,48,1536]{2,1,0:T(8,128)(2,1)} %bitcast.51), calls=%async_computation.1 | async-start | bytes 4718592 | tf_op jit(solution)/shard_map/all_to_all | solution.py:513
  103.2 5.1 %multiply_multiply_fusion = (f32[12,416,128]{2,1,0:T(8,128)}, f32[12,416,128]{2,1,0:T(8,128)}) fusion(f32[12,128]{1,0:T(8,128)S(1)} %bitcast.53, f32[416,128]{1,0:T(8,128)S(1)} %get-tuple-element.30.rstd_ref, f32[12,416,128]{2,1,0:T(8,128)} %get-tuple-element.28, f32[416,128]{1,0:T(8,128)S(1)} %get-tuple-element.29), kind=kLoop, calls=%fused_computation.4 | loop fusion | flops 7028736 | bytes 8099840 | tf_op jit(solution)/shard_map/mul | solution.py:519
  108.3 8.5 %all-gather.5.cloned.1.call-done.second_ref = bf16[1536,1536]{1,0:T(8,128)(2,1)} async-done(((bf16[96,1536]{1,0:T(8,128)(2,1)}), bf16[1536,1536]{1,0:T(8,128)(2,1)}) %all-gather.5.cloned.1.call-update) | async-done | bytes 4718608 | tf_op jit(solution)/shard_map/all_gather | solution.py:494
  116.8 13.5 %backward.1 = f32[32,1536]{1,0:T(8,128)} custom-call(bf16[416,1536]{1,0:T(8,128)(2,1)} %copy-done.1, bf16[1536,1536]{1,0:T(8,128)(2,1)} %all-gather.5.cloned.1.call-done.second_ref, f32[12,416,128]{2,1,0:T(8,128)} %get-tuple-element.38.slope_ref, f32[12,416,128]{2,1,0:T(8,128)} %get-tuple-element.39.centered_ref, f32[416,128]{1,0:T(8,128)} %copy-done.4, ...), custom_call_target="tpu_custom_call" | custom-call | flops 2359099392 | bytes 12386304 | tf_op jit(solution)/shard_map/backward/pallas_call | solution.py:366
  135.8 2.1 %collective-permute-start.5 = (f32[4,2,1536]{2,1,0:T(2,128)S(1)}, f32[4,2,1536]{2,1,0:T(2,128)S(1)}, u32[]{:S(2)}, u32[]{:S(2)}) collective-permute-start(f32[4,2,1536]{2,1,0:T(2,128)S(1)} %get-tuple-element.43), channel_id=1, source_target_pairs={{0,48},{16,0},{32,16},{48,32},{64,112},{80,64},{96,80},{112,96},{1... | collective-permute-start | bytes 147464 | tf_op jit(solution)/shard_map/ppermute | solution.py:467
  137.8 2.5 %collective-permute-done.4 = f32[4,2,1536]{2,1,0:T(2,128)S(1)} collective-permute-done((f32[4,2,1536]{2,1,0:T(2,128)S(1)}, f32[4,2,1536]{2,1,0:T(2,128)S(1)}, u32[]{:S(2)}, u32[]{:S(2)}) %collective-permute-start.4) | collective-permute-done | bytes 49184 | tf_op jit(solution)/shard_map/ppermute | solution.py:467
  142.0 2.7 %collective-permute-start.7 = (f32[2,1536]{1,0:T(2,128)S(1)}, f32[2,1536]{1,0:T(2,128)S(1)}, u32[]{:S(2)}, u32[]{:S(2)}) collective-permute-start(f32[2,1536]{1,0:T(2,128)S(1)} %get-tuple-element.47), channel_id=1, source_target_pairs={{0,128},{16,144},{32,160},{48,176},{64,192},{80,208},{96,224},{112... | collective-permute-start | bytes 36872 | tf_op jit(solution)/shard_map/ppermute | solution.py:473
  148.6 13.9 %all_to_all.20 = bf16[8,8,1536]{2,1,0:T(8,128)(2,1)S(1)} all-to-all(bf16[8,8,1536]{2,1,0:T(8,128)(2,1)S(1)} %pad_maximum_fusion.1), channel_id=1, replica_groups={{0,2,4,6,8,10,12,14},{1,3,5,7,9,11,13,15},{16,18,20,22,24,26,28,30},{17..., dimensions={0} | all-to-all | bytes 393216 | tf_op jit(solution)/shard_map/all_to_all | solution.py:530
  163.3 7.6 %all-to-all-start.3 = ((bf16[16,8,1536]{2,1,0:T(8,128)(2,1)}), bf16[16,8,1536]{2,1,0:T(8,128)(2,1)S(1)}, u32[]{:S(2)}, u32[]{:S(2)}) async-start(bf16[16,8,1536]{2,1,0:T(8,128)(2,1)} %broadcast_in_dim.5), calls=%async_computation.3 | async-start | bytes 786432 | tf_op jit(solution)/shard_map/all_to_all | solution.py:448
  170.9 5.7 %fusion.1 = bf16[1,1,384,1536]{3,2,1,0:T(8,128)(2,1)} fusion(bf16[384,1536]{1,0:T(8,128)(2,1)S(1)} %copy-done.9, bf16[1536,1536]{1,0:T(8,128)(2,1)} %all-gather.5.cloned.1.call-done.second_ref, bf16[384,1536]{1,0:T(8,128)(2,1)} %copy-done.11), kind=kOutput, calls=%fused_computation.3 | convolution fusion | flops 1813708800 | bytes 8257536 | tf_op jit(solution)/shard_map/dot_general | solution.py:55
  176.7 2.3 %all-to-all-done.3.refs_0_ = bf16[16,8,1536]{2,1,0:T(8,128)(2,1)S(1)} async-done(((bf16[16,8,1536]{2,1,0:T(8,128)(2,1)}), bf16[16,8,1536]{2,1,0:T(8,128)(2,1)S(1)}, u32[]{:S(2)}, u32[]{:S(2)}) %all-to-all-start.3) | async-done | bytes 393248 | tf_op jit(solution)/shard_map/all_to_all | solution.py:448
  (74 shorter events, 26.1 us)
Async XLA Ops:
  7.2 66.5 %all-gather.3.cloned.1.call-start = ((), (), s32[]{:S(2)}) async-start(), calls=%async_computation.4 | async-start | bytes 10027008 | tf_op jit(solution)/shard_map/all_gather | solution.py:493
  7.9 108.9 %all-gather.5.cloned.1.call-start = ((), (), s32[]{:S(2)}) async-start(), calls=%async_computation.5 | async-start | bytes 5013504 | tf_op jit(solution)/shard_map/all_gather | solution.py:494
  13.2 7.6 %copy-start.3 = (bf16[1,1,384,1536]{3,2,1,0:T(8,128)(2,1)S(1)}, bf16[1,1,384,1536]{3,2,1,0:T(8,128)(2,1)}, u32[]{:S(2)}) copy-start(bf16[1,1,384,1536]{3,2,1,0:T(8,128)(2,1)} %param.19) | copy-start | bytes 3538948
  13.2 35.1 %all-to-all-start = ((bf16[16,104,640]{2,1,0:T(8,128)(2,1)}), bf16[16,104,640]{2,1,0:T(8,128)(2,1)S(1)}, u32[]{:S(2)}, u32[]{:S(2)}) async-start(bf16[16,104,640]{2,1,0:T(8,128)(2,1)} %send_rows.1), calls=%async_computation | async-start | bytes 4259840 | tf_op jit(solution)/shard_map/all_to_all | solution.py:500
  29.0 6.3 %copy-start.14 = (f32[1536]{0:T(1024)S(1)}, f32[1536]{0:T(1024)}, u32[]{:S(2)}) copy-start(f32[1536]{0:T(1024)} %param.14) | copy-start | bytes 18436
  29.0 6.3 %copy-start.13 = (f32[1536]{0:T(1024)S(1)}, f32[1536]{0:T(1024)}, u32[]{:S(2)}) copy-start(f32[1536]{0:T(1024)} %param.17) | copy-start | bytes 18436
  31.0 4.3 %collective-permute-start = (bf16[768,384]{1,0:T(8,128)(2,1)}, bf16[768,384]{1,0:T(8,128)(2,1)}, u32[]{:S(2)}, u32[]{:S(2)}) collective-permute-start(bf16[768,384]{1,0:T(8,128)(2,1)} %reshape.63), channel_id=1, source_target_pairs={{0,1},{1,0},{2,3},{3,2},{4,5},{5,4},{6,7},{7,6},{8,9},{9,8},{10,11... | collective-permute-start | bytes 1769480 | tf_op jit(solution)/shard_map/ppermute | solution.py:491
  35.3 38.4 %copy-start.7 = (f32[1,1536]{1,0:T(1,128)}, f32[1,1536]{1,0:T(1,128)S(1)}, u32[]{:S(2)}) copy-start(f32[1,1536]{1,0:T(1,128)S(1)} %reshape.64.refs_5_.gain_ref) | copy-start | bytes 18436
  49.5 24.2 %copy-start.6 = (f32[31,1536]{1,0:T(8,128)S(1)}, f32[31,1536]{1,0:T(8,128)}, u32[]{:S(2)}) copy-start(f32[31,1536]{1,0:T(8,128)} %refs_4_.1) | copy-start | bytes 571396
  73.7 18.9 %copy-start.12 = (bf16[768,768]{1,0:T(8,128)(2,1)S(1)}, bf16[768,768]{1,0:T(8,128)(2,1)}, u32[]{:S(2)}) copy-start(bf16[768,768]{1,0:T(8,128)(2,1)} %pad_maximum_fusion) | copy-start | bytes 3538948
  89.6 6.3 %copy-start.2 = (bf16[416,1536]{1,0:T(8,128)(2,1)}, bf16[416,1536]{1,0:T(8,128)(2,1)S(1)}, u32[]{:S(2)}) copy-start(bf16[416,1536]{1,0:T(8,128)(2,1)S(1)} %get-tuple-element.31.glu_ref) | copy-start | bytes 3833860
  89.6 6.3 %copy-start.8 = (bf16[384,1536]{1,0:T(8,128)(2,1)}, bf16[384,1536]{1,0:T(8,128)(2,1)S(1)}, u32[]{:S(2)}) copy-start(bf16[384,1536]{1,0:T(8,128)(2,1)S(1)} %get-tuple-element.24) | copy-start | bytes 3538948
  89.6 13.6 %copy-start.4 = (f32[416,128]{1,0:T(8,128)}, f32[416,128]{1,0:T(8,128)S(1)}, u32[]{:S(2)}) copy-start(f32[416,128]{1,0:T(8,128)S(1)} %get-tuple-element.30.rstd_ref) | copy-start | bytes 638980
  89.6 2.9 %collective-permute-start.1 = (bf16[384,1536]{1,0:T(8,128)(2,1)S(1)}, bf16[384,1536]{1,0:T(8,128)(2,1)S(1)}, u32[]{:S(2)}, u32[]{:S(2)}) collective-permute-start(bf16[384,1536]{1,0:T(8,128)(2,1)S(1)} %get-tuple-element.24), channel_id=1, source_target_pairs={{0,1},{1,0},{2,3},{3,2},{4,5},{5,4},{6,7},{7,6},{8,9},{9,8},{10,11... | collective-permute-start | bytes 3538952 | tf_op jit(solution)/shard_map/ppermute | solution.py:491
  95.9 44.5 %all-to-all-start.1 = ((bf16[16,48,1536]{2,1,0:T(8,128)(2,1)}), bf16[16,48,1536]{2,1,0:T(8,128)(2,1)S(1)}, u32[]{:S(2)}, u32[]{:S(2)}) async-start(bf16[16,48,1536]{2,1,0:T(8,128)(2,1)} %bitcast.51), calls=%async_computation.1 | async-start | bytes 4718592 | tf_op jit(solution)/shard_map/all_to_all | solution.py:513
  130.3 1.7 collective-permute-start.2
  133.1 4.8 %collective-permute-start.3 = (f32[4,2,1536]{2,1,0:T(2,128)S(1)}, f32[4,2,1536]{2,1,0:T(2,128)S(1)}, u32[]{:S(2)}, u32[]{:S(2)}) collective-permute-start(f32[4,2,1536]{2,1,0:T(2,128)S(1)} %get-tuple-element.42), channel_id=1, source_target_pairs={{0,16},{16,32},{32,48},{48,0},{64,80},{80,96},{96,112},{112,64},{1... | collective-permute-start | bytes 147464 | tf_op jit(solution)/shard_map/ppermute | solution.py:467
  134.6 5.8 %collective-permute-start.4 = (f32[4,2,1536]{2,1,0:T(2,128)S(1)}, f32[4,2,1536]{2,1,0:T(2,128)S(1)}, u32[]{:S(2)}, u32[]{:S(2)}) collective-permute-start(f32[4,2,1536]{2,1,0:T(2,128)S(1)} %get-tuple-element.44), channel_id=1, source_target_pairs={{0,32},{16,48},{32,0},{48,16},{64,96},{80,112},{96,64},{112,80},{1... | collective-permute-start | bytes 147464 | tf_op jit(solution)/shard_map/ppermute | solution.py:467
  135.8 4.6 %collective-permute-start.5 = (f32[4,2,1536]{2,1,0:T(2,128)S(1)}, f32[4,2,1536]{2,1,0:T(2,128)S(1)}, u32[]{:S(2)}, u32[]{:S(2)}) collective-permute-start(f32[4,2,1536]{2,1,0:T(2,128)S(1)} %get-tuple-element.43), channel_id=1, source_target_pairs={{0,48},{16,0},{32,16},{48,32},{64,112},{80,64},{96,80},{112,96},{1... | collective-permute-start | bytes 147464 | tf_op jit(solution)/shard_map/ppermute | solution.py:467
  140.5 6.3 %collective-permute-start.6 = (f32[2,1536]{1,0:T(2,128)S(1)}, f32[2,1536]{1,0:T(2,128)S(1)}, u32[]{:S(2)}, u32[]{:S(2)}) collective-permute-start(f32[2,1536]{1,0:T(2,128)S(1)} %get-tuple-element.45), channel_id=1, source_target_pairs={{0,64},{16,80},{32,96},{48,112},{64,128},{80,144},{96,160},{112,17... | collective-permute-start | bytes 36872 | tf_op jit(solution)/shard_map/ppermute | solution.py:473
  142.0 5.2 %collective-permute-start.7 = (f32[2,1536]{1,0:T(2,128)S(1)}, f32[2,1536]{1,0:T(2,128)S(1)}, u32[]{:S(2)}, u32[]{:S(2)}) collective-permute-start(f32[2,1536]{1,0:T(2,128)S(1)} %get-tuple-element.47), channel_id=1, source_target_pairs={{0,128},{16,144},{32,160},{48,176},{64,192},{80,208},{96,224},{112... | collective-permute-start | bytes 36872 | tf_op jit(solution)/shard_map/ppermute | solution.py:473
  144.8 3.7 %collective-permute-start.8 = (f32[2,1536]{1,0:T(2,128)S(1)}, f32[2,1536]{1,0:T(2,128)S(1)}, u32[]{:S(2)}, u32[]{:S(2)}) collective-permute-start(f32[2,1536]{1,0:T(2,128)S(1)} %get-tuple-element.46), channel_id=1, source_target_pairs={{0,192},{16,208},{32,224},{48,240},{64,0},{80,16},{96,32},{112,48}... | collective-permute-start | bytes 36872 | tf_op jit(solution)/shard_map/ppermute | solution.py:473
  146.7 24.2 %copy-start.9 = (bf16[384,1536]{1,0:T(8,128)(2,1)S(1)}, bf16[384,1536]{1,0:T(8,128)(2,1)}, u32[]{:S(2)}) copy-start(bf16[384,1536]{1,0:T(8,128)(2,1)} %copy-done.8) | copy-start | bytes 3538948
  163.3 15.6 %all-to-all-start.3 = ((bf16[16,8,1536]{2,1,0:T(8,128)(2,1)}), bf16[16,8,1536]{2,1,0:T(8,128)(2,1)S(1)}, u32[]{:S(2)}, u32[]{:S(2)}) async-start(bf16[16,8,1536]{2,1,0:T(8,128)(2,1)} %broadcast_in_dim.5), calls=%async_computation.3 | async-start | bytes 786432 | tf_op jit(solution)/shard_map/all_to_all | solution.py:448
  (5 other events, 5.4 us)
Sparse Core Ops, SparseCore 0:
  9.8 63.7 all-gather.2
  75.5 41.2 all-gather.4

commit v5 on v4

--- a/solution.py
+++ b/solution.py
@@ -427,7 +427,7 @@
             if row < kernel:
                 taps_ref[row : row + 1, :] = block[own + index : own + index + 1]
             else:
-                gain_ref[...] = block[own + index : own + index + 1]
+                gain_ref[...] = block[own + index]
 
 
 def outputs(both, own, kernel):
@@ -437,7 +437,7 @@
         lambda *refs: outputs_kernel(own, *refs),
         in_specs=vmem(1),
         out_specs=vmem(3),
-        out_shape=[f32(owners * own, model), f32(kernel, model), f32(1, model)],
+        out_shape=[f32(owners * own, model), f32(kernel, model), f32(model)],
         compiler_params=pltpu.CompilerParams(vmem_limit_bytes=12 * 2**20),
         name="outputs",
     )(both)
@@ -530,7 +530,7 @@
     both = lax.all_to_all(both, "fsdp", 0, 0, tiled=True, axis_index_groups=same_core)
     both = jnp.sum(both.astype(jnp.float32), axis=0).astype(jnp.bfloat16)
     grad_second, grad_taps, grad_gain = outputs(spread(both, "dp"), own, kernel)
-    return (block.reshape(1, 1, rows, model), grad_second, grad_taps, grad_gain.reshape(model))
+    return (block.reshape(1, 1, rows, model), grad_second, grad_taps, grad_gain)
 
 
 def solution(mesh):

time: 188 us -> 187 us (level)
  no operation moved by 1% of the time
where the time goes in v5:
time: 187 us
  waiting for transfers between devices  45.5 us (24%)
  Pallas kernels  40 us (21%)
  starting transfers between devices  33.5 us (18%)
  local copies, waits for them, and re-layouts  21.9 us (12%)
  between operations  14.2 us (8%)
  blocking collectives  13.9 us (7%)
  matrix products  9.1 us (5%)
  other arithmetic  8.7 us (5%)
    pallas_call x1, Pallas kernels, forward(): pl.pallas_call(lambda *refs: forward_kernel(utt, owners, *refs), grid=(st...  15.9 us
    all_gather x1, waiting for transfers between devices, body(): first_t = lax.all_gather(w_first.T, 'fsdp', axis=0, tiled=True)  14.4 us
    all_to_all x1, blocking collectives, body(): lax.all_to_all(both, 'fsdp', 0, 0, tiled=True, axis_index_groups=same_core)  13.9 us
    pallas_call x1, Pallas kernels, backward(): pl.pallas_call(backward_kernel, grid=(2 * steps,), in_specs=[pl.BlockSpec...  13.5 us
    all_to_all x1, waiting for transfers between devices, body(): received = lax.all_to_all(blocks, 'dp', 0, 0, tiled=True)  10.6 us
    all_gather x1, waiting for transfers between devices, body(): second = lax.all_gather(w_second, 'fsdp', axis=0, tiled=True)  8.5 us
    all_to_all x1, starting transfers between devices, body(): received = lax.all_to_all(blocks, 'dp', 0, 0, tiled=True)  7.61 us
    all_to_all x1, starting transfers between devices, spread(): return lax.all_to_all(copies, axis, 0, 0, tiled=True)  7.6 us
  transfers between devices with their start and end apart: 14, of which 9 were waited for; matrix products, arithmetic and copies ran while one was open for 18% of the time, Pallas kernels for 21%

profile of v5, /device:TPU:2, one launch (start us, length us, event | category | flops | bytes accessed | tf_op | source)
XLA Modules:
  0.0 186.8 jit_solution(3429168328221980195)
XLA Ops:
  10.8 2.4 %send_rows.1 = bf16[16,104,640]{2,1,0:T(8,128)(2,1)} custom-call(s32[98]{0:T(128)S(1)} %pad_add_fusion.refs_0_, bf16[300,640]{1,0:T(8,128)(2,1)S(1)} %bitcast.50), custom_call_target="tpu_custom_call" | custom-call | flops 119808000 | bytes 2097152 | tf_op jit(solution)/shard_map/send_rows/pallas_call | solution.py:101
  13.2 7.6 %all-to-all-start = ((bf16[16,104,640]{2,1,0:T(8,128)(2,1)}), bf16[16,104,640]{2,1,0:T(8,128)(2,1)S(1)}, u32[]{:S(2)}, u32[]{:S(2)}) async-start(bf16[16,104,640]{2,1,0:T(8,128)(2,1)} %send_rows.1), calls=%async_computation | async-start | bytes 4259840 | tf_op jit(solution)/shard_map/all_to_all | solution.py:500
  22.2 3.3 %reshape.58 = bf16[8,2,16,6,384]{4,3,2,1,0:T(8,128)(2,1)} reshape(bf16[1536,384]{1,0:T(8,128)(2,1)} %copy.21) | data formatting | bytes 2359296 | tf_op jit(solution)/shard_map/reshape | solution.py:503
  25.5 2.4 %dynamic-slice_bitcast_fusion.1 = (bf16[16,8,6,384]{3,2,0,1:T(8,128)(2,1)}, bf16[16,8,6,384]{3,2,0,1:T(8,128)(2,1)S(1)}) fusion(bf16[8,2,16,6,384]{4,3,2,1,0:T(8,128)(2,1)} %reshape.58, s32[]{:T(128)S(6)} %select_n.39, s32[]{:T(128)S(6)} %select_n.40), kind=kLoop, calls=%fused_computation.11 | loop fusion | bytes 2359304 | tf_op jit(solution)/shard_map/transpose | solution.py:504
  29.0 2.1 %reshape.60 = bf16[768,384]{1,0:T(8,128)(2,1)} reshape(bf16[16,8,6,384]{3,2,1,0:T(8,128)(2,1)} %copy.25) | data formatting | bytes 1179648 | tf_op jit(solution)/shard_map/reshape | solution.py:504
  31.0 2.1 %copy.23 = bf16[16,8,6,384]{3,2,1,0:T(8,128)(2,1)} copy(bf16[16,8,6,384]{3,2,0,1:T(8,128)(2,1)} %get-tuple-element.40) | data formatting | bytes 1179648 | tf_op jit(solution)/shard_map/transpose | solution.py:504
  33.2 2.1 %reshape.59 = bf16[768,384]{1,0:T(8,128)(2,1)} reshape(bf16[16,8,6,384]{3,2,1,0:T(8,128)(2,1)} %copy.23) | data formatting | bytes 1179648 | tf_op jit(solution)/shard_map/reshape | solution.py:504
  35.3 2.4 %pad_maximum_fusion = bf16[768,768]{1,0:T(8,128)(2,1)} fusion(bf16[768,384]{1,0:T(8,128)(2,1)} %collective-permute-done, bf16[768,384]{1,0:T(8,128)(2,1)} %reshape.59), kind=kLoop, calls=%fused_computation.9 | loop fusion | flops 2359296 | bytes 2359296 | tf_op jit(solution)/shard_map/concatenate | solution.py:505
  37.7 10.6 %all-to-all-done.refs_1_ = bf16[16,104,640]{2,1,0:T(8,128)(2,1)S(1)} async-done(((bf16[16,104,640]{2,1,0:T(8,128)(2,1)}), bf16[16,104,640]{2,1,0:T(8,128)(2,1)S(1)}, u32[]{:S(2)}, u32[]{:S(2)}) %all-to-all-start) | async-done | bytes 2129952 | tf_op jit(solution)/shard_map/all_to_all | solution.py:500
  49.5 6.7 %front.1 = (bf16[416,1536]{1,0:T(8,128)(2,1)S(1)}, bf16[384,1536]{1,0:T(8,128)(2,1)S(1)}, bf16[416,1536]{1,0:T(8,128)(2,1)S(1)}) custom-call(s32[98]{0:T(128)S(1)} %pad_add_fusion.refs_0_, bf16[16,104,640]{2,1,0:T(8,128)(2,1)S(1)} %all-to-all-done.refs_1_, bf16[320,1536]{1,0:T(8,128)(2,1)S(1)} %copy-done.10, f32[1,1536]{1,0:T(1,128)S(1)} %reshape.56.refs_3_, ...), custom_call_target="tpu_custom_call" | custom-call | flops 4000000000 | bytes 16777216 | tf_op jit(solution)/shard_map/front/pallas_call | solution.py:166
  59.3 14.4 %all-gather.3.cloned.1.call-done.refs_2_.refs_3_ = bf16[3072,1536]{1,0:T(8,128)(2,1)} async-done(((bf16[192,1536]{1,0:T(8,128)(2,1)}), bf16[3072,1536]{1,0:T(8,128)(2,1)}) %all-gather.3.cloned.1.call-update) | async-done | bytes 9437200 | tf_op jit(solution)/shard_map/all_gather | solution.py:493
  73.7 15.9 %forward.1 = (bf16[416,1536]{1,0:T(8,128)(2,1)S(1)}, f32[12,416,128]{2,1,0:T(8,128)}, f32[416,128]{1,0:T(8,128)S(1)}, f32[416,128]{1,0:T(8,128)S(1)}, bf16[384,1536]{1,0:T(8,128)(2,1)S(1)}) custom-call(s32[98]{0:T(128)S(1)} %pad_add_fusion.refs_0_, bf16[416,1536]{1,0:T(8,128)(2,1)} %copy-done, ...), custom_call_target="tpu_custom_call" | custom-call | flops 4322033664 | bytes 15826944 | tf_op jit(solution)/shard_map/forward/pallas_call | solution.py:244
  89.9 2.6 %collective-permute-done.1 = bf16[384,1536]{1,0:T(8,128)(2,1)S(1)} collective-permute-done((bf16[384,1536]{1,0:T(8,128)(2,1)S(1)}, bf16[384,1536]{1,0:T(8,128)(2,1)S(1)}, u32[]{:S(2)}, u32[]{:S(2)}) %collective-permute-start.1) | collective-permute-done | bytes 1179680 | tf_op jit(solution)/shard_map/ppermute | solution.py:491
  92.5 3.4 %convolution_convert_fusion = bf16[768,1536]{1,0:T(8,128)(2,1)} fusion(bf16[768,768]{1,0:T(8,128)(2,1)S(1)} %copy-done.12, bf16[384,1536]{1,0:T(8,128)(2,1)S(1)} %collective-permute-done.1, bf16[384,1536]{1,0:T(8,128)(2,1)S(1)} %get-tuple-element.24), kind=kOutput, calls=%fused_computation | convolution fusion | flops 1817837568 | bytes 5898240 | tf_op jit(solution)/shard_map/dot_general | solution.py:51
  95.9 7.3 %all-to-all-start.1 = ((bf16[16,48,1536]{2,1,0:T(8,128)(2,1)}), bf16[16,48,1536]{2,1,0:T(8,128)(2,1)S(1)}, u32[]{:S(2)}, u32[]{:S(2)}) async-start(bf16[16,48,1536]{2,1,0:T(8,128)(2,1)} %bitcast.51), calls=%async_computation.1 | async-start | bytes 4718592 | tf_op jit(solution)/shard_map/all_to_all | solution.py:513
  103.2 5.1 %multiply_multiply_fusion = (f32[12,416,128]{2,1,0:T(8,128)}, f32[12,416,128]{2,1,0:T(8,128)}) fusion(f32[12,128]{1,0:T(8,128)S(1)} %bitcast.53, f32[416,128]{1,0:T(8,128)S(1)} %get-tuple-element.30.rstd_ref, f32[12,416,128]{2,1,0:T(8,128)} %get-tuple-element.28, f32[416,128]{1,0:T(8,128)S(1)} %get-tuple-element.29), kind=kLoop, calls=%fused_computation.4 | loop fusion | flops 7028736 | bytes 8099840 | tf_op jit(solution)/shard_map/mul | solution.py:519
  108.3 8.5 %all-gather.5.cloned.1.call-done.second_ref = bf16[1536,1536]{1,0:T(8,128)(2,1)} async-done(((bf16[96,1536]{1,0:T(8,128)(2,1)}), bf16[1536,1536]{1,0:T(8,128)(2,1)}) %all-gather.5.cloned.1.call-update) | async-done | bytes 4718608 | tf_op jit(solution)/shard_map/all_gather | solution.py:494
  116.8 13.5 %backward.1 = f32[32,1536]{1,0:T(8,128)} custom-call(bf16[416,1536]{1,0:T(8,128)(2,1)} %copy-done.1, bf16[1536,1536]{1,0:T(8,128)(2,1)} %all-gather.5.cloned.1.call-done.second_ref, f32[12,416,128]{2,1,0:T(8,128)} %get-tuple-element.38.slope_ref, f32[12,416,128]{2,1,0:T(8,128)} %get-tuple-element.39.centered_ref, f32[416,128]{1,0:T(8,128)} %copy-done.4, ...), custom_call_target="tpu_custom_call" | custom-call | flops 2359099392 | bytes 12386304 | tf_op jit(solution)/shard_map/backward/pallas_call | solution.py:366
  137.7 2.7 %collective-permute-done.4 = f32[4,2,1536]{2,1,0:T(2,128)S(1)} collective-permute-done((f32[4,2,1536]{2,1,0:T(2,128)S(1)}, f32[4,2,1536]{2,1,0:T(2,128)S(1)}, u32[]{:S(2)}, u32[]{:S(2)}) %collective-permute-start.4) | collective-permute-done | bytes 49184 | tf_op jit(solution)/shard_map/ppermute | solution.py:467
  142.0 2.7 %collective-permute-start.7 = (f32[2,1536]{1,0:T(2,128)S(1)}, f32[2,1536]{1,0:T(2,128)S(1)}, u32[]{:S(2)}, u32[]{:S(2)}) collective-permute-start(f32[2,1536]{1,0:T(2,128)S(1)} %get-tuple-element.47), channel_id=1, source_target_pairs={{0,128},{16,144},{32,160},{48,176},{64,192},{80,208},{96,224},{112... | collective-permute-start | bytes 36872 | tf_op jit(solution)/shard_map/ppermute | solution.py:473
  148.6 13.9 %all_to_all.20 = bf16[8,8,1536]{2,1,0:T(8,128)(2,1)S(1)} all-to-all(bf16[8,8,1536]{2,1,0:T(8,128)(2,1)S(1)} %pad_maximum_fusion.1), channel_id=1, replica_groups={{0,2,4,6,8,10,12,14},{1,3,5,7,9,11,13,15},{16,18,20,22,24,26,28,30},{17..., dimensions={0} | all-to-all | bytes 393216 | tf_op jit(solution)/shard_map/all_to_all | solution.py:530
  163.3 7.6 %all-to-all-start.3 = ((bf16[16,8,1536]{2,1,0:T(8,128)(2,1)}), bf16[16,8,1536]{2,1,0:T(8,128)(2,1)S(1)}, u32[]{:S(2)}, u32[]{:S(2)}) async-start(bf16[16,8,1536]{2,1,0:T(8,128)(2,1)} %broadcast_in_dim.5), calls=%async_computation.3 | async-start | bytes 786432 | tf_op jit(solution)/shard_map/all_to_all | solution.py:448
  170.9 5.7 %fusion.1 = bf16[1,1,384,1536]{3,2,1,0:T(8,128)(2,1)} fusion(bf16[384,1536]{1,0:T(8,128)(2,1)S(1)} %copy-done.9, bf16[1536,1536]{1,0:T(8,128)(2,1)} %all-gather.5.cloned.1.call-done.second_ref, bf16[384,1536]{1,0:T(8,128)(2,1)} %copy-done.11), kind=kOutput, calls=%fused_computation.3 | convolution fusion | flops 1813708800 | bytes 8257536 | tf_op jit(solution)/shard_map/dot_general | solution.py:55
  176.7 2.3 %all-to-all-done.3.refs_0_ = bf16[16,8,1536]{2,1,0:T(8,128)(2,1)S(1)} async-done(((bf16[16,8,1536]{2,1,0:T(8,128)(2,1)}), bf16[16,8,1536]{2,1,0:T(8,128)(2,1)S(1)}, u32[]{:S(2)}, u32[]{:S(2)}) %all-to-all-start.3) | async-done | bytes 393248 | tf_op jit(solution)/shard_map/all_to_all | solution.py:448
  (73 shorter events, 25.4 us)
Async XLA Ops:
  7.2 66.5 %all-gather.3.cloned.1.call-start = ((), (), s32[]{:S(2)}) async-start(), calls=%async_computation.4 | async-start | bytes 10027008 | tf_op jit(solution)/shard_map/all_gather | solution.py:493
  7.9 108.9 %all-gather.5.cloned.1.call-start = ((), (), s32[]{:S(2)}) async-start(), calls=%async_computation.5 | async-start | bytes 5013504 | tf_op jit(solution)/shard_map/all_gather | solution.py:494
  13.2 7.6 %copy-start.3 = (bf16[1,1,384,1536]{3,2,1,0:T(8,128)(2,1)S(1)}, bf16[1,1,384,1536]{3,2,1,0:T(8,128)(2,1)}, u32[]{:S(2)}) copy-start(bf16[1,1,384,1536]{3,2,1,0:T(8,128)(2,1)} %param.19) | copy-start | bytes 3538948
  13.2 35.1 %all-to-all-start = ((bf16[16,104,640]{2,1,0:T(8,128)(2,1)}), bf16[16,104,640]{2,1,0:T(8,128)(2,1)S(1)}, u32[]{:S(2)}, u32[]{:S(2)}) async-start(bf16[16,104,640]{2,1,0:T(8,128)(2,1)} %send_rows.1), calls=%async_computation | async-start | bytes 4259840 | tf_op jit(solution)/shard_map/all_to_all | solution.py:500
  29.0 6.3 %copy-start.14 = (f32[1536]{0:T(1024)S(1)}, f32[1536]{0:T(1024)}, u32[]{:S(2)}) copy-start(f32[1536]{0:T(1024)} %param.14) | copy-start | bytes 18436
  29.0 6.3 %copy-start.13 = (f32[1536]{0:T(1024)S(1)}, f32[1536]{0:T(1024)}, u32[]{:S(2)}) copy-start(f32[1536]{0:T(1024)} %param.17) | copy-start | bytes 18436
  31.0 4.3 %collective-permute-start = (bf16[768,384]{1,0:T(8,128)(2,1)}, bf16[768,384]{1,0:T(8,128)(2,1)}, u32[]{:S(2)}, u32[]{:S(2)}) collective-permute-start(bf16[768,384]{1,0:T(8,128)(2,1)} %reshape.60), channel_id=1, source_target_pairs={{0,1},{1,0},{2,3},{3,2},{4,5},{5,4},{6,7},{7,6},{8,9},{9,8},{10,11... | collective-permute-start | bytes 1769480 | tf_op jit(solution)/shard_map/ppermute | solution.py:491
  35.3 38.4 %copy-start.7 = (f32[1,1536]{1,0:T(1,128)}, f32[1,1536]{1,0:T(1,128)S(1)}, u32[]{:S(2)}) copy-start(f32[1,1536]{1,0:T(1,128)S(1)} %reshape.61.refs_5_.gain_ref) | copy-start | bytes 18436
  49.5 24.2 %copy-start.6 = (f32[31,1536]{1,0:T(8,128)S(1)}, f32[31,1536]{1,0:T(8,128)}, u32[]{:S(2)}) copy-start(f32[31,1536]{1,0:T(8,128)} %refs_4_.1) | copy-start | bytes 571396
  73.7 18.9 %copy-start.12 = (bf16[768,768]{1,0:T(8,128)(2,1)S(1)}, bf16[768,768]{1,0:T(8,128)(2,1)}, u32[]{:S(2)}) copy-start(bf16[768,768]{1,0:T(8,128)(2,1)} %pad_maximum_fusion) | copy-start | bytes 3538948
  89.6 6.3 %copy-start.2 = (bf16[416,1536]{1,0:T(8,128)(2,1)}, bf16[416,1536]{1,0:T(8,128)(2,1)S(1)}, u32[]{:S(2)}) copy-start(bf16[416,1536]{1,0:T(8,128)(2,1)S(1)} %get-tuple-element.31.glu_ref) | copy-start | bytes 3833860
  89.6 6.3 %copy-start.8 = (bf16[384,1536]{1,0:T(8,128)(2,1)}, bf16[384,1536]{1,0:T(8,128)(2,1)S(1)}, u32[]{:S(2)}) copy-start(bf16[384,1536]{1,0:T(8,128)(2,1)S(1)} %get-tuple-element.24) | copy-start | bytes 3538948
  89.6 13.6 %copy-start.4 = (f32[416,128]{1,0:T(8,128)}, f32[416,128]{1,0:T(8,128)S(1)}, u32[]{:S(2)}) copy-start(f32[416,128]{1,0:T(8,128)S(1)} %get-tuple-element.30.rstd_ref) | copy-start | bytes 638980
  89.6 2.9 %collective-permute-start.1 = (bf16[384,1536]{1,0:T(8,128)(2,1)S(1)}, bf16[384,1536]{1,0:T(8,128)(2,1)S(1)}, u32[]{:S(2)}, u32[]{:S(2)}) collective-permute-start(bf16[384,1536]{1,0:T(8,128)(2,1)S(1)} %get-tuple-element.24), channel_id=1, source_target_pairs={{0,1},{1,0},{2,3},{3,2},{4,5},{5,4},{6,7},{7,6},{8,9},{9,8},{10,11... | collective-permute-start | bytes 3538952 | tf_op jit(solution)/shard_map/ppermute | solution.py:491
  95.9 44.5 %all-to-all-start.1 = ((bf16[16,48,1536]{2,1,0:T(8,128)(2,1)}), bf16[16,48,1536]{2,1,0:T(8,128)(2,1)S(1)}, u32[]{:S(2)}, u32[]{:S(2)}) async-start(bf16[16,48,1536]{2,1,0:T(8,128)(2,1)} %bitcast.51), calls=%async_computation.1 | async-start | bytes 4718592 | tf_op jit(solution)/shard_map/all_to_all | solution.py:513
  130.3 1.7 collective-permute-start.2
  133.1 4.6 %collective-permute-start.3 = (f32[4,2,1536]{2,1,0:T(2,128)S(1)}, f32[4,2,1536]{2,1,0:T(2,128)S(1)}, u32[]{:S(2)}, u32[]{:S(2)}) collective-permute-start(f32[4,2,1536]{2,1,0:T(2,128)S(1)} %get-tuple-element.42), channel_id=1, source_target_pairs={{0,16},{16,32},{32,48},{48,0},{64,80},{80,96},{96,112},{112,64},{1... | collective-permute-start | bytes 147464 | tf_op jit(solution)/shard_map/ppermute | solution.py:467
  134.6 5.8 %collective-permute-start.4 = (f32[4,2,1536]{2,1,0:T(2,128)S(1)}, f32[4,2,1536]{2,1,0:T(2,128)S(1)}, u32[]{:S(2)}, u32[]{:S(2)}) collective-permute-start(f32[4,2,1536]{2,1,0:T(2,128)S(1)} %get-tuple-element.44), channel_id=1, source_target_pairs={{0,32},{16,48},{32,0},{48,16},{64,96},{80,112},{96,64},{112,80},{1... | collective-permute-start | bytes 147464 | tf_op jit(solution)/shard_map/ppermute | solution.py:467
  135.8 4.6 %collective-permute-start.5 = (f32[4,2,1536]{2,1,0:T(2,128)S(1)}, f32[4,2,1536]{2,1,0:T(2,128)S(1)}, u32[]{:S(2)}, u32[]{:S(2)}) collective-permute-start(f32[4,2,1536]{2,1,0:T(2,128)S(1)} %get-tuple-element.43), channel_id=1, source_target_pairs={{0,48},{16,0},{32,16},{48,32},{64,112},{80,64},{96,80},{112,96},{1... | collective-permute-start | bytes 147464 | tf_op jit(solution)/shard_map/ppermute | solution.py:467
  140.5 6.3 %collective-permute-start.6 = (f32[2,1536]{1,0:T(2,128)S(1)}, f32[2,1536]{1,0:T(2,128)S(1)}, u32[]{:S(2)}, u32[]{:S(2)}) collective-permute-start(f32[2,1536]{1,0:T(2,128)S(1)} %get-tuple-element.45), channel_id=1, source_target_pairs={{0,64},{16,80},{32,96},{48,112},{64,128},{80,144},{96,160},{112,17... | collective-permute-start | bytes 36872 | tf_op jit(solution)/shard_map/ppermute | solution.py:473
  142.0 5.2 %collective-permute-start.7 = (f32[2,1536]{1,0:T(2,128)S(1)}, f32[2,1536]{1,0:T(2,128)S(1)}, u32[]{:S(2)}, u32[]{:S(2)}) collective-permute-start(f32[2,1536]{1,0:T(2,128)S(1)} %get-tuple-element.47), channel_id=1, source_target_pairs={{0,128},{16,144},{32,160},{48,176},{64,192},{80,208},{96,224},{112... | collective-permute-start | bytes 36872 | tf_op jit(solution)/shard_map/ppermute | solution.py:473
  144.8 3.7 %collective-permute-start.8 = (f32[2,1536]{1,0:T(2,128)S(1)}, f32[2,1536]{1,0:T(2,128)S(1)}, u32[]{:S(2)}, u32[]{:S(2)}) collective-permute-start(f32[2,1536]{1,0:T(2,128)S(1)} %get-tuple-element.46), channel_id=1, source_target_pairs={{0,192},{16,208},{32,224},{48,240},{64,0},{80,16},{96,32},{112,48}... | collective-permute-start | bytes 36872 | tf_op jit(solution)/shard_map/ppermute | solution.py:473
  146.7 24.2 %copy-start.9 = (bf16[384,1536]{1,0:T(8,128)(2,1)S(1)}, bf16[384,1536]{1,0:T(8,128)(2,1)}, u32[]{:S(2)}) copy-start(bf16[384,1536]{1,0:T(8,128)(2,1)} %copy-done.8) | copy-start | bytes 3538948
  163.3 15.6 %all-to-all-start.3 = ((bf16[16,8,1536]{2,1,0:T(8,128)(2,1)}), bf16[16,8,1536]{2,1,0:T(8,128)(2,1)S(1)}, u32[]{:S(2)}, u32[]{:S(2)}) async-start(bf16[16,8,1536]{2,1,0:T(8,128)(2,1)} %broadcast_in_dim.5), calls=%async_computation.3 | async-start | bytes 786432 | tf_op jit(solution)/shard_map/all_to_all | solution.py:448
  (5 other events, 5.4 us)
Sparse Core Ops, SparseCore 0:
  9.8 63.7 all-gather.2
  75.5 41.2 all-gather.4
